TPU v7x, 32 devices: a whole 2x2x4 slice. The times are simulated.
32 devices in a mesh: grp: 2 (over x), ctg: 16 (over z, y, core).
Axes of the slice: x: 2, y: 2, z: 4, core: 2. Of those that a mesh axis runs over, the one named last changes fastest.
Arguments:
- flow_tiles: bfloat16 [128, 256, 3072], P('ctg'), may hold values from -0.109375 to 0.109375
- tile_pattern: int32 [128, 2, 24], P('ctg'), may hold values 0 or 1
- monitored: int32 [128, 256], P('ctg'), may hold values from 0 to 16383
- ratings: float32 [16384], replicated, may hold values from 0.3 to 3
- base_flow: float32 [64, 128, 256], P('grp', 'ctg'), parts along dimension 0, may hold values from -6 to 6
- unit_cost: float32 [64, 3072], P(('grp', 'ctg')), parts along dimension 0, may hold values from -6 to 6
- unit_floor: float32 [3072], replicated, may hold values from 0 to 0.5
- unit_span: float32 [3072], replicated, may hold values from 0.5 to 2
- ramp_limit: float32 [3072], replicated, may hold values from 0.05 to 0.5
- ramp_mask: int32 [3072], replicated, may hold values 0 or 1
- demand: float32 [64], P(('grp', 'ctg')), parts along dimension 0, may hold values from 1228.8 to 2457.6
- start_output: float32 [64, 3072], P(('grp', 'ctg')), parts along dimension 0, may hold values from 0 to 1.5
- start_flow_dual: float32 [64, 128, 256], P('grp', 'ctg'), parts along dimension 0, may hold values from -2 to 2
- start_ramp_dual: float32 [64, 3072], P(('grp', 'ctg')), parts along dimension 0, may hold values from -3 to 3
Outputs:
- output_levels: float32 [64, 3072], P(('grp', 'ctg')), parts along dimension 0
- flow_dual: float32 [64, 128, 256], P('grp', 'ctg'), parts along dimension 0
- ramp_dual: float32 [64, 3072], P(('grp', 'ctg')), parts along dimension 0
- balance_price: float32 [64], P(('grp', 'ctg')), parts along dimension 0
There are 2 independent parts, one for each index of `grp`. A program takes and returns all parts, laid end to end along the dimension named above; an argument that names none is the same for every part. Nothing has to cross between parts.
All inputs are finite; a program needn't handle non-finite values. No bound on the sum of `tile_pattern` on one device may be relied on, other than what follows from the above.
Results may differ from a plain program's by a relative error of at most 0.0045.
Values may be sent and summed in bfloat16 or wider, within the bound.
No kernel may reach another device: no remote copies, remote signals or barrier semaphores. Data moves between devices by JAX's collectives and lax.ppermute only.
A program may use at most 128 MiB of HBM per device.

v0:
```python
import math

import jax
import jax.numpy as jnp
from jax import lax
from jax.sharding import PartitionSpec as P

ITERS = 4


def mask_tiles(flow_tiles, tile_pattern):
    ctg_count, line_count, unit_count = flow_tiles.shape
    blocks = flow_tiles.reshape(ctg_count, line_count // 128, 128, unit_count // 128, 128)
    gates = tile_pattern.astype(jnp.bfloat16)[:, :, None, :, None]
    return (blocks * gates).reshape(ctg_count, line_count, unit_count)


def dual_prox(trial, dual_step, lower_side, upper_side):
    return trial - dual_step * jnp.clip(trial / dual_step, lower_side, upper_side)


def body(
    flow_tiles,
    tile_pattern,
    monitored,
    ratings,
    base_flow,
    unit_cost,
    unit_floor,
    unit_span,
    ramp_limit,
    ramp_mask,
    demand,
    start_output,
    start_flow_dual,
    start_ramp_dual,
):
    ctg_count, line_count, unit_count = flow_tiles.shape
    devices = lax.axis_size("ctg")
    position = lax.axis_index("ctg")
    masked = mask_tiles(flow_tiles, tile_pattern)
    flow_limit = ratings[monitored]
    flow_lower = base_flow - flow_limit[None]
    flow_upper = base_flow + flow_limit[None]
    step_size = 0.5 / (2.0 + math.sqrt(ctg_count * devices * line_count / unit_count))
    balance = 1.0 / math.sqrt(unit_count)
    ceiling = unit_floor + unit_span
    ramp_on = ramp_mask.astype(jnp.float32)
    weight = jnp.float32(1.0)
    hour_rows = start_output.shape[0]
    zero_row = jnp.zeros((1, unit_count), jnp.float32)
    flow_dual = start_flow_dual
    levels, costs, ramp_dual, demands = (
        lax.all_gather(start_output, "ctg", axis=0, tiled=True),
        lax.all_gather(unit_cost, "ctg", axis=0, tiled=True),
        lax.all_gather(start_ramp_dual, "ctg", axis=0, tiled=True),
        lax.all_gather(demand, "ctg", axis=0, tiled=True),
    )
    balance_price = jnp.zeros(demands.shape, jnp.float32)
    for iteration in range(ITERS):
        primal_step = step_size / weight
        dual_step = step_size * weight
        dual_half = flow_dual.astype(jnp.bfloat16)
        own_term = jnp.einsum("tkm,kmu->tu", dual_half, masked, preferred_element_type=jnp.float32)
        pulled = lax.psum(own_term.astype(jnp.bfloat16), "ctg").astype(jnp.float32)
        before = jnp.concatenate([zero_row, ramp_dual[:-1]], axis=0)
        gradient = (
            costs + pulled + ramp_on * (before - ramp_dual) + balance * balance_price[:, None]
        )
        moved = jnp.clip(levels - primal_step * gradient, unit_floor, ceiling)
        extended = 2.0 * moved - levels
        extended_half = extended.astype(jnp.bfloat16)
        flows = jnp.einsum("kmu,tu->tkm", masked, extended_half, preferred_element_type=jnp.float32)
        dual_new = dual_prox(flow_dual + dual_step * flows, dual_step, flow_lower, flow_upper)
        change = ramp_on * jnp.concatenate([extended[1:] - extended[:-1], zero_row], axis=0)
        ramp_new = dual_prox(ramp_dual + dual_step * change, dual_step, -ramp_limit, ramp_limit)
        balance_row = balance * (jnp.sum(extended, axis=1) - demands)
        price_new = balance_price + dual_step * balance_row
        if iteration < ITERS - 1:
            primal_sq = jnp.sum((moved - levels) ** 2)
            flow_sq = lax.psum(jnp.sum((dual_new - flow_dual) ** 2), "ctg")
            dual_sq = (
                flow_sq
                + jnp.sum((ramp_new - ramp_dual) ** 2)
                + jnp.sum((price_new - balance_price) ** 2)
            )
            weight = jnp.sqrt(weight) * ((dual_sq + 1e-06) / (primal_sq + 1e-06)) ** 0.25
        levels = moved
        flow_dual = dual_new
        ramp_dual = ramp_new
        balance_price = price_new
    first_hour = position * hour_rows
    own_levels = lax.dynamic_slice_in_dim(levels, first_hour, hour_rows, 0)
    own_ramp = lax.dynamic_slice_in_dim(ramp_dual, first_hour, hour_rows, 0)
    own_price = lax.dynamic_slice_in_dim(balance_price, first_hour, hour_rows, 0)
    return (own_levels, flow_dual, own_ramp, own_price)


def solution(mesh):
    return jax.shard_map(
        body,
        mesh=mesh,
        in_specs=(
            P("ctg", None, None),
            P("ctg", None, None),
            P("ctg", None),
            P(),
            P("grp", "ctg", None),
            P(("grp", "ctg"), None),
            P(),
            P(),
            P(),
            P(),
            P(("grp", "ctg")),
            P(("grp", "ctg"), None),
            P("grp", "ctg", None),
            P(("grp", "ctg"), None),
        ),
        out_specs=(
            P(("grp", "ctg"), None),
            P("grp", "ctg", None),
            P(("grp", "ctg"), None),
            P(("grp", "ctg")),
        ),
        check_vma=False,
    )
```

profile of v0, /device:TPU:0, one launch (start us, length us, event | category | flops | bytes accessed | tf_op | source)
XLA Modules:
  0.0 487.5 jit_solution(2523741557012118708)
XLA Ops:
  7.2 0.0 copy-start
  7.2 0.0 all-reduce.15.cloned.1.call-start
  7.2 0.7 convert_element_type.57
  7.9 6.3 %mul.232 = bf16[8,2,128,24,128]{4,3,2,1,0:T(8,128)(2,1)} broadcast(bf16[8,2,24]{2,1,0:T(2,128)(2,1)S(1)} %convert_element_type.57), dimensions={0,1,3} | broadcast | bytes 12583680 | tf_op jit(solution)/shard_map/mul | solution.py:15
  14.2 19.3 %mul.233 = bf16[8,256,3072]{2,1,0:T(8,128)(2,1)} reshape(bf16[8,2,128,24,128]{4,3,2,1,0:T(8,128)(2,1)} %mul.232) | data formatting | bytes 25165824 | tf_op jit(solution)/shard_map/mul | solution.py:15
  33.5 0.0 copy-done.3
  33.5 11.4 %mul.234 = bf16[8,256,3072]{2,1,0:T(8,128)(2,1)S(1)} multiply(bf16[8,256,3072]{2,1,0:T(8,128)(2,1)} %param.14, bf16[8,256,3072]{2,1,0:T(8,128)(2,1)} %mul.233) | non-fusion elementwise | flops 6291456 | bytes 37748736 | tf_op jit(solution)/shard_map/mul | solution.py:15
  45.0 4.6 copy-done.1
  49.6 0.0 copy-start.8
  49.6 0.0 copy-start.5
  49.6 0.0 copy-start.4
  49.6 0.0 copy-start.10
  49.6 0.0 copy-start.13
  49.6 0.0 copy-start.12
  49.7 0.0 copy-start.2
  49.7 2.9 fusion.4
  52.6 0.0 all-reduce.15.cloned.1.call-update
  52.6 0.0 all-reduce.17.cloned.1.call-start
  52.7 24.3 %all-gather.1 = f32[16,2,3072]{2,1,0:T(2,128)S(1)} all-gather(f32[1,2,3072]{2,1,0:T(2,128)S(1)} %bitcast.64), channel_id=1, replica_groups=mesh['grp'=2,'ctg'=16] {'ctg'}, dimensions={0}, use_global_device_ids=true | all-gather | bytes 417792 | tf_op jit(solution)/shard_map/all_gather | solution.py:55
  77.0 0.3 reshape.40
  77.3 0.0 copy-done.7
  77.3 18.6 %all-gather.2 = f32[16,2,3072]{2,1,0:T(2,128)S(1)} all-gather(f32[1,2,3072]{2,1,0:T(2,128)S(1)} %bitcast.65), channel_id=1, replica_groups=mesh['grp'=2,'ctg'=16] {'ctg'}, dimensions={0}, use_global_device_ids=true | all-gather | bytes 417792 | tf_op jit(solution)/shard_map/all_gather | solution.py:56
  95.9 0.3 reshape.42
  96.2 0.0 copy-done.8
  96.2 20.1 %all-gather = f32[16,2,3072]{2,1,0:T(2,128)S(1)} all-gather(f32[1,2,3072]{2,1,0:T(2,128)S(1)} %bitcast.66), channel_id=1, replica_groups=mesh['grp'=2,'ctg'=16] {'ctg'}, dimensions={0}, use_global_device_ids=true | all-gather | bytes 417792 | tf_op jit(solution)/shard_map/all_gather | solution.py:54
  116.3 0.3 reshape.38
  116.6 11.8 %gather_fusion = f32[2048]{0:T(1024)S(1)} fusion(f32[16384]{0:T(1024)S(1)} %copy-done, s32[2048]{0:T(1024)S(1)} %broadcast_clamp_fusion), kind=kCustom, calls=%fused_computation | custom fusion | bytes 24576 | tf_op jit(solution)/shard_map/gather | solution.py:42
  128.5 0.6 dynamic-slice
  129.7 0.2 dynamic-update-slice
  130.0 15.3 %all-reduce.15.cloned.1.call-done = bf16[32,3072]{1,0:T(8,128)(2,1)} async-done(((bf16[32,3072]{1,0:T(8,128)(2,1)}), bf16[32,3072]{1,0:T(8,128)(2,1)}) %all-reduce.15.cloned.1.call-update) | async-done | bytes 196624 | tf_op jit(solution)/shard_map/psum | solution.py:65
  145.3 1.7 multiply_reduce_fusion.4
  147.0 0.2 fusion.34
  147.3 9.1 %multiply_reduce_fusion.8 = (f32[]{:T(128)}, f32[32,8,256]{2,0,1:T(8,128)S(1)}) fusion(f32[32,8,256]{2,1,0:T(8,128)S(1)} %copy-done.3, f32[8,256]{1,0:T(8,128)S(1)} %reshape.25, f32[32,8,256]{2,1,0:T(8,128)S(1)} %copy-done.2, bf16[8,256,3072]{2,1,0:T(8,128)(2,1)} %copy-done.1, f32[32,3072]{1,0:T(8,128)S(1)} %get-tuple-element.42), kind=kOutput, calls=%fused_computation.47 | convolution fusion | flops 403537920 | bytes 13770756 | tf_op jit(solution)/shard_map/kmu,tu->tkm/dot_general | solution.py:73
  156.4 7.5 %fusion = bf16[32,3072]{1,0:T(8,128)(2,1)} fusion(bf16[8,256,3072]{2,1,0:T(8,128)(2,1)} %copy-done.1, f32[32,8,256]{2,0,1:T(8,128)S(1)} %get-tuple-element.46, f32[32,8,256]{2,1,0:T(8,128)S(1)} %copy-done.2, f32[8,256]{1,0:T(8,128)S(1)} %reshape.25), kind=kOutput, calls=%fused_computation.5 | convolution fusion | flops 403275776 | bytes 13312000 | tf_op jit(solution)/shard_map/tkm,kmu->tu/dot_general | solution.py:64
  163.9 0.0 all-reduce.17.cloned.1.call-update
  163.9 0.0 all-reduce.19.cloned.1.call-start
  163.9 31.2 %all-reduce.9 = (f32[32]{0:T(128)S(1)}, f32[]{:T(128)}) all-reduce(f32[32]{0:T(128)S(1)} %dynamic-update-slice, f32[]{:T(128)} %get-tuple-element.45), channel_id=1, replica_groups=mesh['grp'=2,'ctg'=16] {'ctg'}, use_global_device_ids=true, to_apply=%add.8 | all-reduce | flops 33 | bytes 264
  195.1 0.8 multiply_reduce_fusion.5
  195.9 0.6 multiply_reduce_fusion.11
  199.2 53.6 %all-reduce.17.cloned.1.call-done = bf16[32,3072]{1,0:T(8,128)(2,1)} async-done(((bf16[32,3072]{1,0:T(8,128)(2,1)}), bf16[32,3072]{1,0:T(8,128)(2,1)}) %all-reduce.17.cloned.1.call-update) | async-done | bytes 196624 | tf_op jit(solution)/shard_map/psum | solution.py:65
  252.8 1.7 multiply_reduce_fusion.2
  254.5 0.2 fusion.33
  254.7 9.1 %multiply_reduce_fusion.7 = (f32[]{:T(128)}, f32[32,8,256]{2,0,1:T(8,128)S(1)}) fusion(f32[32,8,256]{2,0,1:T(8,128)S(1)} %get-tuple-element.46, f32[]{:T(128)S(6)} %mul.251, f32[8,256]{1,0:T(8,128)S(1)} %reshape.25, f32[32,8,256]{2,1,0:T(8,128)S(1)} %copy-done.2, bf16[8,256,3072]{2,1,0:T(8,128)(2,1)} %copy-done.1, f32[32,3072]{1,0:T(8,128)S(1)} %get-tuple-element.36), kind=kOutput, calls=%fused_computation.44 | convolution fusion | flops 403865600 | bytes 13770760 | tf_op jit(solution)/shard_map/kmu,tu->tkm/dot_general | solution.py:73
  263.8 0.8 multiply_reduce_fusion.3
  264.6 7.5 %fusion.1 = bf16[32,3072]{1,0:T(8,128)(2,1)} fusion(bf16[8,256,3072]{2,1,0:T(8,128)(2,1)} %copy-done.1, f32[32,8,256]{2,0,1:T(8,128)S(1)} %get-tuple-element.48, f32[]{:T(128)S(6)} %mul.251, f32[32,8,256]{2,1,0:T(8,128)S(1)} %copy-done.2, f32[8,256]{1,0:T(8,128)S(1)} %reshape.25), kind=kOutput, calls=%fused_computation.6 | convolution fusion | flops 403275776 | bytes 13312004 | tf_op jit(solution)/shard_map/tkm,kmu->tu/dot_general | solution.py:64
  272.0 0.0 all-reduce.19.cloned.1.call-update
  272.1 0.0 all-reduce.21.cloned.1.call-start
  272.1 0.6 multiply_reduce_fusion.10
  272.7 31.4 %psum.52 = f32[]{:T(128)} all-reduce(f32[]{:T(128)} %get-tuple-element.47), channel_id=1, replica_groups=mesh['grp'=2,'ctg'=16] {'ctg'}, use_global_device_ids=true, to_apply=%region_9.10 | all-reduce | flops 1 | bytes 8 | tf_op jit(solution)/shard_map/psum | solution.py:81
  306.9 54.0 %all-reduce.19.cloned.1.call-done = bf16[32,3072]{1,0:T(8,128)(2,1)} async-done(((bf16[32,3072]{1,0:T(8,128)(2,1)}), bf16[32,3072]{1,0:T(8,128)(2,1)}) %all-reduce.19.cloned.1.call-update) | async-done | bytes 196624 | tf_op jit(solution)/shard_map/psum | solution.py:65
  360.9 1.7 multiply_reduce_fusion
  362.7 0.2 fusion.32
  362.9 9.1 %multiply_reduce_fusion.6 = (f32[]{:T(128)}, f32[32,8,256]{2,0,1:T(8,128)S(1)}) fusion(f32[32,8,256]{2,0,1:T(8,128)S(1)} %get-tuple-element.48, f32[]{:T(128)S(6)} %mul.268, f32[]{:T(128)S(6)} %mul.251, f32[8,256]{1,0:T(8,128)S(1)} %reshape.25, f32[32,8,256]{2,1,0:T(8,128)S(1)} %copy-done.2, bf16[8,256,3072]{2,1,0:T(8,128)(2,1)} %copy-done.1, ...), kind=kOutput, calls=%fused_computation.41 | convolution fusion | flops 403865600 | bytes 13770764 | tf_op jit(solution)/shard_map/kmu,tu->tkm/dot_general | solution.py:73
  371.9 0.8 multiply_reduce_fusion.1
  372.7 7.5 %fusion.2 = bf16[32,3072]{1,0:T(8,128)(2,1)} fusion(bf16[8,256,3072]{2,1,0:T(8,128)(2,1)} %copy-done.1, f32[32,8,256]{2,0,1:T(8,128)S(1)} %get-tuple-element.50, f32[]{:T(128)S(6)} %mul.268, f32[32,8,256]{2,1,0:T(8,128)S(1)} %copy-done.2, f32[8,256]{1,0:T(8,128)S(1)} %reshape.25), kind=kOutput, calls=%fused_computation.7 | convolution fusion | flops 403275776 | bytes 13312004 | tf_op jit(solution)/shard_map/tkm,kmu->tu/dot_general | solution.py:64
  380.1 0.0 all-reduce.21.cloned.1.call-update
  380.2 0.6 multiply_reduce_fusion.9
  380.8 31.2 %psum.54 = f32[]{:T(128)} all-reduce(f32[]{:T(128)} %get-tuple-element.49), channel_id=1, replica_groups=mesh['grp'=2,'ctg'=16] {'ctg'}, use_global_device_ids=true, to_apply=%region_16.17 | all-reduce | flops 1 | bytes 8 | tf_op jit(solution)/shard_map/psum | solution.py:81
  414.7 54.4 %all-reduce.21.cloned.1.call-done = bf16[32,3072]{1,0:T(8,128)(2,1)} async-done(((bf16[32,3072]{1,0:T(8,128)(2,1)}), bf16[32,3072]{1,0:T(8,128)(2,1)}) %all-reduce.21.cloned.1.call-update) | async-done | bytes 196624 | tf_op jit(solution)/shard_map/psum | solution.py:65
  469.1 1.2 fusion.31
  470.3 8.4 %multiply_subtract_fusion.7 = f32[32,8,256]{2,0,1:T(8,128)S(1)} fusion(bf16[8,256,3072]{2,1,0:T(8,128)(2,1)} %copy-done.1, f32[32,8,256]{2,0,1:T(8,128)S(1)} %get-tuple-element.50, f32[32,3072]{1,0:T(8,128)S(1)} %get-tuple-element.19, f32[]{:T(128)S(6)} %mul.286, f32[]{:T(128)S(6)} %mul.268, f32[8,256]{1,0:T(8,128)S(1)} %reshape.25, ...), kind=kOutput, calls=%fused_computation.40 | convolution fusion | flops 403668992 | bytes 13770760 | tf_op jit(solution)/shard_map/kmu,tu->tkm/dot_general | solution.py:73
  478.8 0.9 copy.35
  479.7 0.6 dynamic_slice.11
  480.3 0.7 multiply_subtract_fusion.11
  (33 shorter events, 0.3 us)
Async XLA Ops:
  7.2 109.4 %copy-start = (f32[16384]{0:T(1024)S(1)}, f32[16384]{0:T(1024)}, u32[]{:S(2)}) copy-start(f32[16384]{0:T(1024)} %param.17) | copy-start | bytes 196612
  7.2 138.1 %all-reduce.15.cloned.1.call-start = ((), (), s32[]{:S(2)}) async-start(), calls=%async_computation | async-start | bytes 393216 | tf_op jit(solution)/shard_map/psum | solution.py:65
  14.2 19.3 %copy-start.3 = (f32[32,8,256]{2,1,0:T(8,128)S(1)}, f32[32,8,256]{2,1,0:T(8,128)}, u32[]{:S(2)}) copy-start(f32[32,8,256]{2,1,0:T(8,128)} %param.26) | copy-start | bytes 786436
  45.0 4.6 copy-start.1
  49.6 3.1 copy-start.9
  49.6 3.1 copy-start.6
  49.6 27.7 %copy-start.7 = (f32[2,3072]{1,0:T(2,128)S(1)}, f32[2,3072]{1,0:T(2,128)}, u32[]{:S(2)}) copy-start(f32[2,3072]{1,0:T(2,128)} %param.27) | copy-start | bytes 73732
  49.6 46.6 %copy-start.11 = (s32[8,256]{1,0:T(8,128)S(1)}, s32[8,256]{1,0:T(8,128)}, u32[]{:S(2)}) copy-start(s32[8,256]{1,0:T(8,128)} %param.16) | copy-start | bytes 24580
  49.6 46.6 %copy-start.8 = (f32[2,3072]{1,0:T(2,128)S(1)}, f32[2,3072]{1,0:T(2,128)}, u32[]{:S(2)}) copy-start(f32[2,3072]{1,0:T(2,128)} %param.25) | copy-start | bytes 73732
  49.6 78.8 %copy-start.5 = (f32[3072]{0:T(1024)S(1)}, f32[3072]{0:T(1024)}, u32[]{:S(2)}) copy-start(f32[3072]{0:T(1024)} %param.22) | copy-start | bytes 36868
  49.6 78.8 %copy-start.4 = (f32[3072]{0:T(1024)S(1)}, f32[3072]{0:T(1024)}, u32[]{:S(2)}) copy-start(f32[3072]{0:T(1024)} %param.20) | copy-start | bytes 36868
  49.6 78.8 %copy-start.10 = (f32[3072]{0:T(1024)S(1)}, f32[3072]{0:T(1024)}, u32[]{:S(2)}) copy-start(f32[3072]{0:T(1024)} %param.21) | copy-start | bytes 36868
  49.6 78.8 %copy-start.13 = (u32[32]{0:T(128)S(1)}, u32[32]{0:T(128)}, u32[]{:S(2)}) copy-start(u32[32]{0:T(128)} %constant.69) | copy-start | bytes 388
  49.6 80.1 %copy-start.12 = (f32[2]{0:T(128)S(1)}, f32[2]{0:T(128)}, u32[]{:S(2)}) copy-start(f32[2]{0:T(128)} %param.24) | copy-start | bytes 28
  49.7 97.6 %copy-start.2 = (f32[32,8,256]{2,1,0:T(8,128)S(1)}, f32[32,8,256]{2,1,0:T(8,128)}, u32[]{:S(2)}) copy-start(f32[32,8,256]{2,1,0:T(8,128)} %param.18) | copy-start | bytes 786436
  52.6 200.2 %all-reduce.17.cloned.1.call-start = ((), (), s32[]{:S(2)}) async-start(), calls=%async_computation.1 | async-start | bytes 393216 | tf_op jit(solution)/shard_map/psum | solution.py:65
  163.9 197.0 %all-reduce.19.cloned.1.call-start = ((), (), s32[]{:S(2)}) async-start(), calls=%async_computation.2 | async-start | bytes 393216 | tf_op jit(solution)/shard_map/psum | solution.py:65
  272.1 197.0 %all-reduce.21.cloned.1.call-start = ((), (), s32[]{:S(2)}) async-start(), calls=%async_computation.3 | async-start | bytes 393216 | tf_op jit(solution)/shard_map/psum | solution.py:65
Sparse Core Ops, SparseCore 0:
  52.8 92.5 all-reduce.14
  164.0 88.7 all-reduce.16
  272.2 88.6 all-reduce.18
  380.3 88.7 all-reduce.20
where the time goes:
time: 489 us; the launch traced here: 487 us
  waiting for transfers between devices  177 us (36%)
  blocking collectives  157 us (32%)
  matrix products  61 us (12%)
  local copies, waits for them, and re-layouts  45.1 us (9%)
  other arithmetic  24.1 us (5%)
  between operations  23 us (5%)
    psum x4, waiting for transfers between devices, body(): pulled = lax.psum(own_term.astype(jnp.bfloat16), 'ctg').astype(jnp.float32)  177 us
    psum x2, blocking collectives, body(): flow_sq = lax.psum(jnp.sum((dual_new - flow_dual) ** 2), 'ctg')  62.6 us
    dot_general x4, matrix products, body(): jnp.einsum('kmu,tu->tkm', masked, extended_half, preferred_element_type=j...  35.6 us
    unnamed x1, blocking collectives  31.2 us
    mul x2, local copies, waits for them, and re-layouts, mask_tiles(): return (blocks * gates).reshape(ctg_count, line_count, unit_count)  25.6 us
    dot_general x4, matrix products, body(): jnp.einsum('tkm,kmu->tu', dual_half, masked, preferred_element_type=jnp.f...  25.4 us
    all_gather x1, blocking collectives, body(): lax.all_gather(unit_cost, 'ctg', axis=0, tiled=True)  24.3 us
    all_gather x1, blocking collectives, body(): lax.all_gather(start_output, 'ctg', axis=0, tiled=True)  20.1 us
  transfers between devices with their start and end apart: 4, of which 4 were waited for; matrix products, arithmetic and copies ran while one was open for 3% of the time, Pallas kernels for 0%

commit v1 on v0

v1 whole, which is shorter than its diff:
```python
import functools
import math

import jax
import jax.numpy as jnp
from jax import lax
from jax.experimental import pallas as pl
from jax.experimental.pallas import tpu as pltpu
from jax.sharding import PartitionSpec as P

ITERS = 4
LANES = 128
WIDE = 256
MIB = 2**20
HALF = jnp.bfloat16
FULL = jnp.float32

VMEM = pl.BlockSpec(memory_space=pltpu.VMEM)
SMEM = pl.BlockSpec(memory_space=pltpu.SMEM)
HBM = pl.BlockSpec(memory_space=pltpu.HBM)


def total(x):
    return jnp.sum(jnp.sum(x, axis=1, keepdims=True), axis=0, keepdims=True)


def add_rows(values, first, rows):
    row = lax.broadcasted_iota(jnp.int32, values.shape, 0)
    for j, extra in enumerate(rows):
        values = values + jnp.where(row == first + j, extra, 0.0)
    return values


def hour_terms(cost, ramp, on, price_terms):
    hours = len(cost)
    rows = []
    for j in range(hours + 1):
        if j == hours:
            rows.append(on * ramp[j - 1])
            continue
        row = cost[j] + on * ((ramp[j - 1] if j else 0.0) - ramp[j])
        if price_terms is not None:
            row = row + price_terms[j]
        rows.append(row)
    return rows


def scalar_block(value, place, shape):
    row = lax.broadcasted_iota(jnp.int32, shape, 0)
    lane = lax.broadcasted_iota(jnp.int32, shape, 1)
    block = jnp.zeros(shape, FULL)
    left = value
    for j in range(3):
        part = left.astype(HALF).astype(FULL)
        left = left - part
        block = block + jnp.where((row == j) & (lane == place), part, 0.0)
    return block.astype(HALF)


def own_first(place, s, width):
    core = place % 2
    return pl.multiple_of((core if s == 0 else 1 - core) * width, LANES)


def start_kernel(
    place_ref,
    gate_ref,
    tiles_ref,
    dual_ref,
    base_ref,
    monitored_ref,
    ratings_ref,
    floor_ref,
    span_ref,
    limit_ref,
    on_ref,
    cost_ref,
    ramp_ref,
    masked_ref,
    send_ref,
    keep_ref,
    dual_out,
    base_out,
    rating_out,
    unit_out,
    cost_out,
    ramp_out,
    acc_ref,
    sems,
):
    ctgs, lines, units = masked_ref.shape
    width = units // 2
    half_tiles = width // LANES
    hours = cost_ref.shape[0]
    place = place_ref[0]

    def copy(k, s):
        return pltpu.make_async_copy(
            tiles_ref.at[k, :, pl.ds(own_first(place, s, width), width)],
            masked_ref.at[k, :, pl.ds(s * width, width)],
            sems.at[k, s],
        )

    for k in range(ctgs):
        for s in range(2):
            copy(k, s).start()

    table = ratings_ref[...].T
    hi = table.astype(HALF)
    left = table - hi.astype(FULL)
    mid = left.astype(HALF)
    lo = (left - mid.astype(FULL)).astype(HALF)
    groups = table.shape[1]
    for k in range(ctgs):
        cols = pl.ds(k * lines, lines)
        dual_out[:, cols] = dual_ref[:, k, :]
        base_out[:, cols] = base_ref[:, k, :]
        index = monitored_ref[k : k + 1, :]
        group = lax.broadcasted_iota(jnp.int32, (groups, lines), 0)
        chosen = (group == index // LANES).astype(FULL).astype(HALF)
        picked = (
            jnp.dot(hi, chosen, preferred_element_type=FULL)
            + jnp.dot(mid, chosen, preferred_element_type=FULL)
            + jnp.dot(lo, chosen, preferred_element_type=FULL)
        )
        lane = lax.broadcasted_iota(jnp.int32, (LANES, lines), 0)
        rating_out[:, cols] = jnp.sum(jnp.where(lane == index % LANES, picked, 0.0), axis=0, keepdims=True)
    for s in range(2):
        cols, own = pl.ds(s * width, width), pl.ds(own_first(place, s, width), width)
        floor = floor_ref[:, own]
        unit_out[0:1, cols] = floor
        unit_out[1:2, cols] = floor + span_ref[:, own]
        unit_out[2:3, cols] = limit_ref[:, own]
        unit_out[3:4, cols] = on_ref[:, own].astype(FULL)
        cost_out[:, cols] = cost_ref[:, own]
        ramp_out[:, cols] = ramp_ref[:, own]

    for k in range(ctgs):
        lhs = dual_out[:, pl.ds(k * lines, lines)].astype(HALF)
        for s in range(2):
            copy(k, s).wait()
            gate_at = (place % 2 if s == 0 else 1 - place % 2) * half_tiles
            for j in range(0, half_tiles, 2):
                at = s * width + j * LANES
                block = []
                for m in range(lines // LANES):
                    line = []
                    for i in range(2):
                        gate = gate_ref[k, m, gate_at + j + i]
                        part = masked_ref[k, pl.ds(m * LANES, LANES), pl.ds(at + i * LANES, LANES)]
                        line.append(jnp.where(gate > 0, part, jnp.zeros((), HALF)))
                    block.append(jnp.concatenate(line, axis=1))
                block = jnp.concatenate(block, axis=0)
                cols = pl.ds(at, WIDE)
                masked_ref[k, :, cols] = block
                part = jnp.dot(lhs, block, preferred_element_type=FULL)
                acc_ref[:, cols] = part if k == 0 else acc_ref[:, cols] + part

    for s, out_ref in ((1, send_ref), (0, keep_ref)):
        cols = pl.ds(s * width, width)
        on = unit_out[3:4, cols]
        cost = [cost_out[j : j + 1, cols] for j in range(hours)]
        ramp = [ramp_out[j : j + 1, cols] for j in range(hours)]
        rows = hour_terms(cost, ramp, on, None)
        out_ref[:, :width] = add_rows(acc_ref[:, cols], place * hours, rows).astype(HALF)
        out_ref[:, width:] = jnp.zeros((out_ref.shape[0], LANES), HALF)


def step_kernel(step_size, balance, first, last, *refs):
    refs = list(refs)
    place_ref, masked_ref, own_ref, other_ref = refs[:4]
    del refs[:4]
    level_refs = [refs.pop(0) for _ in range(2 if first else 1)]
    stat_ref = None if first else refs.pop(0)
    dual_ref, base_ref, rating_ref, unit_ref, cost_ref, demand_ref, ramp_ref = refs[:7]
    del refs[:7]
    price_ref = None if first else refs.pop(0)
    level_out, dual_out, ramp_out, price_out = refs[:4]
    del refs[:4]
    if not last:
        send_ref, keep_ref, stat_out, half_dual = refs[:4]
        del refs[:4]
    extended_ref, half_ref = refs[:2]
    moved_ref = refs[2] if last else level_out

    ctgs, lines, units = masked_ref.shape
    width = units // 2
    all_hours = own_ref.shape[0]
    hours = cost_ref.shape[0]
    place = place_ref[0]
    first_hour = place * hours

    if first:
        weight = jnp.full((1, 1), 1.0, FULL)
    else:
        dual_sq = total(own_ref[:, width:].astype(FULL))
        primal_sq = stat_ref[1:2, 0:1]
        weight = jnp.sqrt(stat_ref[0:1, 0:1]) * jnp.sqrt(jnp.sqrt((dual_sq + 1e-06) / (primal_sq + 1e-06)))
    primal_step = step_size / weight
    dual_step = step_size * weight

    if first:
        for d in range(all_hours // hours):
            for s in range(2):
                block = place ^ d ^ s
                for j in range(hours):
                    level_out[pl.ds(d * hours + j, 1), pl.ds(s * width, width)] = level_refs[s][
                        pl.ds(block * hours + j, 1), :
                    ]
        level_refs = [level_out]
    primal_acc = jnp.zeros((all_hours, WIDE), FULL)
    for at in range(0, units, WIDE):
        cols = pl.ds(at, WIDE)
        s, inner = at // width, pl.ds(at % width, WIDE)
        gradient = (own_ref, other_ref)[s][:, inner].astype(FULL)
        levels = level_refs[0][:, cols]
        moved = jnp.clip(levels - primal_step * gradient, unit_ref[0:1, cols], unit_ref[1:2, cols])
        extended = 2.0 * moved - levels
        moved_ref[:, cols] = moved
        extended_ref[:, cols] = extended
        half_ref[:, cols] = extended.astype(HALF)
        if not last:
            primal_acc = primal_acc + (moved - levels) ** 2

    flow_acc = jnp.zeros((all_hours, lines), FULL)
    for k in range(ctgs):
        cols = pl.ds(k * lines, lines)
        flows = lax.dot_general(
            half_ref[...], masked_ref[k], (((1,), (1,)), ((), ())), preferred_element_type=FULL
        )
        old = dual_ref[:, cols]
        trial = old + dual_step * flows
        base, rating = base_ref[:, cols], rating_ref[:, cols]
        new = trial - jnp.clip(trial, dual_step * (base - rating), dual_step * (base + rating))
        if last:
            dual_out[:, k, :] = new
        else:
            dual_out[:, cols] = new
            half_dual[:, cols] = new.astype(HALF)
            flow_acc = flow_acc + (new - old) ** 2

    ramp_limit, ramp_on = unit_ref[2:3, :], unit_ref[3:4, :]
    moved_sq = total(flow_acc)
    rows, ramp_rows, price_rows = [], [], []
    for j in range(hours + 1):
        rows.append(extended_ref[pl.ds(jnp.minimum(first_hour + j, all_hours - 1), 1), :])
    for j in range(hours):
        old = ramp_ref[j : j + 1, :]
        trial = old + dual_step * (ramp_on * (rows[j + 1] - rows[j]))
        reach = dual_step * ramp_limit
        new = trial - jnp.clip(trial, -reach, reach)
        old_price = jnp.zeros((1, 1), FULL) if first else price_ref[j : j + 1, :]
        supply = jnp.sum(rows[j], axis=1, keepdims=True)
        new_price = old_price + dual_step * (balance * (supply - demand_ref[0:1, j : j + 1]))
        if last:
            price_out[j] = new_price[0, 0]
        else:
            price_out[j : j + 1, :] = new_price
        moved_sq = moved_sq + total((new - old) ** 2) + (new_price - old_price) ** 2
        ramp_rows.append(new)
        price_rows.append(new_price)
        if last:
            for s in range(2):
                own = pl.ds(own_first(place, s, width), width)
                level_out[j : j + 1, own] = moved_ref[pl.ds(first_hour + j, 1), pl.ds(s * width, width)]
                ramp_out[j : j + 1, own] = new[:, s * width : (s + 1) * width]
        else:
            ramp_out[j : j + 1, :] = new
    if last:
        return

    primal_sq = total(primal_acc)
    row = lax.broadcasted_iota(jnp.int32, stat_out.shape, 0)
    stat_out[...] = jnp.where(row == 0, weight, primal_sq)
    block = scalar_block(moved_sq, place, (all_hours, LANES))
    price_terms = [balance * price for price in price_rows]
    whole = masked_ref.reshape(ctgs * lines, units)
    for s, out_ref in ((1, send_ref), (0, keep_ref)):
        out_ref[:, width:] = block
        for at in range(0, width, WIDE):
            cols = pl.ds(s * width + at, WIDE)
            pulled = jnp.dot(half_dual[...], whole[:, cols], preferred_element_type=FULL)
            here = slice(s * width + at, s * width + at + WIDE)
            terms = hour_terms(
                [cost_ref[j : j + 1, cols] for j in range(hours)],
                [ramp[:, here] for ramp in ramp_rows],
                ramp_on[:, here],
                price_terms,
            )
            out_ref[:, pl.ds(at, WIDE)] = add_rows(pulled, first_hour, terms).astype(HALF)


def exchange(x, mask):
    devices = lax.axis_size("ctg")
    return lax.ppermute(x, "ctg", [(i, i ^ mask) for i in range(devices)])


def far_masks():
    devices = lax.axis_size("ctg")
    assert devices & (devices - 1) == 0 and 2 <= devices <= LANES
    return [1 << b for b in range(1, devices.bit_length() - 1)]


def sum_over_devices(send, keep):
    own = keep + exchange(send, 1)
    for mask in far_masks():
        own = own + exchange(own, mask)
    return own, exchange(own, 1)


def split_kernel(place_ref, x_ref, own_ref, other_ref):
    width = x_ref.shape[1] // 2
    for s, out_ref in ((0, own_ref), (1, other_ref)):
        out_ref[...] = x_ref[:, pl.ds(own_first(place_ref[0], s, width), width)]


def join_kernel(first_ref, second_ref, out_ref):
    rows = first_ref.shape[0]
    out_ref[:rows, :] = first_ref[...]
    out_ref[rows:, :] = second_ref[...]


def join(first, second):
    return pl.pallas_call(
        join_kernel,
        out_shape=jax.ShapeDtypeStruct((2 * first.shape[0], first.shape[1]), first.dtype),
        in_specs=[VMEM, VMEM],
        out_specs=VMEM,
        compiler_params=params(12),
        name="join",
    )(first, second)


def gather_levels(here, levels):
    half = jax.ShapeDtypeStruct((levels.shape[0], levels.shape[1] // 2), FULL)
    own, other = pl.pallas_call(
        split_kernel,
        out_shape=(half, half),
        in_specs=[SMEM, VMEM],
        out_specs=(VMEM, VMEM),
        compiler_params=params(12),
        name="split",
    )(here, levels)
    own = join(own, exchange(other, 1))
    for mask in far_masks():
        own = join(own, exchange(own, mask))
    return own, exchange(own, 1)


def params(limit):
    return pltpu.CompilerParams(vmem_limit_bytes=limit * MIB)


def body(
    flow_tiles,
    tile_pattern,
    monitored,
    ratings,
    base_flow,
    unit_cost,
    unit_floor,
    unit_span,
    ramp_limit,
    ramp_mask,
    demand,
    start_output,
    start_flow_dual,
    start_ramp_dual,
):
    ctgs, lines, units = flow_tiles.shape
    all_hours, hours = start_flow_dual.shape[0], start_output.shape[0]
    devices = lax.axis_size("ctg")
    place = lax.axis_index("ctg")
    here = place.astype(jnp.int32).reshape(1)
    width = units // 2
    step_size = 0.5 / (2.0 + math.sqrt(ctgs * devices * lines / units))
    balance = 1.0 / math.sqrt(units)
    spread = -ratings.shape[0] % (8 * LANES)
    table = jnp.pad(ratings, (0, spread)).reshape(-1, LANES)
    row = lambda x: x.reshape(1, units)
    f32 = lambda *shape: jax.ShapeDtypeStruct(shape, FULL)
    near = lambda *shape: pltpu.VMEM(shape, FULL)
    message = pltpu.VMEM((all_hours, width + LANES), HALF)

    masked, send, keep, dual, base, rating, unit, cost, ramp = pl.pallas_call(
        start_kernel,
        out_shape=(
            pltpu.VMEM(flow_tiles.shape, HALF),
            message,
            message,
            near(all_hours, ctgs * lines),
            near(all_hours, ctgs * lines),
            near(1, ctgs * lines),
            near(4, units),
            near(hours, units),
            near(hours, units),
        ),
        in_specs=[SMEM, SMEM, HBM] + [VMEM] * 10,
        out_specs=(VMEM,) * 9,
        scratch_shapes=[pltpu.VMEM((all_hours, units), FULL), pltpu.SemaphoreType.DMA((ctgs, 2))],
        compiler_params=params(44),
        name="start",
    )(
        here,
        tile_pattern,
        flow_tiles,
        start_flow_dual,
        base_flow,
        monitored,
        table,
        row(unit_floor),
        row(unit_span),
        row(ramp_limit),
        row(ramp_mask),
        unit_cost,
        start_ramp_dual,
    )
    masked = pltpu.with_memory_space_constraint(masked, pltpu.VMEM)
    levels = gather_levels(here, start_output)
    demands = demand.reshape(1, hours)
    stat = ()
    for iteration in range(ITERS):
        first, last = iteration == 0, iteration == ITERS - 1
        own, other = sum_over_devices(send, keep)
        out_shape = [near(all_hours, units), near(all_hours, ctgs * lines), near(hours, units), near(hours, 1)]
        scratch = [pltpu.VMEM((all_hours, units), FULL), pltpu.VMEM((all_hours, units), HALF)]
        if last:
            out_shape = [f32(hours, units), f32(all_hours, ctgs, lines), f32(hours, units), f32(hours)]
            scratch.append(pltpu.VMEM((all_hours, units), FULL))
        else:
            out_shape += [message, message, near(8, LANES)]
            scratch.insert(0, pltpu.VMEM((all_hours, ctgs * lines), HALF))
        operands = [here, masked, own, other, *levels, *stat]
        operands += [dual, base, rating, unit, cost, demands, ramp] + ([] if first else [price])
        outs = pl.pallas_call(
            functools.partial(step_kernel, step_size, balance, first, last),
            out_shape=tuple(out_shape),
            in_specs=[SMEM] + [VMEM] * (len(operands) - 1),
            out_specs=tuple(SMEM if last and j == 3 else VMEM for j in range(len(out_shape))),
            scratch_shapes=scratch,
            compiler_params=params(12),
            name="step",
        )(*operands)
        levels, dual, ramp, price = (outs[0],), outs[1], outs[2], outs[3]
        if not last:
            send, keep, stat = outs[4], outs[5], (outs[6],)
    return levels[0], dual, ramp, price


def solution(mesh):
    return jax.shard_map(
        body,
        mesh=mesh,
        in_specs=(
            P("ctg", None, None),
            P("ctg", None, None),
            P("ctg", None),
            P(),
            P("grp", "ctg", None),
            P(("grp", "ctg"), None),
            P(),
            P(),
            P(),
            P(),
            P(("grp", "ctg")),
            P(("grp", "ctg"), None),
            P("grp", "ctg", None),
            P(("grp", "ctg"), None),
        ),
        out_specs=(
            P(("grp", "ctg"), None),
            P("grp", "ctg", None),
            P(("grp", "ctg"), None),
            P(("grp", "ctg")),
        ),
        check_vma=False,
    )
```

time: 489 us -> 115 us (0.24)
  blocking collectives: 157 us -> 0 us
  waiting for transfers between devices: 177 us -> 64.3 us
  matrix products: 61 us -> 0 us
  local copies, waits for them, and re-layouts: 45.1 us -> 0.01 us
  Pallas kernels: 0 us -> 30.5 us
  other arithmetic: 24.1 us -> 0.46 us
  between operations: 23 us -> 1.01 us
  starting transfers between devices: 0.16 us -> 18.4 us
    psum x4 -> x0, waiting for transfers between devices: 177 us -> none  [body(): pulled = lax.psum(own_term.astype(jnp.bfloat16), 'ctg').astype(jnp.float32)]
    ppermute x0 -> x25, waiting for transfers between devices: none -> 64.3 us  [exchange(): return lax.ppermute(x, 'ctg', [(i, i ^ mask) for i in range(devices)])]
    all_gather x3 -> x0, blocking collectives: 63 us -> none  [the longest x1 24.3 us: body(): lax.all_gather(unit_cost, 'ctg', axis=0, tiled=True)]
    psum x2 -> x0, blocking collectives: 62.6 us -> none  [body(): flow_sq = lax.psum(jnp.sum((dual_new - flow_dual) ** 2), 'ctg')]
    dot_general x8 -> x0, matrix products: 61 us -> none  [the longest x4 35.6 us: body(): jnp.einsum('kmu,tu->tkm', masked, extended_half, preferred_element_type=j...]
    unnamed x1 -> x0, blocking collectives: 31.2 us -> none
    pallas_call x0 -> x10, Pallas kernels: none -> 30.5 us  [the longest x4 23.7 us: body(): pl.pallas_call(functools.partial(step_kernel, step_size, balance, first,...]
    mul x2 -> x0, local copies, waits for them, and re-layouts: 25.6 us -> none  [mask_tiles(): return (blocks * gates).reshape(ctg_count, line_count, unit_count)]
  transfers between devices with their start and end apart: 4 -> 25, of which waited for: 4 -> 24; matrix products, arithmetic and copies ran while one was open for 3% -> 0% of each run, Pallas kernels for 0% -> 0%
where the time goes in v1:
time: 115 us
  waiting for transfers between devices  64.3 us (56%)
  Pallas kernels  30.5 us (27%)
  starting transfers between devices  18.4 us (16%)
    ppermute x25, waiting for transfers between devices, exchange(): return lax.ppermute(x, 'ctg', [(i, i ^ mask) for i in range(devices)])  64.3 us
    pallas_call x4, Pallas kernels, body(): pl.pallas_call(functools.partial(step_kernel, step_size, balance, first,...  23.7 us
    ppermute x25, starting transfers between devices, exchange(): return lax.ppermute(x, 'ctg', [(i, i ^ mask) for i in range(devices)])  18.4 us
    pallas_call x1, Pallas kernels, body(): pl.pallas_call(start_kernel, out_shape=(pltpu.VMEM(flow_tiles.shape, HALF...  6.76 us
  transfers between devices with their start and end apart: 25, of which 24 were waited for; matrix products, arithmetic and copies ran while one was open for 0% of the time, Pallas kernels for 0%

profile of v1, /device:TPU:0, one launch (start us, length us, event | category | flops | bytes accessed | tf_op | source)
XLA Modules:
  0.0 114.7 jit_solution(4370901046643134078)
XLA Ops:
  0.6 0.0 copy-start
  0.6 0.0 copy-start.1
  0.7 6.8 %start.1 = (bf16[8,256,3072]{2,1,0:T(8,128)(2,1)S(1)}, bf16[32,1664]{1,0:T(8,128)(2,1)S(1)}, bf16[32,1664]{1,0:T(8,128)(2,1)S(1)}, f32[32,2048]{1,0:T(8,128)S(1)...) custom-call(s32[1]{0:T(128)} %bitcast.place_ref.refs_0_, ...), custom_call_target="tpu_custom_call" | custom-call | tf_op jit(solution)/shard_map/start/pallas_call | solution.py:385
  7.4 0.5 collective-permute-start
  7.9 1.0 collective-permute-done
  8.9 2.9 %collective-permute-start.1 = (bf16[32,1664]{1,0:T(8,128)(2,1)S(1)}, bf16[32,1664]{1,0:T(8,128)(2,1)S(1)}, u32[]{:S(2)}, u32[]{:S(2)}) collective-permute-start(bf16[32,1664]{1,0:T(8,128)(2,1)S(1)} %add.48), channel_id=1, source_target_pairs={{0,2},{1,3},{2,0},{3,1},{4,6},{5,7},{6,4},{7,5},{8,10},{9,11},{10,... | collective-permute-start | bytes 319496 | tf_op jit(solution)/shard_map/ppermute | solution.py:295
  11.9 0.0 copy-done
  11.9 0.0 collective-permute-start.5
  11.9 1.2 %collective-permute-done.5.second_ref = f32[2,1536]{1,0:T(2,128)S(1)} collective-permute-done((f32[2,1536]{1,0:T(2,128)S(1)}, f32[2,1536]{1,0:T(2,128)S(1)}, u32[]{:S(2)}, u32[]{:S(2)}) %collective-permute-start.5) | collective-permute-done | bytes 12320 | tf_op jit(solution)/shard_map/ppermute | solution.py:295
  13.1 0.2 collective-permute-start.6
  13.2 3.7 %collective-permute-done.6.second_ref = f32[4,1536]{1,0:T(4,128)S(1)} collective-permute-done((f32[4,1536]{1,0:T(4,128)S(1)}, f32[4,1536]{1,0:T(4,128)S(1)}, u32[]{:S(2)}, u32[]{:S(2)}) %collective-permute-start.6) | collective-permute-done | bytes 24608 | tf_op jit(solution)/shard_map/ppermute | solution.py:295
  17.0 1.6 %collective-permute-start.7 = (f32[8,1536]{1,0:T(8,128)S(1)}, f32[8,1536]{1,0:T(8,128)S(1)}, u32[]{:S(2)}, u32[]{:S(2)}) collective-permute-start(f32[8,1536]{1,0:T(8,128)S(1)} %join.5.first_ref), channel_id=1, source_target_pairs={{0,4},{1,5},{2,6},{3,7},{4,0},{5,1},{6,2},{7,3},{8,12},{9,13},{10,... | collective-permute-start | bytes 147464 | tf_op jit(solution)/shard_map/ppermute | solution.py:295
  18.6 0.0 collective-permute-done.1
  18.6 0.5 collective-permute-start.2
  19.2 2.4 %collective-permute-done.7.second_ref = f32[8,1536]{1,0:T(8,128)S(1)} collective-permute-done((f32[8,1536]{1,0:T(8,128)S(1)}, f32[8,1536]{1,0:T(8,128)S(1)}, u32[]{:S(2)}, u32[]{:S(2)}) %collective-permute-start.7) | collective-permute-done | bytes 49184 | tf_op jit(solution)/shard_map/ppermute | solution.py:295
  21.6 2.7 %collective-permute-start.8 = (f32[16,1536]{1,0:T(8,128)S(1)}, f32[16,1536]{1,0:T(8,128)S(1)}, u32[]{:S(2)}, u32[]{:S(2)}) collective-permute-start(f32[16,1536]{1,0:T(8,128)S(1)} %join.6.first_ref), channel_id=1, source_target_pairs={{0,8},{1,9},{2,10},{3,11},{4,12},{5,13},{6,14},{7,15},{8,0},{9,1},... | collective-permute-start | bytes 294920 | tf_op jit(solution)/shard_map/ppermute | solution.py:295
  24.3 0.2 collective-permute-done.2
  24.5 2.0 %collective-permute-start.3 = (bf16[32,1664]{1,0:T(8,128)(2,1)S(1)}, bf16[32,1664]{1,0:T(8,128)(2,1)S(1)}, u32[]{:S(2)}, u32[]{:S(2)}) collective-permute-start(bf16[32,1664]{1,0:T(8,128)(2,1)S(1)} %add.50), channel_id=1, source_target_pairs={{0,8},{1,9},{2,10},{3,11},{4,12},{5,13},{6,14},{7,15},{8,0},{9,1},... | collective-permute-start | bytes 319496 | tf_op jit(solution)/shard_map/ppermute | solution.py:295
  26.5 4.3 %collective-permute-done.8.second_ref = f32[16,1536]{1,0:T(8,128)S(1)} collective-permute-done((f32[16,1536]{1,0:T(8,128)S(1)}, f32[16,1536]{1,0:T(8,128)S(1)}, u32[]{:S(2)}, u32[]{:S(2)}) %collective-permute-start.8) | collective-permute-done | bytes 98336 | tf_op jit(solution)/shard_map/ppermute | solution.py:295
  30.9 0.1 collective-permute-start.9
  30.9 1.0 collective-permute-done.3
  32.0 0.1 collective-permute-start.4
  32.1 0.3 collective-permute-done.9.refs_5_
  32.4 1.0 collective-permute-done.4.refs_3_
  33.4 0.0 copy-done.1
  33.4 6.1 %step.4 = (f32[32,3072]{1,0:T(8,128)S(1)}, f32[32,2048]{1,0:T(8,128)S(1)}, f32[2,3072]{1,0:T(2,128)S(1)}, f32[2,1]{1,0:T(2,128)S(1)}, bf16[32,1664]{1,0:T(8,128)...) custom-call(s32[1]{0:T(128)} %bitcast.place_ref.refs_0_, ...), custom_call_target="tpu_custom_call" | custom-call | tf_op jit(solution)/shard_map/step/pallas_call | solution.py:435
  39.5 0.2 collective-permute-start.10
  39.7 1.2 %collective-permute-done.10 = bf16[32,1664]{1,0:T(8,128)(2,1)S(1)} collective-permute-done((bf16[32,1664]{1,0:T(8,128)(2,1)S(1)}, bf16[32,1664]{1,0:T(8,128)(2,1)S(1)}, u32[]{:S(2)}, u32[]{:S(2)}) %collective-permute-start.10) | collective-permute-done | bytes 106528 | tf_op jit(solution)/shard_map/ppermute | solution.py:295
  40.9 1.2 %collective-permute-start.11 = (bf16[32,1664]{1,0:T(8,128)(2,1)S(1)}, bf16[32,1664]{1,0:T(8,128)(2,1)S(1)}, u32[]{:S(2)}, u32[]{:S(2)}) collective-permute-start(bf16[32,1664]{1,0:T(8,128)(2,1)S(1)} %add.52), channel_id=1, source_target_pairs={{0,2},{1,3},{2,0},{3,1},{4,6},{5,7},{6,4},{7,5},{8,10},{9,11},{10,... | collective-permute-start | bytes 319496 | tf_op jit(solution)/shard_map/ppermute | solution.py:295
  42.1 3.9 %collective-permute-done.11 = bf16[32,1664]{1,0:T(8,128)(2,1)S(1)} collective-permute-done((bf16[32,1664]{1,0:T(8,128)(2,1)S(1)}, bf16[32,1664]{1,0:T(8,128)(2,1)S(1)}, u32[]{:S(2)}, u32[]{:S(2)}) %collective-permute-start.11) | collective-permute-done | bytes 106528 | tf_op jit(solution)/shard_map/ppermute | solution.py:295
  46.1 0.1 collective-permute-start.12
  46.1 4.7 %collective-permute-done.12 = bf16[32,1664]{1,0:T(8,128)(2,1)S(1)} collective-permute-done((bf16[32,1664]{1,0:T(8,128)(2,1)S(1)}, bf16[32,1664]{1,0:T(8,128)(2,1)S(1)}, u32[]{:S(2)}, u32[]{:S(2)}) %collective-permute-start.12) | collective-permute-done | bytes 106528 | tf_op jit(solution)/shard_map/ppermute | solution.py:295
  50.9 1.4 %collective-permute-start.13 = (bf16[32,1664]{1,0:T(8,128)(2,1)S(1)}, bf16[32,1664]{1,0:T(8,128)(2,1)S(1)}, u32[]{:S(2)}, u32[]{:S(2)}) collective-permute-start(bf16[32,1664]{1,0:T(8,128)(2,1)S(1)} %add.54), channel_id=1, source_target_pairs={{0,8},{1,9},{2,10},{3,11},{4,12},{5,13},{6,14},{7,15},{8,0},{9,1},... | collective-permute-start | bytes 319496 | tf_op jit(solution)/shard_map/ppermute | solution.py:295
  52.3 5.3 %collective-permute-done.13 = bf16[32,1664]{1,0:T(8,128)(2,1)S(1)} collective-permute-done((bf16[32,1664]{1,0:T(8,128)(2,1)S(1)}, bf16[32,1664]{1,0:T(8,128)(2,1)S(1)}, u32[]{:S(2)}, u32[]{:S(2)}) %collective-permute-start.13) | collective-permute-done | bytes 106528 | tf_op jit(solution)/shard_map/ppermute | solution.py:295
  57.6 0.1 collective-permute-start.14
  57.7 1.3 %collective-permute-done.14.refs_3_ = bf16[32,1664]{1,0:T(8,128)(2,1)S(1)} collective-permute-done((bf16[32,1664]{1,0:T(8,128)(2,1)S(1)}, bf16[32,1664]{1,0:T(8,128)(2,1)S(1)}, u32[]{:S(2)}, u32[]{:S(2)}) %collective-permute-start.14) | collective-permute-done | bytes 106528 | tf_op jit(solution)/shard_map/ppermute | solution.py:295
  59.0 6.5 %step.5 = (f32[32,3072]{1,0:T(8,128)S(1)}, f32[32,2048]{1,0:T(8,128)S(1)}, f32[2,3072]{1,0:T(2,128)S(1)}, f32[2,1]{1,0:T(2,128)S(1)}, bf16[32,1664]{1,0:T(8,128)...) custom-call(s32[1]{0:T(128)} %bitcast.place_ref.refs_0_, ...), custom_call_target="tpu_custom_call" | custom-call | tf_op jit(solution)/shard_map/step/pallas_call | solution.py:435
  65.4 0.2 collective-permute-start.15
  65.7 1.2 %collective-permute-done.15 = bf16[32,1664]{1,0:T(8,128)(2,1)S(1)} collective-permute-done((bf16[32,1664]{1,0:T(8,128)(2,1)S(1)}, bf16[32,1664]{1,0:T(8,128)(2,1)S(1)}, u32[]{:S(2)}, u32[]{:S(2)}) %collective-permute-start.15) | collective-permute-done | bytes 106528 | tf_op jit(solution)/shard_map/ppermute | solution.py:295
  66.9 1.1 collective-permute-start.16
  68.0 4.0 %collective-permute-done.16 = bf16[32,1664]{1,0:T(8,128)(2,1)S(1)} collective-permute-done((bf16[32,1664]{1,0:T(8,128)(2,1)S(1)}, bf16[32,1664]{1,0:T(8,128)(2,1)S(1)}, u32[]{:S(2)}, u32[]{:S(2)}) %collective-permute-start.16) | collective-permute-done | bytes 106528 | tf_op jit(solution)/shard_map/ppermute | solution.py:295
  72.0 0.1 collective-permute-start.17
  72.1 4.7 %collective-permute-done.17 = bf16[32,1664]{1,0:T(8,128)(2,1)S(1)} collective-permute-done((bf16[32,1664]{1,0:T(8,128)(2,1)S(1)}, bf16[32,1664]{1,0:T(8,128)(2,1)S(1)}, u32[]{:S(2)}, u32[]{:S(2)}) %collective-permute-start.17) | collective-permute-done | bytes 106528 | tf_op jit(solution)/shard_map/ppermute | solution.py:295
  76.8 1.0 collective-permute-start.18
  77.8 5.3 %collective-permute-done.18 = bf16[32,1664]{1,0:T(8,128)(2,1)S(1)} collective-permute-done((bf16[32,1664]{1,0:T(8,128)(2,1)S(1)}, bf16[32,1664]{1,0:T(8,128)(2,1)S(1)}, u32[]{:S(2)}, u32[]{:S(2)}) %collective-permute-start.18) | collective-permute-done | bytes 106528 | tf_op jit(solution)/shard_map/ppermute | solution.py:295
  83.1 0.1 collective-permute-start.19
  83.2 1.3 %collective-permute-done.19.refs_3_ = bf16[32,1664]{1,0:T(8,128)(2,1)S(1)} collective-permute-done((bf16[32,1664]{1,0:T(8,128)(2,1)S(1)}, bf16[32,1664]{1,0:T(8,128)(2,1)S(1)}, u32[]{:S(2)}, u32[]{:S(2)}) %collective-permute-start.19) | collective-permute-done | bytes 106528 | tf_op jit(solution)/shard_map/ppermute | solution.py:295
  84.5 6.3 %step.6 = (f32[32,3072]{1,0:T(8,128)S(1)}, f32[32,2048]{1,0:T(8,128)S(1)}, f32[2,3072]{1,0:T(2,128)S(1)}, f32[2,1]{1,0:T(2,128)S(1)}, bf16[32,1664]{1,0:T(8,128)...) custom-call(s32[1]{0:T(128)} %bitcast.place_ref.refs_0_, ...), custom_call_target="tpu_custom_call" | custom-call | tf_op jit(solution)/shard_map/step/pallas_call | solution.py:435
  90.8 0.2 collective-permute-start.20
  91.0 1.2 %collective-permute-done.20 = bf16[32,1664]{1,0:T(8,128)(2,1)S(1)} collective-permute-done((bf16[32,1664]{1,0:T(8,128)(2,1)S(1)}, bf16[32,1664]{1,0:T(8,128)(2,1)S(1)}, u32[]{:S(2)}, u32[]{:S(2)}) %collective-permute-start.20) | collective-permute-done | bytes 106528 | tf_op jit(solution)/shard_map/ppermute | solution.py:295
  92.2 1.1 collective-permute-start.21
  93.3 4.0 %collective-permute-done.21 = bf16[32,1664]{1,0:T(8,128)(2,1)S(1)} collective-permute-done((bf16[32,1664]{1,0:T(8,128)(2,1)S(1)}, bf16[32,1664]{1,0:T(8,128)(2,1)S(1)}, u32[]{:S(2)}, u32[]{:S(2)}) %collective-permute-start.21) | collective-permute-done | bytes 106528 | tf_op jit(solution)/shard_map/ppermute | solution.py:295
  97.3 0.1 collective-permute-start.22
  97.4 4.7 %collective-permute-done.22 = bf16[32,1664]{1,0:T(8,128)(2,1)S(1)} collective-permute-done((bf16[32,1664]{1,0:T(8,128)(2,1)S(1)}, bf16[32,1664]{1,0:T(8,128)(2,1)S(1)}, u32[]{:S(2)}, u32[]{:S(2)}) %collective-permute-start.22) | collective-permute-done | bytes 106528 | tf_op jit(solution)/shard_map/ppermute | solution.py:295
  102.1 1.0 collective-permute-start.23
  103.1 5.3 %collective-permute-done.23 = bf16[32,1664]{1,0:T(8,128)(2,1)S(1)} collective-permute-done((bf16[32,1664]{1,0:T(8,128)(2,1)S(1)}, bf16[32,1664]{1,0:T(8,128)(2,1)S(1)}, u32[]{:S(2)}, u32[]{:S(2)}) %collective-permute-start.23) | collective-permute-done | bytes 106528 | tf_op jit(solution)/shard_map/ppermute | solution.py:295
  108.4 0.1 collective-permute-start.24
  108.5 1.3 %collective-permute-done.24.refs_3_ = bf16[32,1664]{1,0:T(8,128)(2,1)S(1)} collective-permute-done((bf16[32,1664]{1,0:T(8,128)(2,1)S(1)}, bf16[32,1664]{1,0:T(8,128)(2,1)S(1)}, u32[]{:S(2)}, u32[]{:S(2)}) %collective-permute-start.24) | collective-permute-done | bytes 106528 | tf_op jit(solution)/shard_map/ppermute | solution.py:295
  109.8 4.7 %step.7 = (f32[2,3072]{1,0:T(2,128)}, f32[32,8,256]{2,1,0:T(8,128)}, f32[2,3072]{1,0:T(2,128)}, f32[2]{0:T(128)}) custom-call(s32[1]{0:T(128)} %bitcast.place_ref.refs_0_, bf16[8,256,3072]{2,1,0:T(8,128)(2,1)S(1)} %get-tuple-element.36.refs_1_, bf16[32,1664]{1,0:T(8,128)(2,1)S(1)} %add.63.refs_2_, bf16[32,1664]{1,0:T(8,128)(2,1)S(1)} %collective-permute-done.24.refs_3_, ...), custom_call_target="tpu_custom_call" | custom-call | tf_op jit(solution)/shard_map/step/pallas_call | solution.py:435
  (21 shorter events, 0.5 us)
Async XLA Ops:
  0.6 11.2 %copy-start = (f32[2,3072]{1,0:T(2,128)S(1)}, f32[2,3072]{1,0:T(2,128)}, u32[]{:S(2)}) copy-start(f32[2,3072]{1,0:T(2,128)} %x_ref.1) | copy-start | bytes 73732
  0.6 32.8 %copy-start.1 = (f32[2]{0:T(128)S(1)}, f32[2]{0:T(128)}, u32[]{:S(2)}) copy-start(f32[2]{0:T(128)} %param.24) | copy-start | bytes 28
  7.4 1.5 %collective-permute-start = (bf16[32,1664]{1,0:T(8,128)(2,1)S(1)}, bf16[32,1664]{1,0:T(8,128)(2,1)S(1)}, u32[]{:S(2)}, u32[]{:S(2)}) collective-permute-start(bf16[32,1664]{1,0:T(8,128)(2,1)S(1)} %get-tuple-element.38), channel_id=1, source_target_pairs={{0,1},{1,0},{2,3},{3,2},{4,5},{5,4},{6,7},{7,6},{8,9},{9,8},{10,11... | collective-permute-start | bytes 319496 | tf_op jit(solution)/shard_map/ppermute | solution.py:295
  8.9 9.7 %collective-permute-start.1 = (bf16[32,1664]{1,0:T(8,128)(2,1)S(1)}, bf16[32,1664]{1,0:T(8,128)(2,1)S(1)}, u32[]{:S(2)}, u32[]{:S(2)}) collective-permute-start(bf16[32,1664]{1,0:T(8,128)(2,1)S(1)} %add.48), channel_id=1, source_target_pairs={{0,2},{1,3},{2,0},{3,1},{4,6},{5,7},{6,4},{7,5},{8,10},{9,11},{10,... | collective-permute-start | bytes 319496 | tf_op jit(solution)/shard_map/ppermute | solution.py:295
  11.9 1.2 %collective-permute-start.5 = (f32[2,1536]{1,0:T(2,128)S(1)}, f32[2,1536]{1,0:T(2,128)S(1)}, u32[]{:S(2)}, u32[]{:S(2)}) collective-permute-start(f32[2,1536]{1,0:T(2,128)S(1)} %get-tuple-element.40), channel_id=1, source_target_pairs={{0,1},{1,0},{2,3},{3,2},{4,5},{5,4},{6,7},{7,6},{8,9},{9,8},{10,11... | collective-permute-start | bytes 36872 | tf_op jit(solution)/shard_map/ppermute | solution.py:295
  13.1 3.9 %collective-permute-start.6 = (f32[4,1536]{1,0:T(4,128)S(1)}, f32[4,1536]{1,0:T(4,128)S(1)}, u32[]{:S(2)}, u32[]{:S(2)}) collective-permute-start(f32[4,1536]{1,0:T(4,128)S(1)} %join.4.first_ref), channel_id=1, source_target_pairs={{0,2},{1,3},{2,0},{3,1},{4,6},{5,7},{6,4},{7,5},{8,10},{9,11},{10,... | collective-permute-start | bytes 73736 | tf_op jit(solution)/shard_map/ppermute | solution.py:295
  17.0 4.6 %collective-permute-start.7 = (f32[8,1536]{1,0:T(8,128)S(1)}, f32[8,1536]{1,0:T(8,128)S(1)}, u32[]{:S(2)}, u32[]{:S(2)}) collective-permute-start(f32[8,1536]{1,0:T(8,128)S(1)} %join.5.first_ref), channel_id=1, source_target_pairs={{0,4},{1,5},{2,6},{3,7},{4,0},{5,1},{6,2},{7,3},{8,12},{9,13},{10,... | collective-permute-start | bytes 147464 | tf_op jit(solution)/shard_map/ppermute | solution.py:295
  18.6 5.8 %collective-permute-start.2 = (bf16[32,1664]{1,0:T(8,128)(2,1)S(1)}, bf16[32,1664]{1,0:T(8,128)(2,1)S(1)}, u32[]{:S(2)}, u32[]{:S(2)}) collective-permute-start(bf16[32,1664]{1,0:T(8,128)(2,1)S(1)} %add.49), channel_id=1, source_target_pairs={{0,4},{1,5},{2,6},{3,7},{4,0},{5,1},{6,2},{7,3},{8,12},{9,13},{10,... | collective-permute-start | bytes 319496 | tf_op jit(solution)/shard_map/ppermute | solution.py:295
  21.6 9.2 %collective-permute-start.8 = (f32[16,1536]{1,0:T(8,128)S(1)}, f32[16,1536]{1,0:T(8,128)S(1)}, u32[]{:S(2)}, u32[]{:S(2)}) collective-permute-start(f32[16,1536]{1,0:T(8,128)S(1)} %join.6.first_ref), channel_id=1, source_target_pairs={{0,8},{1,9},{2,10},{3,11},{4,12},{5,13},{6,14},{7,15},{8,0},{9,1},... | collective-permute-start | bytes 294920 | tf_op jit(solution)/shard_map/ppermute | solution.py:295
  24.5 7.5 %collective-permute-start.3 = (bf16[32,1664]{1,0:T(8,128)(2,1)S(1)}, bf16[32,1664]{1,0:T(8,128)(2,1)S(1)}, u32[]{:S(2)}, u32[]{:S(2)}) collective-permute-start(bf16[32,1664]{1,0:T(8,128)(2,1)S(1)} %add.50), channel_id=1, source_target_pairs={{0,8},{1,9},{2,10},{3,11},{4,12},{5,13},{6,14},{7,15},{8,0},{9,1},... | collective-permute-start | bytes 319496 | tf_op jit(solution)/shard_map/ppermute | solution.py:295
  30.9 1.5 %collective-permute-start.9 = (f32[32,1536]{1,0:T(8,128)S(1)}, f32[32,1536]{1,0:T(8,128)S(1)}, u32[]{:S(2)}, u32[]{:S(2)}) collective-permute-start(f32[32,1536]{1,0:T(8,128)S(1)} %join.7.refs_4_), channel_id=1, source_target_pairs={{0,1},{1,0},{2,3},{3,2},{4,5},{5,4},{6,7},{7,6},{8,9},{9,8},{10,11... | collective-permute-start | bytes 589832 | tf_op jit(solution)/shard_map/ppermute | solution.py:295
  32.0 1.4 %collective-permute-start.4 = (bf16[32,1664]{1,0:T(8,128)(2,1)S(1)}, bf16[32,1664]{1,0:T(8,128)(2,1)S(1)}, u32[]{:S(2)}, u32[]{:S(2)}) collective-permute-start(bf16[32,1664]{1,0:T(8,128)(2,1)S(1)} %add.51.refs_2_), channel_id=1, source_target_pairs={{0,1},{1,0},{2,3},{3,2},{4,5},{5,4},{6,7},{7,6},{8,9},{9,8},{10,11... | collective-permute-start | bytes 319496 | tf_op jit(solution)/shard_map/ppermute | solution.py:295
  39.5 1.4 %collective-permute-start.10 = (bf16[32,1664]{1,0:T(8,128)(2,1)S(1)}, bf16[32,1664]{1,0:T(8,128)(2,1)S(1)}, u32[]{:S(2)}, u32[]{:S(2)}) collective-permute-start(bf16[32,1664]{1,0:T(8,128)(2,1)S(1)} %get-tuple-element.48), channel_id=1, source_target_pairs={{0,1},{1,0},{2,3},{3,2},{4,5},{5,4},{6,7},{7,6},{8,9},{9,8},{10,11... | collective-permute-start | bytes 319496 | tf_op jit(solution)/shard_map/ppermute | solution.py:295
  40.9 5.1 %collective-permute-start.11 = (bf16[32,1664]{1,0:T(8,128)(2,1)S(1)}, bf16[32,1664]{1,0:T(8,128)(2,1)S(1)}, u32[]{:S(2)}, u32[]{:S(2)}) collective-permute-start(bf16[32,1664]{1,0:T(8,128)(2,1)S(1)} %add.52), channel_id=1, source_target_pairs={{0,2},{1,3},{2,0},{3,1},{4,6},{5,7},{6,4},{7,5},{8,10},{9,11},{10,... | collective-permute-start | bytes 319496 | tf_op jit(solution)/shard_map/ppermute | solution.py:295
  46.1 4.8 %collective-permute-start.12 = (bf16[32,1664]{1,0:T(8,128)(2,1)S(1)}, bf16[32,1664]{1,0:T(8,128)(2,1)S(1)}, u32[]{:S(2)}, u32[]{:S(2)}) collective-permute-start(bf16[32,1664]{1,0:T(8,128)(2,1)S(1)} %add.53), channel_id=1, source_target_pairs={{0,4},{1,5},{2,6},{3,7},{4,0},{5,1},{6,2},{7,3},{8,12},{9,13},{10,... | collective-permute-start | bytes 319496 | tf_op jit(solution)/shard_map/ppermute | solution.py:295
  50.9 6.7 %collective-permute-start.13 = (bf16[32,1664]{1,0:T(8,128)(2,1)S(1)}, bf16[32,1664]{1,0:T(8,128)(2,1)S(1)}, u32[]{:S(2)}, u32[]{:S(2)}) collective-permute-start(bf16[32,1664]{1,0:T(8,128)(2,1)S(1)} %add.54), channel_id=1, source_target_pairs={{0,8},{1,9},{2,10},{3,11},{4,12},{5,13},{6,14},{7,15},{8,0},{9,1},... | collective-permute-start | bytes 319496 | tf_op jit(solution)/shard_map/ppermute | solution.py:295
  57.6 1.4 %collective-permute-start.14 = (bf16[32,1664]{1,0:T(8,128)(2,1)S(1)}, bf16[32,1664]{1,0:T(8,128)(2,1)S(1)}, u32[]{:S(2)}, u32[]{:S(2)}) collective-permute-start(bf16[32,1664]{1,0:T(8,128)(2,1)S(1)} %add.55.refs_2_), channel_id=1, source_target_pairs={{0,1},{1,0},{2,3},{3,2},{4,5},{5,4},{6,7},{7,6},{8,9},{9,8},{10,11... | collective-permute-start | bytes 319496 | tf_op jit(solution)/shard_map/ppermute | solution.py:295
  65.4 1.4 %collective-permute-start.15 = (bf16[32,1664]{1,0:T(8,128)(2,1)S(1)}, bf16[32,1664]{1,0:T(8,128)(2,1)S(1)}, u32[]{:S(2)}, u32[]{:S(2)}) collective-permute-start(bf16[32,1664]{1,0:T(8,128)(2,1)S(1)} %get-tuple-element.55), channel_id=1, source_target_pairs={{0,1},{1,0},{2,3},{3,2},{4,5},{5,4},{6,7},{7,6},{8,9},{9,8},{10,11... | collective-permute-start | bytes 319496 | tf_op jit(solution)/shard_map/ppermute | solution.py:295
  66.9 5.1 %collective-permute-start.16 = (bf16[32,1664]{1,0:T(8,128)(2,1)S(1)}, bf16[32,1664]{1,0:T(8,128)(2,1)S(1)}, u32[]{:S(2)}, u32[]{:S(2)}) collective-permute-start(bf16[32,1664]{1,0:T(8,128)(2,1)S(1)} %add.56), channel_id=1, source_target_pairs={{0,2},{1,3},{2,0},{3,1},{4,6},{5,7},{6,4},{7,5},{8,10},{9,11},{10,... | collective-permute-start | bytes 319496 | tf_op jit(solution)/shard_map/ppermute | solution.py:295
  72.0 4.8 %collective-permute-start.17 = (bf16[32,1664]{1,0:T(8,128)(2,1)S(1)}, bf16[32,1664]{1,0:T(8,128)(2,1)S(1)}, u32[]{:S(2)}, u32[]{:S(2)}) collective-permute-start(bf16[32,1664]{1,0:T(8,128)(2,1)S(1)} %add.57), channel_id=1, source_target_pairs={{0,4},{1,5},{2,6},{3,7},{4,0},{5,1},{6,2},{7,3},{8,12},{9,13},{10,... | collective-permute-start | bytes 319496 | tf_op jit(solution)/shard_map/ppermute | solution.py:295
  76.8 6.3 %collective-permute-start.18 = (bf16[32,1664]{1,0:T(8,128)(2,1)S(1)}, bf16[32,1664]{1,0:T(8,128)(2,1)S(1)}, u32[]{:S(2)}, u32[]{:S(2)}) collective-permute-start(bf16[32,1664]{1,0:T(8,128)(2,1)S(1)} %add.58), channel_id=1, source_target_pairs={{0,8},{1,9},{2,10},{3,11},{4,12},{5,13},{6,14},{7,15},{8,0},{9,1},... | collective-permute-start | bytes 319496 | tf_op jit(solution)/shard_map/ppermute | solution.py:295
  83.1 1.4 %collective-permute-start.19 = (bf16[32,1664]{1,0:T(8,128)(2,1)S(1)}, bf16[32,1664]{1,0:T(8,128)(2,1)S(1)}, u32[]{:S(2)}, u32[]{:S(2)}) collective-permute-start(bf16[32,1664]{1,0:T(8,128)(2,1)S(1)} %add.59.refs_2_), channel_id=1, source_target_pairs={{0,1},{1,0},{2,3},{3,2},{4,5},{5,4},{6,7},{7,6},{8,9},{9,8},{10,11... | collective-permute-start | bytes 319496 | tf_op jit(solution)/shard_map/ppermute | solution.py:295
  90.8 1.4 %collective-permute-start.20 = (bf16[32,1664]{1,0:T(8,128)(2,1)S(1)}, bf16[32,1664]{1,0:T(8,128)(2,1)S(1)}, u32[]{:S(2)}, u32[]{:S(2)}) collective-permute-start(bf16[32,1664]{1,0:T(8,128)(2,1)S(1)} %get-tuple-element.62), channel_id=1, source_target_pairs={{0,1},{1,0},{2,3},{3,2},{4,5},{5,4},{6,7},{7,6},{8,9},{9,8},{10,11... | collective-permute-start | bytes 319496 | tf_op jit(solution)/shard_map/ppermute | solution.py:295
  92.2 5.1 %collective-permute-start.21 = (bf16[32,1664]{1,0:T(8,128)(2,1)S(1)}, bf16[32,1664]{1,0:T(8,128)(2,1)S(1)}, u32[]{:S(2)}, u32[]{:S(2)}) collective-permute-start(bf16[32,1664]{1,0:T(8,128)(2,1)S(1)} %add.60), channel_id=1, source_target_pairs={{0,2},{1,3},{2,0},{3,1},{4,6},{5,7},{6,4},{7,5},{8,10},{9,11},{10,... | collective-permute-start | bytes 319496 | tf_op jit(solution)/shard_map/ppermute | solution.py:295
  97.3 4.8 %collective-permute-start.22 = (bf16[32,1664]{1,0:T(8,128)(2,1)S(1)}, bf16[32,1664]{1,0:T(8,128)(2,1)S(1)}, u32[]{:S(2)}, u32[]{:S(2)}) collective-permute-start(bf16[32,1664]{1,0:T(8,128)(2,1)S(1)} %add.61), channel_id=1, source_target_pairs={{0,4},{1,5},{2,6},{3,7},{4,0},{5,1},{6,2},{7,3},{8,12},{9,13},{10,... | collective-permute-start | bytes 319496 | tf_op jit(solution)/shard_map/ppermute | solution.py:295
  102.1 6.3 %collective-permute-start.23 = (bf16[32,1664]{1,0:T(8,128)(2,1)S(1)}, bf16[32,1664]{1,0:T(8,128)(2,1)S(1)}, u32[]{:S(2)}, u32[]{:S(2)}) collective-permute-start(bf16[32,1664]{1,0:T(8,128)(2,1)S(1)} %add.62), channel_id=1, source_target_pairs={{0,8},{1,9},{2,10},{3,11},{4,12},{5,13},{6,14},{7,15},{8,0},{9,1},... | collective-permute-start | bytes 319496 | tf_op jit(solution)/shard_map/ppermute | solution.py:295
  108.4 1.4 %collective-permute-start.24 = (bf16[32,1664]{1,0:T(8,128)(2,1)S(1)}, bf16[32,1664]{1,0:T(8,128)(2,1)S(1)}, u32[]{:S(2)}, u32[]{:S(2)}) collective-permute-start(bf16[32,1664]{1,0:T(8,128)(2,1)S(1)} %add.63.refs_2_), channel_id=1, source_target_pairs={{0,1},{1,0},{2,3},{3,2},{4,5},{5,4},{6,7},{7,6},{8,9},{9,8},{10,11... | collective-permute-start | bytes 319496 | tf_op jit(solution)/shard_map/ppermute | solution.py:295

commit v2 on v1

v2 whole, which is shorter than its diff:
```python
import functools
import math

import jax
import jax.numpy as jnp
from jax import lax
from jax.experimental import pallas as pl
from jax.experimental.pallas import tpu as pltpu
from jax.sharding import PartitionSpec as P

ITERS = 4
LANES = 128
WIDE = 256
MIB = 2**20
HALF = jnp.bfloat16
FULL = jnp.float32

PIECES = 4

VMEM = pl.BlockSpec(memory_space=pltpu.VMEM)
SMEM = pl.BlockSpec(memory_space=pltpu.SMEM)
HBM = pl.BlockSpec(memory_space=pltpu.HBM)


def near(*shape, dtype=FULL):
    return pltpu.VMEM(shape, dtype)


def far(x):
    return pltpu.with_memory_space_constraint(x, pltpu.HBM)


def call(kernel, name, us, operands, out_shape, scratch=(), smem=(), smem_out=(), limit=12):
    return pl.pallas_call(
        kernel,
        out_shape=tuple(out_shape),
        in_specs=[SMEM if j in smem else VMEM for j in range(len(operands))],
        out_specs=tuple(SMEM if j in smem_out else VMEM for j in range(len(out_shape))),
        scratch_shapes=list(scratch),
        compiler_params=pltpu.CompilerParams(vmem_limit_bytes=limit * MIB),
        cost_estimate=pl.CostEstimate(flops=0, bytes_accessed=int(us * 3.69e6), transcendentals=0),
        name=name,
    )(*operands)


def total(x):
    return jnp.sum(jnp.sum(x, axis=1, keepdims=True), axis=0, keepdims=True)


def piece_at(piece, units):
    return (piece % 2) * (units // 2) + (piece // 2) * (units // 4)


def own_first(place, s, width):
    core = place % 2
    return pl.multiple_of((core if s == 0 else 1 - core) * width, LANES)


def add_rows(values, first, rows):
    row = lax.broadcasted_iota(jnp.int32, values.shape, 0)
    for j, extra in enumerate(rows):
        values = values + jnp.where(row == first + j, extra, 0.0)
    return values


def hour_terms(cost, ramp, on, price_terms):
    hours = len(cost)
    rows = []
    for j in range(hours + 1):
        if j == hours:
            rows.append(on * ramp[j - 1])
            continue
        row = cost[j] + on * ((ramp[j - 1] if j else 0.0) - ramp[j])
        if price_terms is not None:
            row = row + price_terms[j]
        rows.append(row)
    return rows


def scalar_block(value, place, shape):
    row = lax.broadcasted_iota(jnp.int32, shape, 0)
    lane = lax.broadcasted_iota(jnp.int32, shape, 1)
    block = jnp.zeros(shape, FULL)
    left = value
    for j in range(3):
        part = left.astype(HALF).astype(FULL)
        left = left - part
        block = block + jnp.where((row == j) & (lane == place), part, 0.0)
    return block.astype(HALF)


def start_kernel(
    place_ref,
    gate_hbm,
    tiles_ref,
    dual_ref,
    base_ref,
    monitored_ref,
    ratings_ref,
    floor_ref,
    span_ref,
    limit_ref,
    on_ref,
    cost_ref,
    ramp_ref,
    level_ref,
    masked_ref,
    send_a,
    keep_a,
    send_b,
    keep_b,
    dual_out,
    base_out,
    rating_out,
    unit_out,
    cost_out,
    ramp_out,
    gate_ref,
    acc_ref,
    sems,
    gate_sem,
):
    ctgs, lines, units = masked_ref.shape
    width, quarter = units // 2, units // 4
    half_tiles = width // LANES
    all_hours, hours = dual_ref.shape[0], cost_ref.shape[0]
    place = place_ref[0]

    def copy(k, s):
        return pltpu.make_async_copy(
            tiles_ref.at[k, :, pl.ds(own_first(place, s, width), width)],
            masked_ref.at[k, :, pl.ds(s * width, width)],
            sems.at[k, s],
        )

    gates = pltpu.make_async_copy(gate_hbm, gate_ref, gate_sem)
    gates.start()
    for k in range(ctgs):
        for s in range(2):
            copy(k, s).start()

    table = ratings_ref[...].T
    hi = table.astype(HALF)
    left = table - hi.astype(FULL)
    mid = left.astype(HALF)
    lo = (left - mid.astype(FULL)).astype(HALF)
    groups = table.shape[1]
    for k in range(ctgs):
        cols = pl.ds(k * lines, lines)
        dual_out[:, cols] = dual_ref[:, k, :]
        base_out[:, cols] = base_ref[:, k, :]
        index = monitored_ref[k : k + 1, :]
        group = lax.broadcasted_iota(jnp.int32, (groups, lines), 0)
        chosen = (group == index // LANES).astype(FULL).astype(HALF)
        picked = (
            jnp.dot(hi, chosen, preferred_element_type=FULL)
            + jnp.dot(mid, chosen, preferred_element_type=FULL)
            + jnp.dot(lo, chosen, preferred_element_type=FULL)
        )
        lane = lax.broadcasted_iota(jnp.int32, (LANES, lines), 0)
        rating_out[:, cols] = jnp.sum(jnp.where(lane == index % LANES, picked, 0.0), axis=0, keepdims=True)
    for s in range(2):
        cols, own = pl.ds(s * width, width), pl.ds(own_first(place, s, width), width)
        floor = floor_ref[:, own]
        unit_out[0:1, cols] = floor
        unit_out[1:2, cols] = floor + span_ref[:, own]
        unit_out[2:3, cols] = limit_ref[:, own]
        unit_out[3:4, cols] = on_ref[:, own].astype(FULL)
        cost_out[:, cols] = cost_ref[:, own]
        ramp_out[:, cols] = ramp_ref[:, own]

    gates.wait()
    for k in range(ctgs):
        lhs = dual_out[:, pl.ds(k * lines, lines)].astype(HALF)
        for s in range(2):
            copy(k, s).wait()
            gate_at = (place % 2 if s == 0 else 1 - place % 2) * half_tiles
            for j in range(0, half_tiles, 2):
                at = s * width + j * LANES
                block = []
                for m in range(lines // LANES):
                    line = []
                    for i in range(2):
                        gate = gate_ref[k, m, gate_at + j + i]
                        part = masked_ref[k, pl.ds(m * LANES, LANES), pl.ds(at + i * LANES, LANES)]
                        line.append(jnp.where(gate > 0, part, jnp.zeros((), HALF)))
                    block.append(jnp.concatenate(line, axis=1))
                block = jnp.concatenate(block, axis=0)
                cols = pl.ds(at, WIDE)
                masked_ref[k, :, cols] = block
                part = jnp.dot(lhs, block, preferred_element_type=FULL)
                acc_ref[:, cols] = part if k == 0 else acc_ref[:, cols] + part

    for piece, out_ref in enumerate((keep_a, send_a, keep_b, send_b)):
        cols = pl.ds(piece_at(piece, units), quarter)
        rows = hour_terms(
            [cost_out[j : j + 1, cols] for j in range(hours)],
            [ramp_out[j : j + 1, cols] for j in range(hours)],
            unit_out[3:4, cols],
            None,
        )
        values = add_rows(acc_ref[:, cols], place * hours, rows)
        own = pl.multiple_of(own_first(place, piece % 2, width) + (piece // 2) * quarter, LANES)
        level = level_ref[:, pl.ds(own, quarter)]
        high = level.astype(HALF).astype(FULL)
        message = jnp.concatenate([values, high, level - high], axis=0)
        rest = out_ref.shape[1] - quarter
        if rest:
            message = jnp.concatenate([message, jnp.zeros((out_ref.shape[0], rest), FULL)], axis=1)
        out_ref[...] = message.astype(HALF)


def turn_kernel(first_ctg, masked_ref, before_ref, out_ref):
    ctgs, units, lines = out_ref.shape
    for k in range(ctgs):
        for at in range(0, units, WIDE):
            out_ref[k, pl.ds(at, WIDE), :] = masked_ref[first_ctg + k, :, pl.ds(at, WIDE)].T


def starting_levels(piece, devices, place, message_ref, all_hours, quarter):
    hours = all_hours // devices
    levels = message_ref[all_hours:, :quarter]
    shape = (all_hours, levels.shape[0])
    hour = lax.broadcasted_iota(jnp.int32, shape, 0)
    row = lax.broadcasted_iota(jnp.int32, shape, 1)
    apart = place ^ (hour // hours) ^ (piece % 2)
    block = jnp.zeros(shape, jnp.int32)
    for bit, mask in enumerate([1] + mask_order(devices, piece // 2)):
        block = block + ((apart // mask) % 2) * 2**bit
    chosen = (row // (2 * hours) == block) & (row % hours == hour % hours)
    return jnp.dot(chosen.astype(FULL).astype(HALF), levels, preferred_element_type=FULL)


def primal_piece(piece, step_size, stat_ref, message_ref, levels, unit_ref, moved_ref):
    all_hours, quarter = levels.shape
    cols = pl.ds(piece_at(piece, unit_ref.shape[1]), quarter)
    primal_step = step_size / stat_ref[0:1, 0:1]
    gradient = message_ref[:all_hours, :quarter].astype(FULL)
    moved = jnp.clip(levels - primal_step * gradient, unit_ref[0:1, cols], unit_ref[1:2, cols])
    moved_ref[...] = moved
    return (2.0 * moved - levels).astype(HALF)


def piece_flows(piece, half, turned_refs, k):
    turned_ref = turned_refs[k // turned_refs[0].shape[0]]
    rows = pl.ds(piece_at(piece, turned_ref.shape[1]), half.shape[1])
    return jnp.dot(half, turned_ref[k % turned_refs[0].shape[0], rows, :], preferred_element_type=FULL)


def flow_kernel(step_size, piece, devices, turns, first, *refs):
    refs = list(refs)
    turned_refs = [refs.pop(0) for _ in range(turns)]
    place_ref = refs.pop(0)
    message_ref, unit_ref = refs[:2]
    del refs[:2]
    level_ref = None if first else refs.pop(0)
    stat_ref = None if first and piece == 0 else refs.pop(0)
    flow_ref = refs.pop(0) if piece else None
    moved_ref, flow_out = refs[:2]
    del refs[:2]
    all_hours, quarter = moved_ref.shape
    if first:
        level_out = refs.pop(0)
        levels = starting_levels(piece, devices, place_ref[0], message_ref, all_hours, quarter)
        level_out[...] = levels
    else:
        levels = level_ref[...]
    if piece == 0:
        stat_out = refs.pop(0)
        if first:
            stat_out[...] = jnp.full(stat_out.shape, 1.0, FULL)
        else:
            dual_sq = total(message_ref[:all_hours, quarter:].astype(FULL))
            primal_sq = stat_ref[1:2, 0:1]
            ratio = (dual_sq + 1e-06) / (primal_sq + 1e-06)
            weight = jnp.sqrt(stat_ref[0:1, 0:1]) * jnp.sqrt(jnp.sqrt(ratio))
            stat_out[...] = jnp.broadcast_to(weight, stat_out.shape)
        stat_ref = stat_out
    half = primal_piece(piece, step_size, stat_ref, message_ref, levels, unit_ref, moved_ref)
    lines = turned_refs[0].shape[2]
    for k in range(turns * turned_refs[0].shape[0]):
        at = pl.ds(k * lines, lines)
        part = piece_flows(piece, half, turned_refs, k)
        flow_out[:, at] = part if flow_ref is None else flow_ref[:, at] + part


def dual_kernel(step_size, balance, devices, turns, first, last, *refs):
    refs = list(refs)
    turned_refs = [refs.pop(0) for _ in range(turns)]
    place_ref, masked_ref, message_ref = refs[:3]
    del refs[:3]
    level_refs = [refs.pop(0) for _ in range(3 if first else 4)]
    moved_refs = [refs.pop(0) for _ in range(3)]
    stat_ref, flow_ref, dual_ref, base_ref, rating_ref, unit_ref, cost_ref, demand_ref, ramp_ref = refs[:9]
    del refs[:9]
    price_ref = None if first else refs.pop(0)
    if first:
        level_refs.append(refs.pop())
    if last:
        level_out, dual_out, ramp_out, price_out, last_moved = refs
    else:
        last_moved, dual_out, ramp_out, price_out, stat_out, send_ref, keep_ref, half_dual, term_out = refs
    moved_refs = moved_refs + [last_moved]

    ctgs, lines, units = masked_ref.shape
    width, quarter = units // 2, units // 4
    all_hours, hours = level_refs[0].shape[0], cost_ref.shape[0]
    place = place_ref[0]
    first_hour = place * hours
    weight = stat_ref[0:1, 0:1]
    dual_step = step_size * weight

    if first:
        level_refs[3][...] = starting_levels(3, devices, place, message_ref, all_hours, quarter)
    half = primal_piece(3, step_size, stat_ref, message_ref, level_refs[3][...], unit_ref, last_moved)
    flow_acc = jnp.zeros((all_hours, lines), FULL)
    for k in range(ctgs):
        at = pl.ds(k * lines, lines)
        flows = flow_ref[:, at] + piece_flows(3, half, turned_refs, k)
        old = dual_ref[:, at]
        trial = old + dual_step * flows
        base, rating = base_ref[:, at], rating_ref[:, at]
        new = trial - jnp.clip(trial, dual_step * (base - rating), dual_step * (base + rating))
        if last:
            dual_out[:, k, :] = new
        else:
            dual_out[:, at] = new
            half_dual[:, at] = new.astype(HALF)
            flow_acc = flow_acc + (new - old) ** 2

    places = [pl.ds(piece_at(piece, units), quarter) for piece in range(PIECES)]
    moved_sq = None if last else total(flow_acc)
    supply = [jnp.zeros((1, 1), FULL) for _ in range(hours)]
    ramps = [[] for _ in range(hours)]
    for piece in range(PIECES):
        at = places[piece]
        ramp_limit, ramp_on = unit_ref[2:3, at], unit_ref[3:4, at]
        rows = []
        for j in range(hours + 1):
            spot = pl.ds(jnp.minimum(first_hour + j, all_hours - 1), 1)
            rows.append(2.0 * moved_refs[piece][spot, :] - level_refs[piece][spot, :])
        for j in range(hours):
            old = ramp_ref[j : j + 1, at]
            trial = old + dual_step * (ramp_on * (rows[j + 1] - rows[j]))
            reach = dual_step * ramp_limit
            new = trial - jnp.clip(trial, -reach, reach)
            supply[j] = supply[j] + jnp.sum(rows[j], axis=1, keepdims=True)
            ramps[j].append(new)
            if last:
                own = pl.multiple_of(own_first(place, piece % 2, width) + (piece // 2) * quarter, LANES)
                level_out[j : j + 1, pl.ds(own, quarter)] = moved_refs[piece][pl.ds(first_hour + j, 1), :]
                ramp_out[j : j + 1, pl.ds(own, quarter)] = new
            else:
                ramp_out[j : j + 1, at] = new
                moved_sq = moved_sq + total((new - old) ** 2)
    prices = []
    for j in range(hours):
        old = jnp.zeros((1, 1), FULL) if first else price_ref[j : j + 1, :]
        new = old + dual_step * (balance * (supply[j] - demand_ref[0:1, j : j + 1]))
        prices.append(balance * new)
        if last:
            price_out[j] = new[0, 0]
        else:
            price_out[j : j + 1, :] = new
            moved_sq = moved_sq + (new - old) ** 2
    if last:
        return

    primal_acc = jnp.zeros((all_hours, quarter), FULL)
    for piece in range(PIECES):
        primal_acc = primal_acc + (moved_refs[piece][...] - level_refs[piece][...]) ** 2
    row = lax.broadcasted_iota(jnp.int32, stat_out.shape, 0)
    stat_out[...] = jnp.where(row == 0, weight, total(primal_acc))
    for piece in range(PIECES):
        at = places[piece]
        terms = hour_terms(
            [cost_ref[j : j + 1, at] for j in range(hours)],
            [ramps[j][piece] for j in range(hours)],
            unit_ref[3:4, at],
            prices,
        )
        for j, term in enumerate(terms):
            term_out[j : j + 1, at] = term
    block = scalar_block(moved_sq, place, (all_hours, LANES))
    pull_pieces(0, hours, first_hour, masked_ref, half_dual, term_out, send_ref, keep_ref)
    for out_ref in (send_ref, keep_ref):
        out_ref[:, quarter:] = block


def pull_pieces(q, hours, first_hour, masked_ref, half_dual, term_ref, send_ref, keep_ref):
    ctgs, lines, units = masked_ref.shape
    whole = masked_ref.reshape(ctgs * lines, units)
    for piece, out_ref in ((2 * q + 1, send_ref), (2 * q, keep_ref)):
        for at in range(0, units // 4, WIDE):
            cols = pl.ds(piece_at(piece, units) + at, WIDE)
            pulled = jnp.dot(half_dual[...], whole[:, cols], preferred_element_type=FULL)
            terms = [term_ref[j : j + 1, cols] for j in range(hours + 1)]
            out_ref[:, pl.ds(at, WIDE)] = add_rows(pulled, first_hour, terms).astype(HALF)


def pull_kernel(hours, place_ref, masked_ref, half_dual, term_ref, send_ref, keep_ref):
    pull_pieces(1, hours, place_ref[0] * hours, masked_ref, half_dual, term_ref, send_ref, keep_ref)


def add_kernel(own_ref, received_ref, before_ref, out_ref):
    out_ref[...] = (own_ref[...].astype(FULL) + received_ref[...].astype(FULL)).astype(HALF)


def add_after(own, received, before):
    return call(add_kernel, "add", 0.1, [own, received, before], [near(*own.shape, dtype=HALF)])[0]


def join_kernel(all_hours, own_ref, received_ref, *refs):
    out_ref, scratch_ref = refs[-2:]
    extra = own_ref.shape[0] - all_hours
    own, received = own_ref[...].astype(FULL), received_ref[...].astype(FULL)
    scratch_ref[:all_hours, :] = own[:all_hours] + received[:all_hours]
    scratch_ref[all_hours : all_hours + extra, :] = own[all_hours:]
    scratch_ref[all_hours + extra :, :] = received[all_hours:]
    out_ref[...] = scratch_ref[...].astype(HALF)


def join(all_hours, own, received, *before):
    shape = (2 * own.shape[0] - all_hours, own.shape[1])
    kernel = functools.partial(join_kernel, all_hours)
    return call(kernel, "join", 0.2, [own, received, *before], [near(*shape, dtype=HALF)], [near(*shape)])[0]


def exchange(x, mask):
    devices = lax.axis_size("ctg")
    return lax.ppermute(x, "ctg", [(i, i ^ mask) for i in range(devices)])


def mask_order(devices, q):
    masks = [1 << b for b in range(1, devices.bit_length() - 1)]
    return masks if q == 0 else masks[-1:] + masks[:-1]


def body(
    flow_tiles,
    tile_pattern,
    monitored,
    ratings,
    base_flow,
    unit_cost,
    unit_floor,
    unit_span,
    ramp_limit,
    ramp_mask,
    demand,
    start_output,
    start_flow_dual,
    start_ramp_dual,
):
    ctgs, lines, units = flow_tiles.shape
    all_hours, hours = start_flow_dual.shape[0], start_output.shape[0]
    devices = lax.axis_size("ctg")
    here = lax.axis_index("ctg").astype(jnp.int32).reshape(1)
    quarter = units // 4
    assert devices & (devices - 1) == 0 and 2 <= devices <= LANES and quarter % WIDE == 0
    step_size = 0.5 / (2.0 + math.sqrt(ctgs * devices * lines / units))
    balance = 1.0 / math.sqrt(units)
    spread = -ratings.shape[0] % (8 * LANES)
    table = jnp.pad(ratings, (0, spread)).reshape(-1, LANES)
    row = lambda x: x.reshape(1, units)
    start_rows = all_hours + 2 * hours
    start_a, start_b = near(start_rows, quarter + LANES, dtype=HALF), near(start_rows, quarter, dtype=HALF)
    message_a, message_b = near(all_hours, quarter + LANES, dtype=HALF), near(all_hours, quarter, dtype=HALF)

    operands = [flow_tiles, start_flow_dual, base_flow, monitored, table, row(unit_floor), row(unit_span)]
    operands += [row(ramp_limit), row(ramp_mask), unit_cost, start_ramp_dual, start_output]
    masked, send_a, keep_a, send_b, keep_b, dual, base, rating, unit, cost, ramp = pl.pallas_call(
        start_kernel,
        out_shape=(
            near(ctgs, lines, units, dtype=HALF),
            start_a,
            start_a,
            start_b,
            start_b,
            near(all_hours, ctgs * lines),
            near(all_hours, ctgs * lines),
            near(1, ctgs * lines),
            near(4, units),
            near(hours, units),
            near(hours, units),
        ),
        in_specs=[SMEM, HBM, HBM] + [VMEM] * 11,
        out_specs=(VMEM,) * 11,
        scratch_shapes=[
            pltpu.SMEM(tile_pattern.shape, jnp.int32),
            near(all_hours, units),
            pltpu.SemaphoreType.DMA((ctgs, 2)),
            pltpu.SemaphoreType.DMA,
        ],
        compiler_params=pltpu.CompilerParams(vmem_limit_bytes=44 * MIB),
        name="start",
    )(here, far(tile_pattern), *[far(x) for x in operands])
    masked = pltpu.with_memory_space_constraint(masked, pltpu.VMEM)
    demands = demand.reshape(1, hours)
    price, stat, levels, turned = None, None, None, []
    for iteration in range(ITERS):
        first, last = iteration == 0, iteration == ITERS - 1
        merge = functools.partial(join, all_hours) if first else jnp.add
        owns = [merge(keep_a, exchange(send_a, 1)), merge(keep_b, exchange(send_b, 1))]
        orders = [mask_order(devices, q) for q in range(2)]
        steps = len(orders[0])
        for step in range(steps):
            before = []
            if first:
                for turn in range(ctgs * step // steps, ctgs * (step + 1) // steps):
                    before += call(
                        functools.partial(turn_kernel, turn),
                        "turn",
                        0.45,
                        [masked, owns[0]],
                        [near(1, units, lines, dtype=HALF)],
                    )
                turned += before
            owns[0] = merge(owns[0], exchange(owns[0], orders[0][step]), *before)
            if first or step < steps - 1:
                owns[1] = merge(owns[1], exchange(owns[1], orders[1][step]))
        messages = [owns[0], exchange(owns[0], 1)]
        moved, flows = [], None
        levels = [] if first else levels
        for piece in range(3):
            if piece == 2:
                if not first:
                    owns[1] = add_after(owns[1], exchange(owns[1], orders[1][-1]), after)
                messages += [owns[1], exchange(owns[1], 1)]
            operands = [*turned, here, messages[piece], unit]
            operands += [] if first else [levels[piece]]
            operands += [] if first and piece == 0 else [stat]
            operands += [flows] if piece else []
            out_shape = [near(all_hours, quarter), near(all_hours, ctgs * lines)]
            out_shape += [near(all_hours, quarter)] if first else []
            out_shape += [] if piece else [near(8, LANES)]
            kernel = functools.partial(flow_kernel, step_size, piece, devices, len(turned), first)
            outs = call(kernel, "flow", 0.7, operands, out_shape, smem=(len(turned),))
            moved.append(outs[0])
            flows = outs[1]
            if first:
                levels.append(outs[2])
            if piece == 0:
                stat = after = outs[-1]
        operands = [*turned, here, masked, messages[3], *levels, *moved, stat, flows, dual, base, rating, unit, cost]
        operands += [demands, ramp] if first else [demands, ramp, price]
        kernel = functools.partial(dual_kernel, step_size, balance, devices, len(turned), first, last)
        smem = (len(turned),)
        if last:
            f32 = lambda *shape: jax.ShapeDtypeStruct(shape, FULL)
            out_shape = [f32(hours, units), f32(all_hours, ctgs, lines), f32(hours, units), f32(hours)]
            return call(kernel, "dual", 1.2, operands, out_shape, [near(all_hours, quarter)], smem, (3,))
        out_shape = [near(all_hours, quarter), near(all_hours, ctgs * lines), near(hours, units), near(hours, 1)]
        out_shape += [near(8, LANES), message_a, message_a, near(all_hours, ctgs * lines, dtype=HALF), near(8, units)]
        scratch = [near(all_hours, quarter)] if first else []
        outs = call(kernel, "dual", 2.1, operands, out_shape, scratch, smem)
        levels = (*moved, outs[0])
        dual, ramp, price, stat, send_a, keep_a, half_dual, terms = outs[1:]
        operands = [here, masked, half_dual, terms]
        send_b, keep_b = call(
            functools.partial(pull_kernel, hours), "pull", 1.2, operands, [message_b, message_b], smem=(0,)
        )


def solution(mesh):
    return jax.shard_map(
        body,
        mesh=mesh,
        in_specs=(
            P("ctg", None, None),
            P("ctg", None, None),
            P("ctg", None),
            P(),
            P("grp", "ctg", None),
            P(("grp", "ctg"), None),
            P(),
            P(),
            P(),
            P(),
            P(("grp", "ctg")),
            P(("grp", "ctg"), None),
            P("grp", "ctg", None),
            P(("grp", "ctg"), None),
        ),
        out_specs=(
            P(("grp", "ctg"), None),
            P("grp", "ctg", None),
            P(("grp", "ctg"), None),
            P(("grp", "ctg")),
        ),
        check_vma=False,
    )
```

time: 115 us -> 97.2 us (0.85)
  waiting for transfers between devices: 64.3 us -> 30.1 us
  starting transfers between devices: 18.4 us -> 35.2 us
    ppermute x25 -> x40, waiting for transfers between devices: 64.3 us -> 30.1 us  [exchange(): return lax.ppermute(x, 'ctg', [(i, i ^ mask) for i in range(devices)])]
    ppermute x25 -> x40, starting transfers between devices: 18.4 us -> 35.2 us  [exchange(): return lax.ppermute(x, 'ctg', [(i, i ^ mask) for i in range(devices)])]
    pallas_call x10 -> x39, Pallas kernels: 30.5 us -> 30.2 us  [the longest x38 23.7 us: call(): pl.pallas_call(kernel, out_shape=tuple(out_shape), in_specs=[SMEM if j in...]
  transfers between devices with their start and end apart: 25 -> 40, of which waited for: 24 -> 23; matrix products, arithmetic and copies ran while one was open for 0% -> 0% of each run, Pallas kernels for 0% -> 17%
where the time goes in v2:
time: 97.2 us; the launch traced here: 97.1 us
  starting transfers between devices  35.2 us (36%)
  Pallas kernels  30.2 us (31%)
  waiting for transfers between devices  30.1 us (31%)
  between operations  1.19 us (1%)
    ppermute x40, starting transfers between devices, exchange(): return lax.ppermute(x, 'ctg', [(i, i ^ mask) for i in range(devices)])  35.2 us
    ppermute x40, waiting for transfers between devices, exchange(): return lax.ppermute(x, 'ctg', [(i, i ^ mask) for i in range(devices)])  30.1 us
    pallas_call x38, Pallas kernels, call(): pl.pallas_call(kernel, out_shape=tuple(out_shape), in_specs=[SMEM if j in...  23.7 us
    pallas_call x1, Pallas kernels, body(): pl.pallas_call(start_kernel, out_shape=(near(ctgs, lines, units, dtype=HA...  6.51 us
  transfers between devices with their start and end apart: 40, of which 23 were waited for; matrix products, arithmetic and copies ran while one was open for 0% of the time, Pallas kernels for 17%

profile of v2, /device:TPU:0, one launch (start us, length us, event | category | flops | bytes accessed | tf_op | source)
XLA Modules:
  0.0 97.1 jit_solution(15712756311096850631)
XLA Ops:
  0.6 6.5 %start.1 = (bf16[8,256,3072]{2,1,0:T(8,128)(2,1)S(1)}, bf16[36,896]{1,0:T(8,128)(2,1)S(1)}, bf16[36,896]{1,0:T(8,128)(2,1)S(1)}, bf16[36,768]{1,0:T(8,128)(2,1)S...) custom-call(s32[1]{0:T(128)} %bitcast.place_ref.refs_8_, ...), custom_call_target="tpu_custom_call" | custom-call | tf_op jit(solution)/shard_map/start/pallas_call | solution.py:472
  7.2 0.5 collective-permute-start
  7.7 0.9 collective-permute-done.received_ref
  8.6 2.9 %collective-permute-start.1 = (bf16[40,896]{1,0:T(8,128)(2,1)S(1)}, bf16[40,896]{1,0:T(8,128)(2,1)S(1)}, u32[]{:S(2)}, u32[]{:S(2)}) collective-permute-start(bf16[40,896]{1,0:T(8,128)(2,1)S(1)} %join.8.before_ref.own_ref), channel_id=1, source_target_pairs={{0,2},{1,3},{2,0},{3,1},{4,6},{5,7},{6,4},{7,5},{8,10},{9,11},{10,... | collective-permute-start | bytes 215048 | tf_op jit(solution)/shard_map/ppermute | solution.py:431
  11.5 1.2 %collective-permute-done.3.received_ref = bf16[36,768]{1,0:T(8,128)(2,1)S(1)} collective-permute-done((bf16[36,768]{1,0:T(8,128)(2,1)S(1)}, bf16[36,768]{1,0:T(8,128)(2,1)S(1)}, u32[]{:S(2)}, u32[]{:S(2)}) %collective-permute-start.3) | collective-permute-done | bytes 55328 | tf_op jit(solution)/shard_map/ppermute | solution.py:431
  12.8 2.7 %collective-permute-start.4 = (bf16[40,768]{1,0:T(8,128)(2,1)S(1)}, bf16[40,768]{1,0:T(8,128)(2,1)S(1)}, u32[]{:S(2)}, u32[]{:S(2)}) collective-permute-start(bf16[40,768]{1,0:T(8,128)(2,1)S(1)} %join.11.own_ref), channel_id=1, source_target_pairs={{0,8},{1,9},{2,10},{3,11},{4,12},{5,13},{6,14},{7,15},{8,0},{9,1},... | collective-permute-start | bytes 184328 | tf_op jit(solution)/shard_map/ppermute | solution.py:431
  15.9 0.5 turn.8.refs_0_
  16.4 1.6 %collective-permute-start.2 = (bf16[48,896]{1,0:T(8,128)(2,1)S(1)}, bf16[48,896]{1,0:T(8,128)(2,1)S(1)}, u32[]{:S(2)}, u32[]{:S(2)}) collective-permute-start(bf16[48,896]{1,0:T(8,128)(2,1)S(1)} %join.9.before_ref.own_ref), channel_id=1, source_target_pairs={{0,4},{1,5},{2,6},{3,7},{4,0},{5,1},{6,2},{7,3},{8,12},{9,13},{10,... | collective-permute-start | bytes 258056 | tf_op jit(solution)/shard_map/ppermute | solution.py:431
  18.1 1.2 %collective-permute-done.4.received_ref = bf16[40,768]{1,0:T(8,128)(2,1)S(1)} collective-permute-done((bf16[40,768]{1,0:T(8,128)(2,1)S(1)}, bf16[40,768]{1,0:T(8,128)(2,1)S(1)}, u32[]{:S(2)}, u32[]{:S(2)}) %collective-permute-start.4) | collective-permute-done | bytes 61472 | tf_op jit(solution)/shard_map/ppermute | solution.py:431
  19.3 0.5 collective-permute-start.5
  21.2 1.4 %collective-permute-start.8 = (bf16[64,896]{1,0:T(8,128)(2,1)S(1)}, bf16[64,896]{1,0:T(8,128)(2,1)S(1)}, u32[]{:S(2)}, u32[]{:S(2)}) collective-permute-start(bf16[64,896]{1,0:T(8,128)(2,1)S(1)} %join.10.before_ref.own_ref), channel_id=1, source_target_pairs={{0,8},{1,9},{2,10},{3,11},{4,12},{5,13},{6,14},{7,15},{8,0},{9,1},... | collective-permute-start | bytes 344072 | tf_op jit(solution)/shard_map/ppermute | solution.py:431
  22.7 1.0 %collective-permute-done.5.received_ref = bf16[48,768]{1,0:T(8,128)(2,1)S(1)} collective-permute-done((bf16[48,768]{1,0:T(8,128)(2,1)S(1)}, bf16[48,768]{1,0:T(8,128)(2,1)S(1)}, u32[]{:S(2)}, u32[]{:S(2)}) %collective-permute-start.5) | collective-permute-done | bytes 73760 | tf_op jit(solution)/shard_map/ppermute | solution.py:431
  23.7 1.8 %collective-permute-start.6 = (bf16[64,768]{1,0:T(8,128)(2,1)S(1)}, bf16[64,768]{1,0:T(8,128)(2,1)S(1)}, u32[]{:S(2)}, u32[]{:S(2)}) collective-permute-start(bf16[64,768]{1,0:T(8,128)(2,1)S(1)} %join.13.own_ref), channel_id=1, source_target_pairs={{0,4},{1,5},{2,6},{3,7},{4,0},{5,1},{6,2},{7,3},{8,12},{9,13},{10,... | collective-permute-start | bytes 294920 | tf_op jit(solution)/shard_map/ppermute | solution.py:431
  26.9 2.2 %collective-permute-done.8.received_ref = bf16[64,896]{1,0:T(8,128)(2,1)S(1)} collective-permute-done((bf16[64,896]{1,0:T(8,128)(2,1)S(1)}, bf16[64,896]{1,0:T(8,128)(2,1)S(1)}, u32[]{:S(2)}, u32[]{:S(2)}) %collective-permute-start.8) | collective-permute-done | bytes 114720 | tf_op jit(solution)/shard_map/ppermute | solution.py:431
  29.8 0.7 flow.12
  30.6 0.8 flow.13
  31.4 0.7 flow.14
  32.2 2.0 %dual.4 = (f32[32,768]{1,0:T(8,128)S(1)}, f32[32,2048]{1,0:T(8,128)S(1)}, f32[2,3072]{1,0:T(2,128)S(1)}, f32[2,1]{1,0:T(2,128)S(1)}, f32[8,128]{1,0:T(8,128)S(1)...) custom-call(bf16[1,3072,256]{2,1,0:T(8,128)(2,1)S(1)} %turn.8.refs_0, ...), custom_call_target="tpu_custom_call" | custom-call | bytes 7749000 | tf_op jit(solution)/shard_map/dual/pallas_call | solution.py:34
  34.4 1.2 %pull.3 = (bf16[32,768]{1,0:T(8,128)(2,1)S(1)}, bf16[32,768]{1,0:T(8,128)(2,1)S(1)}) custom-call(s32[1]{0:T(128)} %bitcast.place_ref.refs_8_, bf16[8,256,3072]{2,1,0:T(8,128)(2,1)S(1)} %get-tuple-element.79.masked_ref.refs_9_, bf16[32,2048]{1,0:T(8,128)(2,1)S(1)} %get-tuple-element.100.half_dual, f32[8,3072]{1,0:T(8,128)S(1)} %get-tuple-element.101.term_ref), custom_call_target="tpu_custom_call" | custom-call | bytes 4428000 | tf_op jit(solution)/shard_map/pull/pallas_call | solution.py:34
  36.1 1.5 %collective-permute-start.15 = (bf16[32,896]{1,0:T(8,128)(2,1)S(1)}, bf16[32,896]{1,0:T(8,128)(2,1)S(1)}, u32[]{:S(2)}, u32[]{:S(2)}) collective-permute-start(bf16[32,896]{1,0:T(8,128)(2,1)S(1)} %add.69), channel_id=1, source_target_pairs={{0,2},{1,3},{2,0},{3,1},{4,6},{5,7},{6,4},{7,5},{8,10},{9,11},{10,... | collective-permute-start | bytes 172040 | tf_op jit(solution)/shard_map/ppermute | solution.py:431
  37.6 1.1 %collective-permute-start.11 = (bf16[32,768]{1,0:T(8,128)(2,1)S(1)}, bf16[32,768]{1,0:T(8,128)(2,1)S(1)}, u32[]{:S(2)}, u32[]{:S(2)}) collective-permute-start(bf16[32,768]{1,0:T(8,128)(2,1)S(1)} %add.66), channel_id=1, source_target_pairs={{0,8},{1,9},{2,10},{3,11},{4,12},{5,13},{6,14},{7,15},{8,0},{9,1},... | collective-permute-start | bytes 147464 | tf_op jit(solution)/shard_map/ppermute | solution.py:431
  38.7 1.6 %collective-permute-done.15 = bf16[32,896]{1,0:T(8,128)(2,1)S(1)} collective-permute-done((bf16[32,896]{1,0:T(8,128)(2,1)S(1)}, bf16[32,896]{1,0:T(8,128)(2,1)S(1)}, u32[]{:S(2)}, u32[]{:S(2)}) %collective-permute-start.15) | collective-permute-done | bytes 57376 | tf_op jit(solution)/shard_map/ppermute | solution.py:431
  40.3 1.0 %collective-permute-start.16 = (bf16[32,896]{1,0:T(8,128)(2,1)S(1)}, bf16[32,896]{1,0:T(8,128)(2,1)S(1)}, u32[]{:S(2)}, u32[]{:S(2)}) collective-permute-start(bf16[32,896]{1,0:T(8,128)(2,1)S(1)} %add.70), channel_id=1, source_target_pairs={{0,4},{1,5},{2,6},{3,7},{4,0},{5,1},{6,2},{7,3},{8,12},{9,13},{10,... | collective-permute-start | bytes 172040 | tf_op jit(solution)/shard_map/ppermute | solution.py:431
  41.3 2.0 %collective-permute-done.11 = bf16[32,768]{1,0:T(8,128)(2,1)S(1)} collective-permute-done((bf16[32,768]{1,0:T(8,128)(2,1)S(1)}, bf16[32,768]{1,0:T(8,128)(2,1)S(1)}, u32[]{:S(2)}, u32[]{:S(2)}) %collective-permute-start.11) | collective-permute-done | bytes 49184 | tf_op jit(solution)/shard_map/ppermute | solution.py:431
  43.3 1.3 %collective-permute-start.12 = (bf16[32,768]{1,0:T(8,128)(2,1)S(1)}, bf16[32,768]{1,0:T(8,128)(2,1)S(1)}, u32[]{:S(2)}, u32[]{:S(2)}) collective-permute-start(bf16[32,768]{1,0:T(8,128)(2,1)S(1)} %add.67), channel_id=1, source_target_pairs={{0,2},{1,3},{2,0},{3,1},{4,6},{5,7},{6,4},{7,5},{8,10},{9,11},{10,... | collective-permute-start | bytes 147464 | tf_op jit(solution)/shard_map/ppermute | solution.py:431
  44.6 1.9 %collective-permute-start.17 = (bf16[32,896]{1,0:T(8,128)(2,1)S(1)}, bf16[32,896]{1,0:T(8,128)(2,1)S(1)}, u32[]{:S(2)}, u32[]{:S(2)}) collective-permute-start(bf16[32,896]{1,0:T(8,128)(2,1)S(1)} %add.71), channel_id=1, source_target_pairs={{0,8},{1,9},{2,10},{3,11},{4,12},{5,13},{6,14},{7,15},{8,0},{9,1},... | collective-permute-start | bytes 172040 | tf_op jit(solution)/shard_map/ppermute | solution.py:431
  46.6 0.9 collective-permute-done.12
  47.5 1.2 %collective-permute-start.13 = (bf16[32,768]{1,0:T(8,128)(2,1)S(1)}, bf16[32,768]{1,0:T(8,128)(2,1)S(1)}, u32[]{:S(2)}, u32[]{:S(2)}) collective-permute-start(bf16[32,768]{1,0:T(8,128)(2,1)S(1)} %add.68.own_ref), channel_id=1, source_target_pairs={{0,4},{1,5},{2,6},{3,7},{4,0},{5,1},{6,2},{7,3},{8,12},{9,13},{10,... | collective-permute-start | bytes 147464 | tf_op jit(solution)/shard_map/ppermute | solution.py:431
  48.7 1.3 %collective-permute-done.17 = bf16[32,896]{1,0:T(8,128)(2,1)S(1)} collective-permute-done((bf16[32,896]{1,0:T(8,128)(2,1)S(1)}, bf16[32,896]{1,0:T(8,128)(2,1)S(1)}, u32[]{:S(2)}, u32[]{:S(2)}) %collective-permute-start.17) | collective-permute-done | bytes 57376 | tf_op jit(solution)/shard_map/ppermute | solution.py:431
  50.1 1.0 %flow.15 = (f32[32,768]{1,0:T(8,128)S(1)}, f32[32,2048]{1,0:T(8,128)S(1)}, f32[8,128]{1,0:T(8,128)S(1)}) custom-call(bf16[1,3072,256]{2,1,0:T(8,128)(2,1)S(1)} %turn.8.refs_0_, bf16[1,3072,256]{2,1,0:T(8,128)(2,1)S(1)} %turn.9.refs_1_, bf16[1,3072,256]{2,1,0:T(8,128)(2,1)S(1)} %turn.10.refs_0_.refs_2_, bf16[1,3072,256]{2,1,0:T(8,128)(2,1)S(1)} %turn.11.refs_1_.refs_3_, ...), custom_call_target="tpu_custom_call" | custom-call | bytes 2583000 | tf_op jit(solution)/shard_map/flow/pallas_call | solution.py:34
  51.1 0.6 collective-permute-done.13.received_ref
  51.7 0.7 flow.16
  52.4 0.7 flow.17
  53.1 1.9 %dual.5 = (f32[32,768]{1,0:T(8,128)S(1)}, f32[32,2048]{1,0:T(8,128)S(1)}, f32[2,3072]{1,0:T(2,128)S(1)}, f32[2,1]{1,0:T(2,128)S(1)}, f32[8,128]{1,0:T(8,128)S(1)...) custom-call(bf16[1,3072,256]{2,1,0:T(8,128)(2,1)S(1)} %turn.8.refs_0, ...), custom_call_target="tpu_custom_call" | custom-call | bytes 7749000 | tf_op jit(solution)/shard_map/dual/pallas_call | solution.py:34
  55.0 0.6 collective-permute-start.24
  55.6 1.2 %pull.4 = (bf16[32,768]{1,0:T(8,128)(2,1)S(1)}, bf16[32,768]{1,0:T(8,128)(2,1)S(1)}) custom-call(s32[1]{0:T(128)} %bitcast.place_ref.refs_8_, bf16[8,256,3072]{2,1,0:T(8,128)(2,1)S(1)} %get-tuple-element.79.masked_ref.refs_9_, bf16[32,2048]{1,0:T(8,128)(2,1)S(1)} %get-tuple-element.118.half_dual, f32[8,3072]{1,0:T(8,128)S(1)} %get-tuple-element.119.term_ref), custom_call_target="tpu_custom_call" | custom-call | bytes 4428000 | tf_op jit(solution)/shard_map/pull/pallas_call | solution.py:34
  56.9 1.8 %collective-permute-start.25 = (bf16[32,896]{1,0:T(8,128)(2,1)S(1)}, bf16[32,896]{1,0:T(8,128)(2,1)S(1)}, u32[]{:S(2)}, u32[]{:S(2)}) collective-permute-start(bf16[32,896]{1,0:T(8,128)(2,1)S(1)} %add.76), channel_id=1, source_target_pairs={{0,2},{1,3},{2,0},{3,1},{4,6},{5,7},{6,4},{7,5},{8,10},{9,11},{10,... | collective-permute-start | bytes 172040 | tf_op jit(solution)/shard_map/ppermute | solution.py:431
  58.8 1.1 %collective-permute-start.21 = (bf16[32,768]{1,0:T(8,128)(2,1)S(1)}, bf16[32,768]{1,0:T(8,128)(2,1)S(1)}, u32[]{:S(2)}, u32[]{:S(2)}) collective-permute-start(bf16[32,768]{1,0:T(8,128)(2,1)S(1)} %add.73), channel_id=1, source_target_pairs={{0,8},{1,9},{2,10},{3,11},{4,12},{5,13},{6,14},{7,15},{8,0},{9,1},... | collective-permute-start | bytes 147464 | tf_op jit(solution)/shard_map/ppermute | solution.py:431
  59.9 1.4 %collective-permute-done.25 = bf16[32,896]{1,0:T(8,128)(2,1)S(1)} collective-permute-done((bf16[32,896]{1,0:T(8,128)(2,1)S(1)}, bf16[32,896]{1,0:T(8,128)(2,1)S(1)}, u32[]{:S(2)}, u32[]{:S(2)}) %collective-permute-start.25) | collective-permute-done | bytes 57376 | tf_op jit(solution)/shard_map/ppermute | solution.py:431
  61.3 1.2 %collective-permute-start.26 = (bf16[32,896]{1,0:T(8,128)(2,1)S(1)}, bf16[32,896]{1,0:T(8,128)(2,1)S(1)}, u32[]{:S(2)}, u32[]{:S(2)}) collective-permute-start(bf16[32,896]{1,0:T(8,128)(2,1)S(1)} %add.77), channel_id=1, source_target_pairs={{0,4},{1,5},{2,6},{3,7},{4,0},{5,1},{6,2},{7,3},{8,12},{9,13},{10,... | collective-permute-start | bytes 172040 | tf_op jit(solution)/shard_map/ppermute | solution.py:431
  62.5 1.9 %collective-permute-done.21 = bf16[32,768]{1,0:T(8,128)(2,1)S(1)} collective-permute-done((bf16[32,768]{1,0:T(8,128)(2,1)S(1)}, bf16[32,768]{1,0:T(8,128)(2,1)S(1)}, u32[]{:S(2)}, u32[]{:S(2)}) %collective-permute-start.21) | collective-permute-done | bytes 49184 | tf_op jit(solution)/shard_map/ppermute | solution.py:431
  64.5 1.3 %collective-permute-start.22 = (bf16[32,768]{1,0:T(8,128)(2,1)S(1)}, bf16[32,768]{1,0:T(8,128)(2,1)S(1)}, u32[]{:S(2)}, u32[]{:S(2)}) collective-permute-start(bf16[32,768]{1,0:T(8,128)(2,1)S(1)} %add.74), channel_id=1, source_target_pairs={{0,2},{1,3},{2,0},{3,1},{4,6},{5,7},{6,4},{7,5},{8,10},{9,11},{10,... | collective-permute-start | bytes 147464 | tf_op jit(solution)/shard_map/ppermute | solution.py:431
  65.8 1.4 %collective-permute-start.27 = (bf16[32,896]{1,0:T(8,128)(2,1)S(1)}, bf16[32,896]{1,0:T(8,128)(2,1)S(1)}, u32[]{:S(2)}, u32[]{:S(2)}) collective-permute-start(bf16[32,896]{1,0:T(8,128)(2,1)S(1)} %add.78), channel_id=1, source_target_pairs={{0,8},{1,9},{2,10},{3,11},{4,12},{5,13},{6,14},{7,15},{8,0},{9,1},... | collective-permute-start | bytes 172040 | tf_op jit(solution)/shard_map/ppermute | solution.py:431
  67.2 1.5 %collective-permute-done.22 = bf16[32,768]{1,0:T(8,128)(2,1)S(1)} collective-permute-done((bf16[32,768]{1,0:T(8,128)(2,1)S(1)}, bf16[32,768]{1,0:T(8,128)(2,1)S(1)}, u32[]{:S(2)}, u32[]{:S(2)}) %collective-permute-start.22) | collective-permute-done | bytes 49184 | tf_op jit(solution)/shard_map/ppermute | solution.py:431
  68.7 0.6 collective-permute-start.23
  69.3 2.3 %collective-permute-done.27 = bf16[32,896]{1,0:T(8,128)(2,1)S(1)} collective-permute-done((bf16[32,896]{1,0:T(8,128)(2,1)S(1)}, bf16[32,896]{1,0:T(8,128)(2,1)S(1)}, u32[]{:S(2)}, u32[]{:S(2)}) %collective-permute-start.27) | collective-permute-done | bytes 57376 | tf_op jit(solution)/shard_map/ppermute | solution.py:431
  71.6 0.8 flow.18
  73.1 0.7 flow.19
  73.7 0.7 flow.20
  74.4 1.9 %dual.6 = (f32[32,768]{1,0:T(8,128)S(1)}, f32[32,2048]{1,0:T(8,128)S(1)}, f32[2,3072]{1,0:T(2,128)S(1)}, f32[2,1]{1,0:T(2,128)S(1)}, f32[8,128]{1,0:T(8,128)S(1)...) custom-call(bf16[1,3072,256]{2,1,0:T(8,128)(2,1)S(1)} %turn.8.refs_0, ...), custom_call_target="tpu_custom_call" | custom-call | bytes 7749000 | tf_op jit(solution)/shard_map/dual/pallas_call | solution.py:34
  76.8 1.2 %pull.5 = (bf16[32,768]{1,0:T(8,128)(2,1)S(1)}, bf16[32,768]{1,0:T(8,128)(2,1)S(1)}) custom-call(s32[1]{0:T(128)} %bitcast.place_ref.refs_8_, bf16[8,256,3072]{2,1,0:T(8,128)(2,1)S(1)} %get-tuple-element.79.masked_ref.refs_9_, bf16[32,2048]{1,0:T(8,128)(2,1)S(1)} %get-tuple-element.136.half_dual, f32[8,3072]{1,0:T(8,128)S(1)} %get-tuple-element.137.term_ref), custom_call_target="tpu_custom_call" | custom-call | bytes 4428000 | tf_op jit(solution)/shard_map/pull/pallas_call | solution.py:34
  78.3 1.5 %collective-permute-start.35 = (bf16[32,896]{1,0:T(8,128)(2,1)S(1)}, bf16[32,896]{1,0:T(8,128)(2,1)S(1)}, u32[]{:S(2)}, u32[]{:S(2)}) collective-permute-start(bf16[32,896]{1,0:T(8,128)(2,1)S(1)} %add.83), channel_id=1, source_target_pairs={{0,2},{1,3},{2,0},{3,1},{4,6},{5,7},{6,4},{7,5},{8,10},{9,11},{10,... | collective-permute-start | bytes 172040 | tf_op jit(solution)/shard_map/ppermute | solution.py:431
  79.8 0.6 collective-permute-start.31
  80.3 2.2 %collective-permute-done.35 = bf16[32,896]{1,0:T(8,128)(2,1)S(1)} collective-permute-done((bf16[32,896]{1,0:T(8,128)(2,1)S(1)}, bf16[32,896]{1,0:T(8,128)(2,1)S(1)}, u32[]{:S(2)}, u32[]{:S(2)}) %collective-permute-start.35) | collective-permute-done | bytes 57376 | tf_op jit(solution)/shard_map/ppermute | solution.py:431
  82.5 0.6 collective-permute-start.36
  83.1 2.3 %collective-permute-done.31 = bf16[32,768]{1,0:T(8,128)(2,1)S(1)} collective-permute-done((bf16[32,768]{1,0:T(8,128)(2,1)S(1)}, bf16[32,768]{1,0:T(8,128)(2,1)S(1)}, u32[]{:S(2)}, u32[]{:S(2)}) %collective-permute-start.31) | collective-permute-done | bytes 49184 | tf_op jit(solution)/shard_map/ppermute | solution.py:431
  85.4 1.1 %collective-permute-start.32 = (bf16[32,768]{1,0:T(8,128)(2,1)S(1)}, bf16[32,768]{1,0:T(8,128)(2,1)S(1)}, u32[]{:S(2)}, u32[]{:S(2)}) collective-permute-start(bf16[32,768]{1,0:T(8,128)(2,1)S(1)} %add.81), channel_id=1, source_target_pairs={{0,2},{1,3},{2,0},{3,1},{4,6},{5,7},{6,4},{7,5},{8,10},{9,11},{10,... | collective-permute-start | bytes 147464 | tf_op jit(solution)/shard_map/ppermute | solution.py:431
  86.8 1.0 %collective-permute-start.37 = (bf16[32,896]{1,0:T(8,128)(2,1)S(1)}, bf16[32,896]{1,0:T(8,128)(2,1)S(1)}, u32[]{:S(2)}, u32[]{:S(2)}) collective-permute-start(bf16[32,896]{1,0:T(8,128)(2,1)S(1)} %add.85), channel_id=1, source_target_pairs={{0,8},{1,9},{2,10},{3,11},{4,12},{5,13},{6,14},{7,15},{8,0},{9,1},... | collective-permute-start | bytes 172040 | tf_op jit(solution)/shard_map/ppermute | solution.py:431
  87.8 1.7 %collective-permute-done.32 = bf16[32,768]{1,0:T(8,128)(2,1)S(1)} collective-permute-done((bf16[32,768]{1,0:T(8,128)(2,1)S(1)}, bf16[32,768]{1,0:T(8,128)(2,1)S(1)}, u32[]{:S(2)}, u32[]{:S(2)}) %collective-permute-start.32) | collective-permute-done | bytes 49184 | tf_op jit(solution)/shard_map/ppermute | solution.py:431
  89.9 2.6 %collective-permute-done.37 = bf16[32,896]{1,0:T(8,128)(2,1)S(1)} collective-permute-done((bf16[32,896]{1,0:T(8,128)(2,1)S(1)}, bf16[32,896]{1,0:T(8,128)(2,1)S(1)}, u32[]{:S(2)}, u32[]{:S(2)}) %collective-permute-start.37) | collective-permute-done | bytes 57376 | tf_op jit(solution)/shard_map/ppermute | solution.py:431
  92.6 0.8 flow.21
  94.0 0.7 flow.22
  94.7 0.7 flow.23
  95.4 1.5 %dual.7 = (f32[2,3072]{1,0:T(2,128)}, f32[32,8,256]{2,1,0:T(8,128)}, f32[2,3072]{1,0:T(2,128)}, f32[2]{0:T(128)}) custom-call(bf16[1,3072,256]{2,1,0:T(8,128)(2,1)S(1)} %turn.8.refs_0_, bf16[1,3072,256]{2,1,0:T(8,128)(2,1)S(1)} %turn.9.refs_1_, bf16[1,3072,256]{2,1,0:T(8,128)(2,1)S(1)} %turn.10.refs_0_.refs_2_, ...), custom_call_target="tpu_custom_call" | custom-call | bytes 4428000 | tf_op jit(solution)/shard_map/dual/pallas_call | solution.py:34
  (78 shorter events, 8.0 us)
Async XLA Ops:
  7.2 1.4 %collective-permute-start = (bf16[36,896]{1,0:T(8,128)(2,1)S(1)}, bf16[36,896]{1,0:T(8,128)(2,1)S(1)}, u32[]{:S(2)}, u32[]{:S(2)}) collective-permute-start(bf16[36,896]{1,0:T(8,128)(2,1)S(1)} %get-tuple-element.81), channel_id=1, source_target_pairs={{0,1},{1,0},{2,3},{3,2},{4,5},{5,4},{6,7},{7,6},{8,9},{9,8},{10,11... | collective-permute-start | bytes 193544 | tf_op jit(solution)/shard_map/ppermute | solution.py:431
  8.6 7.8 %collective-permute-start.1 = (bf16[40,896]{1,0:T(8,128)(2,1)S(1)}, bf16[40,896]{1,0:T(8,128)(2,1)S(1)}, u32[]{:S(2)}, u32[]{:S(2)}) collective-permute-start(bf16[40,896]{1,0:T(8,128)(2,1)S(1)} %join.8.before_ref.own_ref), channel_id=1, source_target_pairs={{0,2},{1,3},{2,0},{3,1},{4,6},{5,7},{6,4},{7,5},{8,10},{9,11},{10,... | collective-permute-start | bytes 215048 | tf_op jit(solution)/shard_map/ppermute | solution.py:431
  11.5 1.2 %collective-permute-start.3 = (bf16[36,768]{1,0:T(8,128)(2,1)S(1)}, bf16[36,768]{1,0:T(8,128)(2,1)S(1)}, u32[]{:S(2)}, u32[]{:S(2)}) collective-permute-start(bf16[36,768]{1,0:T(8,128)(2,1)S(1)} %get-tuple-element.83), channel_id=1, source_target_pairs={{0,1},{1,0},{2,3},{3,2},{4,5},{5,4},{6,7},{7,6},{8,9},{9,8},{10,11... | collective-permute-start | bytes 165896 | tf_op jit(solution)/shard_map/ppermute | solution.py:431
  12.8 6.4 %collective-permute-start.4 = (bf16[40,768]{1,0:T(8,128)(2,1)S(1)}, bf16[40,768]{1,0:T(8,128)(2,1)S(1)}, u32[]{:S(2)}, u32[]{:S(2)}) collective-permute-start(bf16[40,768]{1,0:T(8,128)(2,1)S(1)} %join.11.own_ref), channel_id=1, source_target_pairs={{0,8},{1,9},{2,10},{3,11},{4,12},{5,13},{6,14},{7,15},{8,0},{9,1},... | collective-permute-start | bytes 184328 | tf_op jit(solution)/shard_map/ppermute | solution.py:431
  16.4 4.8 %collective-permute-start.2 = (bf16[48,896]{1,0:T(8,128)(2,1)S(1)}, bf16[48,896]{1,0:T(8,128)(2,1)S(1)}, u32[]{:S(2)}, u32[]{:S(2)}) collective-permute-start(bf16[48,896]{1,0:T(8,128)(2,1)S(1)} %join.9.before_ref.own_ref), channel_id=1, source_target_pairs={{0,4},{1,5},{2,6},{3,7},{4,0},{5,1},{6,2},{7,3},{8,12},{9,13},{10,... | collective-permute-start | bytes 258056 | tf_op jit(solution)/shard_map/ppermute | solution.py:431
  19.3 4.4 %collective-permute-start.5 = (bf16[48,768]{1,0:T(8,128)(2,1)S(1)}, bf16[48,768]{1,0:T(8,128)(2,1)S(1)}, u32[]{:S(2)}, u32[]{:S(2)}) collective-permute-start(bf16[48,768]{1,0:T(8,128)(2,1)S(1)} %join.12.own_ref), channel_id=1, source_target_pairs={{0,2},{1,3},{2,0},{3,1},{4,6},{5,7},{6,4},{7,5},{8,10},{9,11},{10,... | collective-permute-start | bytes 221192 | tf_op jit(solution)/shard_map/ppermute | solution.py:431
  21.2 7.9 %collective-permute-start.8 = (bf16[64,896]{1,0:T(8,128)(2,1)S(1)}, bf16[64,896]{1,0:T(8,128)(2,1)S(1)}, u32[]{:S(2)}, u32[]{:S(2)}) collective-permute-start(bf16[64,896]{1,0:T(8,128)(2,1)S(1)} %join.10.before_ref.own_ref), channel_id=1, source_target_pairs={{0,8},{1,9},{2,10},{3,11},{4,12},{5,13},{6,14},{7,15},{8,0},{9,1},... | collective-permute-start | bytes 344072 | tf_op jit(solution)/shard_map/ppermute | solution.py:431
  23.7 5.7 %collective-permute-start.6 = (bf16[64,768]{1,0:T(8,128)(2,1)S(1)}, bf16[64,768]{1,0:T(8,128)(2,1)S(1)}, u32[]{:S(2)}, u32[]{:S(2)}) collective-permute-start(bf16[64,768]{1,0:T(8,128)(2,1)S(1)} %join.13.own_ref), channel_id=1, source_target_pairs={{0,4},{1,5},{2,6},{3,7},{4,0},{5,1},{6,2},{7,3},{8,12},{9,13},{10,... | collective-permute-start | bytes 294920 | tf_op jit(solution)/shard_map/ppermute | solution.py:431
  29.1 1.5 %collective-permute-start.9 = (bf16[96,896]{1,0:T(8,128)(2,1)S(1)}, bf16[96,896]{1,0:T(8,128)(2,1)S(1)}, u32[]{:S(2)}, u32[]{:S(2)}) collective-permute-start(bf16[96,896]{1,0:T(8,128)(2,1)S(1)} %join.15.refs_9_), channel_id=1, source_target_pairs={{0,1},{1,0},{2,3},{3,2},{4,5},{5,4},{6,7},{7,6},{8,9},{9,8},{10,11... | collective-permute-start | bytes 516104 | tf_op jit(solution)/shard_map/ppermute | solution.py:431
  29.4 2.8 %collective-permute-start.7 = (bf16[96,768]{1,0:T(8,128)(2,1)S(1)}, bf16[96,768]{1,0:T(8,128)(2,1)S(1)}, u32[]{:S(2)}, u32[]{:S(2)}) collective-permute-start(bf16[96,768]{1,0:T(8,128)(2,1)S(1)} %join.14.refs_9_), channel_id=1, source_target_pairs={{0,1},{1,0},{2,3},{3,2},{4,5},{5,4},{6,7},{7,6},{8,9},{9,8},{10,11... | collective-permute-start | bytes 442376 | tf_op jit(solution)/shard_map/ppermute | solution.py:431
  31.4 0.8 copy-start
  34.2 1.9 %collective-permute-start.14 = (bf16[32,896]{1,0:T(8,128)(2,1)S(1)}, bf16[32,896]{1,0:T(8,128)(2,1)S(1)}, u32[]{:S(2)}, u32[]{:S(2)}) collective-permute-start(bf16[32,896]{1,0:T(8,128)(2,1)S(1)} %get-tuple-element.105), channel_id=1, source_target_pairs={{0,1},{1,0},{2,3},{3,2},{4,5},{5,4},{6,7},{7,6},{8,9},{9,8},{10,11... | collective-permute-start | bytes 172040 | tf_op jit(solution)/shard_map/ppermute | solution.py:431
  35.6 2.0 %collective-permute-start.10 = (bf16[32,768]{1,0:T(8,128)(2,1)S(1)}, bf16[32,768]{1,0:T(8,128)(2,1)S(1)}, u32[]{:S(2)}, u32[]{:S(2)}) collective-permute-start(bf16[32,768]{1,0:T(8,128)(2,1)S(1)} %get-tuple-element.103), channel_id=1, source_target_pairs={{0,1},{1,0},{2,3},{3,2},{4,5},{5,4},{6,7},{7,6},{8,9},{9,8},{10,11... | collective-permute-start | bytes 147464 | tf_op jit(solution)/shard_map/ppermute | solution.py:431
  36.1 4.2 %collective-permute-start.15 = (bf16[32,896]{1,0:T(8,128)(2,1)S(1)}, bf16[32,896]{1,0:T(8,128)(2,1)S(1)}, u32[]{:S(2)}, u32[]{:S(2)}) collective-permute-start(bf16[32,896]{1,0:T(8,128)(2,1)S(1)} %add.69), channel_id=1, source_target_pairs={{0,2},{1,3},{2,0},{3,1},{4,6},{5,7},{6,4},{7,5},{8,10},{9,11},{10,... | collective-permute-start | bytes 172040 | tf_op jit(solution)/shard_map/ppermute | solution.py:431
  37.6 5.7 %collective-permute-start.11 = (bf16[32,768]{1,0:T(8,128)(2,1)S(1)}, bf16[32,768]{1,0:T(8,128)(2,1)S(1)}, u32[]{:S(2)}, u32[]{:S(2)}) collective-permute-start(bf16[32,768]{1,0:T(8,128)(2,1)S(1)} %add.66), channel_id=1, source_target_pairs={{0,8},{1,9},{2,10},{3,11},{4,12},{5,13},{6,14},{7,15},{8,0},{9,1},... | collective-permute-start | bytes 147464 | tf_op jit(solution)/shard_map/ppermute | solution.py:431
  40.3 4.3 %collective-permute-start.16 = (bf16[32,896]{1,0:T(8,128)(2,1)S(1)}, bf16[32,896]{1,0:T(8,128)(2,1)S(1)}, u32[]{:S(2)}, u32[]{:S(2)}) collective-permute-start(bf16[32,896]{1,0:T(8,128)(2,1)S(1)} %add.70), channel_id=1, source_target_pairs={{0,4},{1,5},{2,6},{3,7},{4,0},{5,1},{6,2},{7,3},{8,12},{9,13},{10,... | collective-permute-start | bytes 172040 | tf_op jit(solution)/shard_map/ppermute | solution.py:431
  43.3 4.2 %collective-permute-start.12 = (bf16[32,768]{1,0:T(8,128)(2,1)S(1)}, bf16[32,768]{1,0:T(8,128)(2,1)S(1)}, u32[]{:S(2)}, u32[]{:S(2)}) collective-permute-start(bf16[32,768]{1,0:T(8,128)(2,1)S(1)} %add.67), channel_id=1, source_target_pairs={{0,2},{1,3},{2,0},{3,1},{4,6},{5,7},{6,4},{7,5},{8,10},{9,11},{10,... | collective-permute-start | bytes 147464 | tf_op jit(solution)/shard_map/ppermute | solution.py:431
  44.6 5.4 %collective-permute-start.17 = (bf16[32,896]{1,0:T(8,128)(2,1)S(1)}, bf16[32,896]{1,0:T(8,128)(2,1)S(1)}, u32[]{:S(2)}, u32[]{:S(2)}) collective-permute-start(bf16[32,896]{1,0:T(8,128)(2,1)S(1)} %add.71), channel_id=1, source_target_pairs={{0,8},{1,9},{2,10},{3,11},{4,12},{5,13},{6,14},{7,15},{8,0},{9,1},... | collective-permute-start | bytes 172040 | tf_op jit(solution)/shard_map/ppermute | solution.py:431
  47.5 4.2 %collective-permute-start.13 = (bf16[32,768]{1,0:T(8,128)(2,1)S(1)}, bf16[32,768]{1,0:T(8,128)(2,1)S(1)}, u32[]{:S(2)}, u32[]{:S(2)}) collective-permute-start(bf16[32,768]{1,0:T(8,128)(2,1)S(1)} %add.68.own_ref), channel_id=1, source_target_pairs={{0,4},{1,5},{2,6},{3,7},{4,0},{5,1},{6,2},{7,3},{8,12},{9,13},{10,... | collective-permute-start | bytes 147464 | tf_op jit(solution)/shard_map/ppermute | solution.py:431
  50.0 1.7 %collective-permute-start.19 = (bf16[32,896]{1,0:T(8,128)(2,1)S(1)}, bf16[32,896]{1,0:T(8,128)(2,1)S(1)}, u32[]{:S(2)}, u32[]{:S(2)}) collective-permute-start(bf16[32,896]{1,0:T(8,128)(2,1)S(1)} %add.72.refs_9_), channel_id=1, source_target_pairs={{0,1},{1,0},{2,3},{3,2},{4,5},{5,4},{6,7},{7,6},{8,9},{9,8},{10,11... | collective-permute-start | bytes 172040 | tf_op jit(solution)/shard_map/ppermute | solution.py:431
  51.7 1.5 %collective-permute-start.18 = (bf16[32,768]{1,0:T(8,128)(2,1)S(1)}, bf16[32,768]{1,0:T(8,128)(2,1)S(1)}, u32[]{:S(2)}, u32[]{:S(2)}) collective-permute-start(bf16[32,768]{1,0:T(8,128)(2,1)S(1)} %add.87.refs_9_), channel_id=1, source_target_pairs={{0,1},{1,0},{2,3},{3,2},{4,5},{5,4},{6,7},{7,6},{8,9},{9,8},{10,11... | collective-permute-start | bytes 147464 | tf_op jit(solution)/shard_map/ppermute | solution.py:431
  55.0 1.9 %collective-permute-start.24 = (bf16[32,896]{1,0:T(8,128)(2,1)S(1)}, bf16[32,896]{1,0:T(8,128)(2,1)S(1)}, u32[]{:S(2)}, u32[]{:S(2)}) collective-permute-start(bf16[32,896]{1,0:T(8,128)(2,1)S(1)} %get-tuple-element.123), channel_id=1, source_target_pairs={{0,1},{1,0},{2,3},{3,2},{4,5},{5,4},{6,7},{7,6},{8,9},{9,8},{10,11... | collective-permute-start | bytes 172040 | tf_op jit(solution)/shard_map/ppermute | solution.py:431
  56.8 1.9 %collective-permute-start.20 = (bf16[32,768]{1,0:T(8,128)(2,1)S(1)}, bf16[32,768]{1,0:T(8,128)(2,1)S(1)}, u32[]{:S(2)}, u32[]{:S(2)}) collective-permute-start(bf16[32,768]{1,0:T(8,128)(2,1)S(1)} %get-tuple-element.121), channel_id=1, source_target_pairs={{0,1},{1,0},{2,3},{3,2},{4,5},{5,4},{6,7},{7,6},{8,9},{9,8},{10,11... | collective-permute-start | bytes 147464 | tf_op jit(solution)/shard_map/ppermute | solution.py:431
  56.9 4.4 %collective-permute-start.25 = (bf16[32,896]{1,0:T(8,128)(2,1)S(1)}, bf16[32,896]{1,0:T(8,128)(2,1)S(1)}, u32[]{:S(2)}, u32[]{:S(2)}) collective-permute-start(bf16[32,896]{1,0:T(8,128)(2,1)S(1)} %add.76), channel_id=1, source_target_pairs={{0,2},{1,3},{2,0},{3,1},{4,6},{5,7},{6,4},{7,5},{8,10},{9,11},{10,... | collective-permute-start | bytes 172040 | tf_op jit(solution)/shard_map/ppermute | solution.py:431
  58.8 5.7 %collective-permute-start.21 = (bf16[32,768]{1,0:T(8,128)(2,1)S(1)}, bf16[32,768]{1,0:T(8,128)(2,1)S(1)}, u32[]{:S(2)}, u32[]{:S(2)}) collective-permute-start(bf16[32,768]{1,0:T(8,128)(2,1)S(1)} %add.73), channel_id=1, source_target_pairs={{0,8},{1,9},{2,10},{3,11},{4,12},{5,13},{6,14},{7,15},{8,0},{9,1},... | collective-permute-start | bytes 147464 | tf_op jit(solution)/shard_map/ppermute | solution.py:431
  61.3 4.4 %collective-permute-start.26 = (bf16[32,896]{1,0:T(8,128)(2,1)S(1)}, bf16[32,896]{1,0:T(8,128)(2,1)S(1)}, u32[]{:S(2)}, u32[]{:S(2)}) collective-permute-start(bf16[32,896]{1,0:T(8,128)(2,1)S(1)} %add.77), channel_id=1, source_target_pairs={{0,4},{1,5},{2,6},{3,7},{4,0},{5,1},{6,2},{7,3},{8,12},{9,13},{10,... | collective-permute-start | bytes 172040 | tf_op jit(solution)/shard_map/ppermute | solution.py:431
  64.5 4.2 %collective-permute-start.22 = (bf16[32,768]{1,0:T(8,128)(2,1)S(1)}, bf16[32,768]{1,0:T(8,128)(2,1)S(1)}, u32[]{:S(2)}, u32[]{:S(2)}) collective-permute-start(bf16[32,768]{1,0:T(8,128)(2,1)S(1)} %add.74), channel_id=1, source_target_pairs={{0,2},{1,3},{2,0},{3,1},{4,6},{5,7},{6,4},{7,5},{8,10},{9,11},{10,... | collective-permute-start | bytes 147464 | tf_op jit(solution)/shard_map/ppermute | solution.py:431
  65.8 5.8 %collective-permute-start.27 = (bf16[32,896]{1,0:T(8,128)(2,1)S(1)}, bf16[32,896]{1,0:T(8,128)(2,1)S(1)}, u32[]{:S(2)}, u32[]{:S(2)}) collective-permute-start(bf16[32,896]{1,0:T(8,128)(2,1)S(1)} %add.78), channel_id=1, source_target_pairs={{0,8},{1,9},{2,10},{3,11},{4,12},{5,13},{6,14},{7,15},{8,0},{9,1},... | collective-permute-start | bytes 172040 | tf_op jit(solution)/shard_map/ppermute | solution.py:431
  68.7 4.2 %collective-permute-start.23 = (bf16[32,768]{1,0:T(8,128)(2,1)S(1)}, bf16[32,768]{1,0:T(8,128)(2,1)S(1)}, u32[]{:S(2)}, u32[]{:S(2)}) collective-permute-start(bf16[32,768]{1,0:T(8,128)(2,1)S(1)} %add.75.own_ref), channel_id=1, source_target_pairs={{0,4},{1,5},{2,6},{3,7},{4,0},{5,1},{6,2},{7,3},{8,12},{9,13},{10,... | collective-permute-start | bytes 147464 | tf_op jit(solution)/shard_map/ppermute | solution.py:431
  71.6 1.5 %collective-permute-start.29 = (bf16[32,896]{1,0:T(8,128)(2,1)S(1)}, bf16[32,896]{1,0:T(8,128)(2,1)S(1)}, u32[]{:S(2)}, u32[]{:S(2)}) collective-permute-start(bf16[32,896]{1,0:T(8,128)(2,1)S(1)} %add.79.refs_9_), channel_id=1, source_target_pairs={{0,1},{1,0},{2,3},{3,2},{4,5},{5,4},{6,7},{7,6},{8,9},{9,8},{10,11... | collective-permute-start | bytes 172040 | tf_op jit(solution)/shard_map/ppermute | solution.py:431
  72.8 1.6 %collective-permute-start.28 = (bf16[32,768]{1,0:T(8,128)(2,1)S(1)}, bf16[32,768]{1,0:T(8,128)(2,1)S(1)}, u32[]{:S(2)}, u32[]{:S(2)}) collective-permute-start(bf16[32,768]{1,0:T(8,128)(2,1)S(1)} %add.88.refs_9_), channel_id=1, source_target_pairs={{0,1},{1,0},{2,3},{3,2},{4,5},{5,4},{6,7},{7,6},{8,9},{9,8},{10,11... | collective-permute-start | bytes 147464 | tf_op jit(solution)/shard_map/ppermute | solution.py:431
  76.4 1.9 %collective-permute-start.34 = (bf16[32,896]{1,0:T(8,128)(2,1)S(1)}, bf16[32,896]{1,0:T(8,128)(2,1)S(1)}, u32[]{:S(2)}, u32[]{:S(2)}) collective-permute-start(bf16[32,896]{1,0:T(8,128)(2,1)S(1)} %get-tuple-element.141), channel_id=1, source_target_pairs={{0,1},{1,0},{2,3},{3,2},{4,5},{5,4},{6,7},{7,6},{8,9},{9,8},{10,11... | collective-permute-start | bytes 172040 | tf_op jit(solution)/shard_map/ppermute | solution.py:431
  78.0 1.7 %collective-permute-start.30 = (bf16[32,768]{1,0:T(8,128)(2,1)S(1)}, bf16[32,768]{1,0:T(8,128)(2,1)S(1)}, u32[]{:S(2)}, u32[]{:S(2)}) collective-permute-start(bf16[32,768]{1,0:T(8,128)(2,1)S(1)} %get-tuple-element.139), channel_id=1, source_target_pairs={{0,1},{1,0},{2,3},{3,2},{4,5},{5,4},{6,7},{7,6},{8,9},{9,8},{10,11... | collective-permute-start | bytes 147464 | tf_op jit(solution)/shard_map/ppermute | solution.py:431
  78.3 4.2 %collective-permute-start.35 = (bf16[32,896]{1,0:T(8,128)(2,1)S(1)}, bf16[32,896]{1,0:T(8,128)(2,1)S(1)}, u32[]{:S(2)}, u32[]{:S(2)}) collective-permute-start(bf16[32,896]{1,0:T(8,128)(2,1)S(1)} %add.83), channel_id=1, source_target_pairs={{0,2},{1,3},{2,0},{3,1},{4,6},{5,7},{6,4},{7,5},{8,10},{9,11},{10,... | collective-permute-start | bytes 172040 | tf_op jit(solution)/shard_map/ppermute | solution.py:431
  79.8 5.6 %collective-permute-start.31 = (bf16[32,768]{1,0:T(8,128)(2,1)S(1)}, bf16[32,768]{1,0:T(8,128)(2,1)S(1)}, u32[]{:S(2)}, u32[]{:S(2)}) collective-permute-start(bf16[32,768]{1,0:T(8,128)(2,1)S(1)} %add.80), channel_id=1, source_target_pairs={{0,8},{1,9},{2,10},{3,11},{4,12},{5,13},{6,14},{7,15},{8,0},{9,1},... | collective-permute-start | bytes 147464 | tf_op jit(solution)/shard_map/ppermute | solution.py:431
  82.5 4.2 %collective-permute-start.36 = (bf16[32,896]{1,0:T(8,128)(2,1)S(1)}, bf16[32,896]{1,0:T(8,128)(2,1)S(1)}, u32[]{:S(2)}, u32[]{:S(2)}) collective-permute-start(bf16[32,896]{1,0:T(8,128)(2,1)S(1)} %add.84), channel_id=1, source_target_pairs={{0,4},{1,5},{2,6},{3,7},{4,0},{5,1},{6,2},{7,3},{8,12},{9,13},{10,... | collective-permute-start | bytes 172040 | tf_op jit(solution)/shard_map/ppermute | solution.py:431
  85.4 4.2 %collective-permute-start.32 = (bf16[32,768]{1,0:T(8,128)(2,1)S(1)}, bf16[32,768]{1,0:T(8,128)(2,1)S(1)}, u32[]{:S(2)}, u32[]{:S(2)}) collective-permute-start(bf16[32,768]{1,0:T(8,128)(2,1)S(1)} %add.81), channel_id=1, source_target_pairs={{0,2},{1,3},{2,0},{3,1},{4,6},{5,7},{6,4},{7,5},{8,10},{9,11},{10,... | collective-permute-start | bytes 147464 | tf_op jit(solution)/shard_map/ppermute | solution.py:431
  86.8 5.7 %collective-permute-start.37 = (bf16[32,896]{1,0:T(8,128)(2,1)S(1)}, bf16[32,896]{1,0:T(8,128)(2,1)S(1)}, u32[]{:S(2)}, u32[]{:S(2)}) collective-permute-start(bf16[32,896]{1,0:T(8,128)(2,1)S(1)} %add.85), channel_id=1, source_target_pairs={{0,8},{1,9},{2,10},{3,11},{4,12},{5,13},{6,14},{7,15},{8,0},{9,1},... | collective-permute-start | bytes 172040 | tf_op jit(solution)/shard_map/ppermute | solution.py:431
  89.6 4.2 %collective-permute-start.33 = (bf16[32,768]{1,0:T(8,128)(2,1)S(1)}, bf16[32,768]{1,0:T(8,128)(2,1)S(1)}, u32[]{:S(2)}, u32[]{:S(2)}) collective-permute-start(bf16[32,768]{1,0:T(8,128)(2,1)S(1)} %add.82.own_ref), channel_id=1, source_target_pairs={{0,4},{1,5},{2,6},{3,7},{4,0},{5,1},{6,2},{7,3},{8,12},{9,13},{10,... | collective-permute-start | bytes 147464 | tf_op jit(solution)/shard_map/ppermute | solution.py:431
  92.5 1.5 %collective-permute-start.39 = (bf16[32,896]{1,0:T(8,128)(2,1)S(1)}, bf16[32,896]{1,0:T(8,128)(2,1)S(1)}, u32[]{:S(2)}, u32[]{:S(2)}) collective-permute-start(bf16[32,896]{1,0:T(8,128)(2,1)S(1)} %add.86.refs_9_), channel_id=1, source_target_pairs={{0,1},{1,0},{2,3},{3,2},{4,5},{5,4},{6,7},{7,6},{8,9},{9,8},{10,11... | collective-permute-start | bytes 172040 | tf_op jit(solution)/shard_map/ppermute | solution.py:431
  93.7 1.6 %collective-permute-start.38 = (bf16[32,768]{1,0:T(8,128)(2,1)S(1)}, bf16[32,768]{1,0:T(8,128)(2,1)S(1)}, u32[]{:S(2)}, u32[]{:S(2)}) collective-permute-start(bf16[32,768]{1,0:T(8,128)(2,1)S(1)} %add.89.refs_9_), channel_id=1, source_target_pairs={{0,1},{1,0},{2,3},{3,2},{4,5},{5,4},{6,7},{7,6},{8,9},{9,8},{10,11... | collective-permute-start | bytes 147464 | tf_op jit(solution)/shard_map/ppermute | solution.py:431

commit v3 on v2

--- a/solution.py
+++ b/solution.py
@@ -16,6 +16,8 @@
 FULL = jnp.float32
 
 PIECES = 4
+TURNS = (2, 3, 3)
+ORDERS = ((0, 0), (2, 0), (0, 0), (2, 0))
 
 VMEM = pl.BlockSpec(memory_space=pltpu.VMEM)
 SMEM = pl.BlockSpec(memory_space=pltpu.SMEM)
@@ -51,9 +53,16 @@
     return (piece % 2) * (units // 2) + (piece // 2) * (units // 4)
 
 
+def parity(index):
+    odd = index % 2
+    for bit in range(1, LANES.bit_length() - 1):
+        odd = odd ^ ((index // 2**bit) % 2)
+    return odd
+
+
 def own_first(place, s, width):
-    core = place % 2
-    return pl.multiple_of((core if s == 0 else 1 - core) * width, LANES)
+    side = parity(place)
+    return pl.multiple_of((side if s == 0 else 1 - side) * width, LANES)
 
 
 def add_rows(values, first, rows):
@@ -94,27 +103,13 @@
     gate_hbm,
     tiles_ref,
     dual_ref,
-    base_ref,
-    monitored_ref,
-    ratings_ref,
-    floor_ref,
-    span_ref,
-    limit_ref,
     on_ref,
     cost_ref,
     ramp_ref,
     level_ref,
     masked_ref,
-    send_a,
-    keep_a,
-    send_b,
-    keep_b,
-    dual_out,
-    base_out,
-    rating_out,
-    unit_out,
-    cost_out,
-    ramp_out,
+    send_ref,
+    keep_ref,
     gate_ref,
     acc_ref,
     sems,
@@ -139,6 +134,69 @@
         for s in range(2):
             copy(k, s).start()
 
+    gates.wait()
+    for k in range(ctgs):
+        lhs = dual_ref[:, k, :].astype(HALF)
+        for s in range(2):
+            copy(k, s).wait()
+            gate_at = own_first(place, s, width) // LANES
+            for j in range(0, half_tiles, 2):
+                at = s * width + j * LANES
+                block = []
+                for m in range(lines // LANES):
+                    line = []
+                    for i in range(2):
+                        gate = gate_ref[k, m, gate_at + j + i]
+                        part = masked_ref[k, pl.ds(m * LANES, LANES), pl.ds(at + i * LANES, LANES)]
+                        line.append(jnp.where(gate > 0, part, jnp.zeros((), HALF)))
+                    block.append(jnp.concatenate(line, axis=1))
+                block = jnp.concatenate(block, axis=0)
+                cols = pl.ds(at, WIDE)
+                masked_ref[k, :, cols] = block
+                part = jnp.dot(lhs, block, preferred_element_type=FULL)
+                acc_ref[:, cols] = part if k == 0 else acc_ref[:, cols] + part
+
+    for s, out_ref in enumerate((keep_ref, send_ref)):
+        message = []
+        for piece in (s, 2 + s):
+            cols = pl.ds(piece_at(piece, units), quarter)
+            own = pl.ds(pl.multiple_of(own_first(place, s, width) + (piece // 2) * quarter, LANES), quarter)
+            rows = hour_terms(
+                [cost_ref[j : j + 1, own] for j in range(hours)],
+                [ramp_ref[j : j + 1, own] for j in range(hours)],
+                on_ref[:, own].astype(FULL),
+                None,
+            )
+            values = add_rows(acc_ref[:, cols], place * hours, rows)
+            level = level_ref[:, own]
+            high = level.astype(HALF).astype(FULL)
+            message.append(jnp.concatenate([values, high, level - high], axis=0))
+        out_ref[...] = jnp.concatenate(message, axis=1).astype(HALF)
+
+
+def prepare_kernel(
+    place_ref,
+    before_ref,
+    dual_ref,
+    base_ref,
+    monitored_ref,
+    ratings_ref,
+    floor_ref,
+    span_ref,
+    limit_ref,
+    on_ref,
+    cost_ref,
+    ramp_ref,
+    dual_out,
+    base_out,
+    rating_out,
+    unit_out,
+    cost_out,
+    ramp_out,
+):
+    ctgs, lines = monitored_ref.shape
+    width = floor_ref.shape[1] // 2
+    place = place_ref[0]
     table = ratings_ref[...].T
     hi = table.astype(HALF)
     left = table - hi.astype(FULL)
@@ -169,46 +227,6 @@
         cost_out[:, cols] = cost_ref[:, own]
         ramp_out[:, cols] = ramp_ref[:, own]
 
-    gates.wait()
-    for k in range(ctgs):
-        lhs = dual_out[:, pl.ds(k * lines, lines)].astype(HALF)
-        for s in range(2):
-            copy(k, s).wait()
-            gate_at = (place % 2 if s == 0 else 1 - place % 2) * half_tiles
-            for j in range(0, half_tiles, 2):
-                at = s * width + j * LANES
-                block = []
-                for m in range(lines // LANES):
-                    line = []
-                    for i in range(2):
-                        gate = gate_ref[k, m, gate_at + j + i]
-                        part = masked_ref[k, pl.ds(m * LANES, LANES), pl.ds(at + i * LANES, LANES)]
-                        line.append(jnp.where(gate > 0, part, jnp.zeros((), HALF)))
-                    block.append(jnp.concatenate(line, axis=1))
-                block = jnp.concatenate(block, axis=0)
-                cols = pl.ds(at, WIDE)
-                masked_ref[k, :, cols] = block
-                part = jnp.dot(lhs, block, preferred_element_type=FULL)
-                acc_ref[:, cols] = part if k == 0 else acc_ref[:, cols] + part
-
-    for piece, out_ref in enumerate((keep_a, send_a, keep_b, send_b)):
-        cols = pl.ds(piece_at(piece, units), quarter)
-        rows = hour_terms(
-            [cost_out[j : j + 1, cols] for j in range(hours)],
-            [ramp_out[j : j + 1, cols] for j in range(hours)],
-            unit_out[3:4, cols],
-            None,
-        )
-        values = add_rows(acc_ref[:, cols], place * hours, rows)
-        own = pl.multiple_of(own_first(place, piece % 2, width) + (piece // 2) * quarter, LANES)
-        level = level_ref[:, pl.ds(own, quarter)]
-        high = level.astype(HALF).astype(FULL)
-        message = jnp.concatenate([values, high, level - high], axis=0)
-        rest = out_ref.shape[1] - quarter
-        if rest:
-            message = jnp.concatenate([message, jnp.zeros((out_ref.shape[0], rest), FULL)], axis=1)
-        out_ref[...] = message.astype(HALF)
-
 
 def turn_kernel(first_ctg, masked_ref, before_ref, out_ref):
     ctgs, units, lines = out_ref.shape
@@ -224,9 +242,9 @@
     hour = lax.broadcasted_iota(jnp.int32, shape, 0)
     row = lax.broadcasted_iota(jnp.int32, shape, 1)
     apart = place ^ (hour // hours) ^ (piece % 2)
-    block = jnp.zeros(shape, jnp.int32)
-    for bit, mask in enumerate([1] + mask_order(devices, piece // 2)):
-        block = block + ((apart // mask) % 2) * 2**bit
+    block = parity(apart)
+    for bit, mask in enumerate(mask_order(devices, piece // 2, True)):
+        block = block + ((apart // mask) % 2) * 2 ** (bit + 1)
     chosen = (row // (2 * hours) == block) & (row % hours == hour % hours)
     return jnp.dot(chosen.astype(FULL).astype(HALF), levels, preferred_element_type=FULL)
 
@@ -299,7 +317,7 @@
     if last:
         level_out, dual_out, ramp_out, price_out, last_moved = refs
     else:
-        last_moved, dual_out, ramp_out, price_out, stat_out, send_ref, keep_ref, half_dual, term_out = refs
+        last_moved, dual_out, ramp_out, price_out, stat_out, send_ref, half_dual, term_out = refs
     moved_refs = moved_refs + [last_moved]
 
     ctgs, lines, units = masked_ref.shape
@@ -382,24 +400,29 @@
         for j, term in enumerate(terms):
             term_out[j : j + 1, at] = term
     block = scalar_block(moved_sq, place, (all_hours, LANES))
-    pull_pieces(0, hours, first_hour, masked_ref, half_dual, term_out, send_ref, keep_ref)
-    for out_ref in (send_ref, keep_ref):
-        out_ref[:, quarter:] = block
-
-
-def pull_pieces(q, hours, first_hour, masked_ref, half_dual, term_ref, send_ref, keep_ref):
+    pull_piece(1, hours, first_hour, masked_ref, half_dual, term_out, send_ref)
+    send_ref[:, quarter:] = block
+
+
+def pull_piece(piece, hours, first_hour, masked_ref, half_dual, term_ref, out_ref):
     ctgs, lines, units = masked_ref.shape
     whole = masked_ref.reshape(ctgs * lines, units)
-    for piece, out_ref in ((2 * q + 1, send_ref), (2 * q, keep_ref)):
-        for at in range(0, units // 4, WIDE):
-            cols = pl.ds(piece_at(piece, units) + at, WIDE)
-            pulled = jnp.dot(half_dual[...], whole[:, cols], preferred_element_type=FULL)
-            terms = [term_ref[j : j + 1, cols] for j in range(hours + 1)]
-            out_ref[:, pl.ds(at, WIDE)] = add_rows(pulled, first_hour, terms).astype(HALF)
-
-
-def pull_kernel(hours, place_ref, masked_ref, half_dual, term_ref, send_ref, keep_ref):
-    pull_pieces(1, hours, place_ref[0] * hours, masked_ref, half_dual, term_ref, send_ref, keep_ref)
+    for at in range(0, units // 4, WIDE):
+        cols = pl.ds(piece_at(piece, units) + at, WIDE)
+        pulled = jnp.dot(half_dual[...], whole[:, cols], preferred_element_type=FULL)
+        terms = [term_ref[j : j + 1, cols] for j in range(hours + 1)]
+        out_ref[:, pl.ds(at, WIDE)] = add_rows(pulled, first_hour, terms).astype(HALF)
+
+
+def middle_pull_kernel(hours, place_ref, masked_ref, half_dual, term_ref, send_a, keep_a, send_b):
+    quarter = send_b.shape[1]
+    pull_piece(0, hours, place_ref[0] * hours, masked_ref, half_dual, term_ref, keep_a)
+    keep_a[:, quarter:] = send_a[:, quarter:]
+    pull_piece(3, hours, place_ref[0] * hours, masked_ref, half_dual, term_ref, send_b)
+
+
+def last_pull_kernel(hours, place_ref, masked_ref, half_dual, term_ref, keep_b):
+    pull_piece(2, hours, place_ref[0] * hours, masked_ref, half_dual, term_ref, keep_b)
 
 
 def add_kernel(own_ref, received_ref, before_ref, out_ref):
@@ -417,7 +440,28 @@
     scratch_ref[:all_hours, :] = own[:all_hours] + received[:all_hours]
     scratch_ref[all_hours : all_hours + extra, :] = own[all_hours:]
     scratch_ref[all_hours + extra :, :] = received[all_hours:]
-    out_ref[...] = scratch_ref[...].astype(HALF)
+    if out_ref is not None:
+        out_ref[...] = scratch_ref[...].astype(HALF)
+
+
+def split_kernel(all_hours, own_ref, received_ref, a_ref, b_ref, scratch_ref):
+    join_kernel(all_hours, own_ref, received_ref, None, scratch_ref)
+    quarter = b_ref.shape[1]
+    a_ref[:, :quarter] = scratch_ref[:, :quarter].astype(HALF)
+    a_ref[:, quarter:] = jnp.zeros((a_ref.shape[0], a_ref.shape[1] - quarter), HALF)
+    b_ref[...] = scratch_ref[:, quarter:].astype(HALF)
+
+
+def first_join(all_hours, own, received):
+    rows, quarter = 2 * own.shape[0] - all_hours, own.shape[1] // 2
+    return call(
+        functools.partial(split_kernel, all_hours),
+        "split",
+        0.3,
+        [own, received],
+        [near(rows, quarter + LANES, dtype=HALF), near(rows, quarter, dtype=HALF)],
+        [near(rows, 2 * quarter)],
+    )
 
 
 def join(all_hours, own, received, *before):
@@ -428,12 +472,15 @@
 
 def exchange(x, mask):
     devices = lax.axis_size("ctg")
-    return lax.ppermute(x, "ctg", [(i, i ^ mask) for i in range(devices)])
-
-
-def mask_order(devices, q):
+    flip = 0 if mask == 1 else 1
+    return lax.ppermute(x, "ctg", [(i, i ^ mask ^ flip) for i in range(devices)])
+
+
+def mask_order(devices, q, first):
     masks = [1 << b for b in range(1, devices.bit_length() - 1)]
-    return masks if q == 0 else masks[-1:] + masks[:-1]
+    turn, back = ORDERS[(2 if first else 0) + q]
+    masks = masks[turn:] + masks[:turn]
+    return masks[::-1] if back else masks
 
 
 def body(
@@ -464,35 +511,22 @@
     table = jnp.pad(ratings, (0, spread)).reshape(-1, LANES)
     row = lambda x: x.reshape(1, units)
     start_rows = all_hours + 2 * hours
-    start_a, start_b = near(start_rows, quarter + LANES, dtype=HALF), near(start_rows, quarter, dtype=HALF)
+    start = near(start_rows, 2 * quarter, dtype=HALF)
     message_a, message_b = near(all_hours, quarter + LANES, dtype=HALF), near(all_hours, quarter, dtype=HALF)
 
-    operands = [flow_tiles, start_flow_dual, base_flow, monitored, table, row(unit_floor), row(unit_span)]
-    operands += [row(ramp_limit), row(ramp_mask), unit_cost, start_ramp_dual, start_output]
-    masked, send_a, keep_a, send_b, keep_b, dual, base, rating, unit, cost, ramp = pl.pallas_call(
+    operands = [flow_tiles, start_flow_dual, row(ramp_mask), unit_cost, start_ramp_dual, start_output]
+    masked, send, keep = pl.pallas_call(
         start_kernel,
-        out_shape=(
-            near(ctgs, lines, units, dtype=HALF),
-            start_a,
-            start_a,
-            start_b,
-            start_b,
-            near(all_hours, ctgs * lines),
-            near(all_hours, ctgs * lines),
-            near(1, ctgs * lines),
-            near(4, units),
-            near(hours, units),
-            near(hours, units),
-        ),
-        in_specs=[SMEM, HBM, HBM] + [VMEM] * 11,
-        out_specs=(VMEM,) * 11,
+        out_shape=(near(ctgs, lines, units, dtype=HALF), start, start),
+        in_specs=[SMEM, HBM, HBM] + [VMEM] * 5,
+        out_specs=(VMEM,) * 3,
         scratch_shapes=[
             pltpu.SMEM(tile_pattern.shape, jnp.int32),
             near(all_hours, units),
             pltpu.SemaphoreType.DMA((ctgs, 2)),
             pltpu.SemaphoreType.DMA,
         ],
-        compiler_params=pltpu.CompilerParams(vmem_limit_bytes=44 * MIB),
+        compiler_params=pltpu.CompilerParams(vmem_limit_bytes=46 * MIB),
         name="start",
     )(here, far(tile_pattern), *[far(x) for x in operands])
     masked = pltpu.with_memory_space_constraint(masked, pltpu.VMEM)
@@ -501,21 +535,44 @@
     for iteration in range(ITERS):
         first, last = iteration == 0, iteration == ITERS - 1
         merge = functools.partial(join, all_hours) if first else jnp.add
-        owns = [merge(keep_a, exchange(send_a, 1)), merge(keep_b, exchange(send_b, 1))]
-        orders = [mask_order(devices, q) for q in range(2)]
+        if first:
+            owns = list(first_join(all_hours, keep, exchange(send, 1)))
+        else:
+            owns = [keep_a + exchange(send_a, 1), keep_b + exchange(send_b, 1)]
+        orders = [mask_order(devices, q, first) for q in range(2)]
         steps = len(orders[0])
         for step in range(steps):
             before = []
+            if first and step == steps - 1:
+                operands = [start_flow_dual, base_flow, monitored, table, row(unit_floor), row(unit_span)]
+                operands += [row(ramp_limit), row(ramp_mask), unit_cost, start_ramp_dual]
+                dual, base, rating, unit, cost, ramp = call(
+                    prepare_kernel,
+                    "prepare",
+                    1.5,
+                    [here, owns[0], *[far(x) for x in operands]],
+                    [
+                        near(all_hours, ctgs * lines),
+                        near(all_hours, ctgs * lines),
+                        near(1, ctgs * lines),
+                        near(4, units),
+                        near(hours, units),
+                        near(hours, units),
+                    ],
+                    smem=(0,),
+                )
+                before.append(rating)
             if first:
-                for turn in range(ctgs * step // steps, ctgs * (step + 1) // steps):
-                    before += call(
+                share = [0] * (steps - len(TURNS)) + [ctgs * part // 8 for part in TURNS]
+                for turn in range(sum(share[:step]), sum(share[: step + 1])):
+                    turned += call(
                         functools.partial(turn_kernel, turn),
                         "turn",
                         0.45,
                         [masked, owns[0]],
                         [near(1, units, lines, dtype=HALF)],
                     )
-                turned += before
+                before += turned
             owns[0] = merge(owns[0], exchange(owns[0], orders[0][step]), *before)
             if first or step < steps - 1:
                 owns[1] = merge(owns[1], exchange(owns[1], orders[1][step]))
@@ -551,15 +608,21 @@
             out_shape = [f32(hours, units), f32(all_hours, ctgs, lines), f32(hours, units), f32(hours)]
             return call(kernel, "dual", 1.2, operands, out_shape, [near(all_hours, quarter)], smem, (3,))
         out_shape = [near(all_hours, quarter), near(all_hours, ctgs * lines), near(hours, units), near(hours, 1)]
-        out_shape += [near(8, LANES), message_a, message_a, near(all_hours, ctgs * lines, dtype=HALF), near(8, units)]
+        out_shape += [near(8, LANES), message_a, near(all_hours, ctgs * lines, dtype=HALF), near(8, units)]
         scratch = [near(all_hours, quarter)] if first else []
-        outs = call(kernel, "dual", 2.1, operands, out_shape, scratch, smem)
+        outs = call(kernel, "dual", 1.5, operands, out_shape, scratch, smem)
         levels = (*moved, outs[0])
-        dual, ramp, price, stat, send_a, keep_a, half_dual, terms = outs[1:]
+        dual, ramp, price, stat, send_a, half_dual, terms = outs[1:]
         operands = [here, masked, half_dual, terms]
-        send_b, keep_b = call(
-            functools.partial(pull_kernel, hours), "pull", 1.2, operands, [message_b, message_b], smem=(0,)
+        keep_a, send_b = call(
+            functools.partial(middle_pull_kernel, hours),
+            "pull",
+            1.2,
+            [*operands, send_a],
+            [message_a, message_b],
+            smem=(0,),
         )
+        (keep_b,) = call(functools.partial(last_pull_kernel, hours), "pull", 0.6, operands, [message_b], smem=(0,))
 
 
 def solution(mesh):

time: 97.2 us -> 95.1 us (0.978)
  waiting for transfers between devices: 30.1 us -> 19.6 us
  starting transfers between devices: 35.2 us -> 41.7 us
  Pallas kernels: 30.2 us -> 32 us
    ppermute x40 -> x39, waiting for transfers between devices: 30.1 us -> 19.6 us  [exchange(): lax.ppermute(x, 'ctg', [(i, i ^ mask ^ flip) for i in range(devices)])]
    ppermute x40 -> x39, starting transfers between devices: 35.2 us -> 41.7 us  [exchange(): lax.ppermute(x, 'ctg', [(i, i ^ mask ^ flip) for i in range(devices)])]
    pallas_call x38 -> x41, Pallas kernels: 23.7 us -> 26 us  [call(): pl.pallas_call(kernel, out_shape=tuple(out_shape), in_specs=[SMEM if j in...]
  transfers between devices with their start and end apart: 40 -> 39, of which waited for: 23 -> 19; matrix products, arithmetic and copies ran while one was open for 0% -> 0% of each run, Pallas kernels for 17% -> 21%
where the time goes in v3:
time: 95.1 us; the launch traced here: 94.9 us
  starting transfers between devices  41.7 us (44%)
  Pallas kernels  32 us (34%)
  waiting for transfers between devices  19.6 us (21%)
  between operations  1.21 us (1%)
    ppermute x39, starting transfers between devices, exchange(): lax.ppermute(x, 'ctg', [(i, i ^ mask ^ flip) for i in range(devices)])  41.7 us
    pallas_call x41, Pallas kernels, call(): pl.pallas_call(kernel, out_shape=tuple(out_shape), in_specs=[SMEM if j in...  26 us
    ppermute x39, waiting for transfers between devices, exchange(): lax.ppermute(x, 'ctg', [(i, i ^ mask ^ flip) for i in range(devices)])  19.6 us
    pallas_call x1, Pallas kernels, body(): pl.pallas_call(start_kernel, out_shape=(near(ctgs, lines, units, dtype=HA...  6.08 us
  transfers between devices with their start and end apart: 39, of which 19 were waited for; matrix products, arithmetic and copies ran while one was open for 0% of the time, Pallas kernels for 21%

profile of v3, /device:TPU:0, one launch (start us, length us, event | category | flops | bytes accessed | tf_op | source)
XLA Modules:
  0.0 94.9 jit_solution(9204319491639947642)
XLA Ops:
  0.6 6.1 %start.1 = (bf16[8,256,3072]{2,1,0:T(8,128)(2,1)S(1)}, bf16[36,1536]{1,0:T(8,128)(2,1)S(1)}, bf16[36,1536]{1,0:T(8,128)(2,1)S(1)}) custom-call(s32[1]{0:T(128)} %bitcast.place_ref.refs_8_, s32[8,2,24]{2,1,0:T(2,128)} %gate_hbm.1, bf16[8,256,3072]{2,1,0:T(8,128)(2,1)} %tiles_ref.1, f32[32,8,256]{2,1,0:T(8,128)} %dual_ref.3, s32[1,3072]{1,0:T(1,128)} %bitcast.12, ...), custom_call_target="tpu_custom_call" | custom-call | tf_op jit(solution)/shard_map/start/pallas_call | solution.py:518
  6.7 0.5 collective-permute-start
  7.2 1.0 %collective-permute-done.received_ref = bf16[36,1536]{1,0:T(8,128)(2,1)S(1)} collective-permute-done((bf16[36,1536]{1,0:T(8,128)(2,1)S(1)}, bf16[36,1536]{1,0:T(8,128)(2,1)S(1)}, u32[]{:S(2)}, u32[]{:S(2)}) %collective-permute-start) | collective-permute-done | bytes 110624 | tf_op jit(solution)/shard_map/ppermute | solution.py:476
  8.3 2.7 %collective-permute-start.1 = (bf16[40,896]{1,0:T(8,128)(2,1)S(1)}, bf16[40,896]{1,0:T(8,128)(2,1)S(1)}, u32[]{:S(2)}, u32[]{:S(2)}) collective-permute-start(bf16[40,896]{1,0:T(8,128)(2,1)S(1)} %get-tuple-element.79.before_ref.own_ref), channel_id=1, source_target_pairs={{0,3},{1,2},{2,1},{3,0},{4,7},{5,6},{6,5},{7,4},{8,11},{9,10},{10,... | collective-permute-start | bytes 215048 | tf_op jit(solution)/shard_map/ppermute | solution.py:476
  11.0 2.6 %collective-permute-start.3 = (bf16[40,768]{1,0:T(8,128)(2,1)S(1)}, bf16[40,768]{1,0:T(8,128)(2,1)S(1)}, u32[]{:S(2)}, u32[]{:S(2)}) collective-permute-start(bf16[40,768]{1,0:T(8,128)(2,1)S(1)} %get-tuple-element.80.own_ref), channel_id=1, source_target_pairs={{0,9},{1,8},{2,11},{3,10},{4,13},{5,12},{6,15},{7,14},{8,1},{9,0},... | collective-permute-start | bytes 184328 | tf_op jit(solution)/shard_map/ppermute | solution.py:476
  14.5 1.4 %collective-permute-start.2 = (bf16[48,896]{1,0:T(8,128)(2,1)S(1)}, bf16[48,896]{1,0:T(8,128)(2,1)S(1)}, u32[]{:S(2)}, u32[]{:S(2)}) collective-permute-start(bf16[48,896]{1,0:T(8,128)(2,1)S(1)} %join.6.before_ref.own_ref), channel_id=1, source_target_pairs={{0,5},{1,4},{2,7},{3,6},{4,1},{5,0},{6,3},{7,2},{8,13},{9,12},{10,... | collective-permute-start | bytes 258056 | tf_op jit(solution)/shard_map/ppermute | solution.py:476
  15.9 1.5 %collective-permute-start.4 = (bf16[48,768]{1,0:T(8,128)(2,1)S(1)}, bf16[48,768]{1,0:T(8,128)(2,1)S(1)}, u32[]{:S(2)}, u32[]{:S(2)}) collective-permute-start(bf16[48,768]{1,0:T(8,128)(2,1)S(1)} %join.8.own_ref), channel_id=1, source_target_pairs={{0,3},{1,2},{2,1},{3,0},{4,7},{5,6},{6,5},{7,4},{8,11},{9,10},{10,... | collective-permute-start | bytes 221192 | tf_op jit(solution)/shard_map/ppermute | solution.py:476
  19.1 1.9 %collective-permute-start.7 = (bf16[64,896]{1,0:T(8,128)(2,1)S(1)}, bf16[64,896]{1,0:T(8,128)(2,1)S(1)}, u32[]{:S(2)}, u32[]{:S(2)}) collective-permute-start(bf16[64,896]{1,0:T(8,128)(2,1)S(1)} %join.7.before_ref.own_ref), channel_id=1, source_target_pairs={{0,9},{1,8},{2,11},{3,10},{4,13},{5,12},{6,15},{7,14},{8,1},{9,0},... | collective-permute-start | bytes 344072 | tf_op jit(solution)/shard_map/ppermute | solution.py:476
  21.0 2.2 %collective-permute-start.5 = (bf16[64,768]{1,0:T(8,128)(2,1)S(1)}, bf16[64,768]{1,0:T(8,128)(2,1)S(1)}, u32[]{:S(2)}, u32[]{:S(2)}) collective-permute-start(bf16[64,768]{1,0:T(8,128)(2,1)S(1)} %join.9.own_ref), channel_id=1, source_target_pairs={{0,5},{1,4},{2,7},{3,6},{4,1},{5,0},{6,3},{7,2},{8,13},{9,12},{10,... | collective-permute-start | bytes 294920 | tf_op jit(solution)/shard_map/ppermute | solution.py:476
  24.6 1.9 %prepare.1 = (f32[32,2048]{1,0:T(8,128)S(1)}, f32[32,2048]{1,0:T(8,128)S(1)}, f32[1,2048]{1,0:T(1,128)S(1)}, f32[4,3072]{1,0:T(4,128)S(1)}, f32[2,3072]{1,0:T(2,128)S(1)}, /*index=5*/f32[2,3072]{1,0:T(2,128)S(1)}) custom-call(s32[1]{0:T(128)} %bitcast.place_ref.refs_8_, bf16[64,896]{1,0:T(8,128)(2,1)S(1)} %join.7.before_ref.own_ref, f32[32,8,256]{2,1,0:T(8,128)} %dual_ref.3, ...), custom_call_target="tpu_custom_call" | custom-call | bytes 5535000 | tf_op jit(solution)/shard_map/prepare/pallas_call | solution.py:36
  26.6 0.8 collective-permute-done.7.received_ref
  27.4 0.5 collective-permute-start.8
  28.1 0.8 flow.12
  28.9 0.8 flow.13
  29.7 0.8 flow.14
  30.6 1.5 %dual.4 = (f32[32,768]{1,0:T(8,128)S(1)}, f32[32,2048]{1,0:T(8,128)S(1)}, f32[2,3072]{1,0:T(2,128)S(1)}, f32[2,1]{1,0:T(2,128)S(1)}, f32[8,128]{1,0:T(8,128)S(1)...) custom-call(bf16[1,3072,256]{2,1,0:T(8,128)(2,1)S(1)} %turn.8.refs_0_.refs_1_, ...), custom_call_target="tpu_custom_call" | custom-call | bytes 5535000 | tf_op jit(solution)/shard_map/dual/pallas_call | solution.py:36
  32.5 1.2 %pull.7 = (bf16[32,896]{1,0:T(8,128)(2,1)S(1)}, bf16[32,768]{1,0:T(8,128)(2,1)S(1)}) custom-call(s32[1]{0:T(128)} %bitcast.place_ref.refs_8_, bf16[8,256,3072]{2,1,0:T(8,128)(2,1)S(1)} %get-tuple-element.76.masked_ref.refs_9_, bf16[32,2048]{1,0:T(8,128)(2,1)S(1)} %get-tuple-element.97.half_dual, f32[8,3072]{1,0:T(8,128)S(1)} %get-tuple-element.98.term_ref, ...), custom_call_target="tpu_custom_call" | custom-call | bytes 4428000 | tf_op jit(solution)/shard_map/pull/pallas_call | solution.py:36
  33.9 1.5 %collective-permute-start.14 = (bf16[32,896]{1,0:T(8,128)(2,1)S(1)}, bf16[32,896]{1,0:T(8,128)(2,1)S(1)}, u32[]{:S(2)}, u32[]{:S(2)}) collective-permute-start(bf16[32,896]{1,0:T(8,128)(2,1)S(1)} %add.69), channel_id=1, source_target_pairs={{0,3},{1,2},{2,1},{3,0},{4,7},{5,6},{6,5},{7,4},{8,11},{9,10},{10,... | collective-permute-start | bytes 172040 | tf_op jit(solution)/shard_map/ppermute | solution.py:476
  35.5 0.7 pull.6
  36.2 1.8 %collective-permute-start.10 = (bf16[32,768]{1,0:T(8,128)(2,1)S(1)}, bf16[32,768]{1,0:T(8,128)(2,1)S(1)}, u32[]{:S(2)}, u32[]{:S(2)}) collective-permute-start(bf16[32,768]{1,0:T(8,128)(2,1)S(1)} %add.66), channel_id=1, source_target_pairs={{0,9},{1,8},{2,11},{3,10},{4,13},{5,12},{6,15},{7,14},{8,1},{9,0},... | collective-permute-start | bytes 147464 | tf_op jit(solution)/shard_map/ppermute | solution.py:476
  38.0 2.4 %collective-permute-start.15 = (bf16[32,896]{1,0:T(8,128)(2,1)S(1)}, bf16[32,896]{1,0:T(8,128)(2,1)S(1)}, u32[]{:S(2)}, u32[]{:S(2)}) collective-permute-start(bf16[32,896]{1,0:T(8,128)(2,1)S(1)} %add.70), channel_id=1, source_target_pairs={{0,5},{1,4},{2,7},{3,6},{4,1},{5,0},{6,3},{7,2},{8,13},{9,12},{10,... | collective-permute-start | bytes 172040 | tf_op jit(solution)/shard_map/ppermute | solution.py:476
  40.7 1.2 %collective-permute-start.11 = (bf16[32,768]{1,0:T(8,128)(2,1)S(1)}, bf16[32,768]{1,0:T(8,128)(2,1)S(1)}, u32[]{:S(2)}, u32[]{:S(2)}) collective-permute-start(bf16[32,768]{1,0:T(8,128)(2,1)S(1)} %add.67), channel_id=1, source_target_pairs={{0,3},{1,2},{2,1},{3,0},{4,7},{5,6},{6,5},{7,4},{8,11},{9,10},{10,... | collective-permute-start | bytes 147464 | tf_op jit(solution)/shard_map/ppermute | solution.py:476
  41.9 0.8 collective-permute-done.15
  42.7 2.5 %collective-permute-start.16 = (bf16[32,896]{1,0:T(8,128)(2,1)S(1)}, bf16[32,896]{1,0:T(8,128)(2,1)S(1)}, u32[]{:S(2)}, u32[]{:S(2)}) collective-permute-start(bf16[32,896]{1,0:T(8,128)(2,1)S(1)} %add.71), channel_id=1, source_target_pairs={{0,9},{1,8},{2,11},{3,10},{4,13},{5,12},{6,15},{7,14},{8,1},{9,0},... | collective-permute-start | bytes 172040 | tf_op jit(solution)/shard_map/ppermute | solution.py:476
  45.2 1.8 %collective-permute-start.12 = (bf16[32,768]{1,0:T(8,128)(2,1)S(1)}, bf16[32,768]{1,0:T(8,128)(2,1)S(1)}, u32[]{:S(2)}, u32[]{:S(2)}) collective-permute-start(bf16[32,768]{1,0:T(8,128)(2,1)S(1)} %add.68.own_ref), channel_id=1, source_target_pairs={{0,5},{1,4},{2,7},{3,6},{4,1},{5,0},{6,3},{7,2},{8,13},{9,12},{10,... | collective-permute-start | bytes 147464 | tf_op jit(solution)/shard_map/ppermute | solution.py:476
  47.0 0.6 collective-permute-done.16
  47.8 0.9 flow.15
  48.8 0.7 collective-permute-start.17
  49.5 0.7 flow.16
  50.1 0.7 flow.17
  50.8 1.3 %dual.5 = (f32[32,768]{1,0:T(8,128)S(1)}, f32[32,2048]{1,0:T(8,128)S(1)}, f32[2,3072]{1,0:T(2,128)S(1)}, f32[2,1]{1,0:T(2,128)S(1)}, f32[8,128]{1,0:T(8,128)S(1)...) custom-call(bf16[1,3072,256]{2,1,0:T(8,128)(2,1)S(1)} %turn.8.refs_0_.refs_1_, ...), custom_call_target="tpu_custom_call" | custom-call | bytes 5535000 | tf_op jit(solution)/shard_map/dual/pallas_call | solution.py:36
  52.3 1.2 %pull.9 = (bf16[32,896]{1,0:T(8,128)(2,1)S(1)}, bf16[32,768]{1,0:T(8,128)(2,1)S(1)}) custom-call(s32[1]{0:T(128)} %bitcast.place_ref.refs_8_, bf16[8,256,3072]{2,1,0:T(8,128)(2,1)S(1)} %get-tuple-element.76.masked_ref.refs_9_, bf16[32,2048]{1,0:T(8,128)(2,1)S(1)} %get-tuple-element.114.half_dual, f32[8,3072]{1,0:T(8,128)S(1)} %get-tuple-element.115.term_ref, ...), custom_call_target="tpu_custom_call" | custom-call | bytes 4428000 | tf_op jit(solution)/shard_map/pull/pallas_call | solution.py:36
  53.5 0.6 collective-permute-start.19
  54.1 2.2 %collective-permute-start.24 = (bf16[32,896]{1,0:T(8,128)(2,1)S(1)}, bf16[32,896]{1,0:T(8,128)(2,1)S(1)}, u32[]{:S(2)}, u32[]{:S(2)}) collective-permute-start(bf16[32,896]{1,0:T(8,128)(2,1)S(1)} %add.76), channel_id=1, source_target_pairs={{0,3},{1,2},{2,1},{3,0},{4,7},{5,6},{6,5},{7,4},{8,11},{9,10},{10,... | collective-permute-start | bytes 172040 | tf_op jit(solution)/shard_map/ppermute | solution.py:476
  56.3 0.6 pull.8
  57.0 1.4 %collective-permute-start.20 = (bf16[32,768]{1,0:T(8,128)(2,1)S(1)}, bf16[32,768]{1,0:T(8,128)(2,1)S(1)}, u32[]{:S(2)}, u32[]{:S(2)}) collective-permute-start(bf16[32,768]{1,0:T(8,128)(2,1)S(1)} %add.73), channel_id=1, source_target_pairs={{0,9},{1,8},{2,11},{3,10},{4,13},{5,12},{6,15},{7,14},{8,1},{9,0},... | collective-permute-start | bytes 147464 | tf_op jit(solution)/shard_map/ppermute | solution.py:476
  58.5 2.0 %collective-permute-start.25 = (bf16[32,896]{1,0:T(8,128)(2,1)S(1)}, bf16[32,896]{1,0:T(8,128)(2,1)S(1)}, u32[]{:S(2)}, u32[]{:S(2)}) collective-permute-start(bf16[32,896]{1,0:T(8,128)(2,1)S(1)} %add.77), channel_id=1, source_target_pairs={{0,5},{1,4},{2,7},{3,6},{4,1},{5,0},{6,3},{7,2},{8,13},{9,12},{10,... | collective-permute-start | bytes 172040 | tf_op jit(solution)/shard_map/ppermute | solution.py:476
  60.5 2.4 %collective-permute-done.20 = bf16[32,768]{1,0:T(8,128)(2,1)S(1)} collective-permute-done((bf16[32,768]{1,0:T(8,128)(2,1)S(1)}, bf16[32,768]{1,0:T(8,128)(2,1)S(1)}, u32[]{:S(2)}, u32[]{:S(2)}) %collective-permute-start.20) | collective-permute-done | bytes 49184 | tf_op jit(solution)/shard_map/ppermute | solution.py:476
  63.2 2.0 %collective-permute-start.26 = (bf16[32,896]{1,0:T(8,128)(2,1)S(1)}, bf16[32,896]{1,0:T(8,128)(2,1)S(1)}, u32[]{:S(2)}, u32[]{:S(2)}) collective-permute-start(bf16[32,896]{1,0:T(8,128)(2,1)S(1)} %add.78), channel_id=1, source_target_pairs={{0,9},{1,8},{2,11},{3,10},{4,13},{5,12},{6,15},{7,14},{8,1},{9,0},... | collective-permute-start | bytes 172040 | tf_op jit(solution)/shard_map/ppermute | solution.py:476
  65.2 1.6 %collective-permute-done.21 = bf16[32,768]{1,0:T(8,128)(2,1)S(1)} collective-permute-done((bf16[32,768]{1,0:T(8,128)(2,1)S(1)}, bf16[32,768]{1,0:T(8,128)(2,1)S(1)}, u32[]{:S(2)}, u32[]{:S(2)}) %collective-permute-start.21) | collective-permute-done | bytes 49184 | tf_op jit(solution)/shard_map/ppermute | solution.py:476
  66.7 0.5 collective-permute-start.22
  67.3 0.8 collective-permute-done.26
  68.0 1.5 %collective-permute-start.28 = (bf16[32,896]{1,0:T(8,128)(2,1)S(1)}, bf16[32,896]{1,0:T(8,128)(2,1)S(1)}, u32[]{:S(2)}, u32[]{:S(2)}) collective-permute-start(bf16[32,896]{1,0:T(8,128)(2,1)S(1)} %add.79.refs_9_), channel_id=1, source_target_pairs={{0,1},{1,0},{2,3},{3,2},{4,5},{5,4},{6,7},{7,6},{8,9},{9,8},{10,11... | collective-permute-start | bytes 172040 | tf_op jit(solution)/shard_map/ppermute | solution.py:476
  69.5 0.8 flow.18
  70.8 0.7 flow.19
  71.4 0.7 flow.20
  72.1 1.3 %dual.6 = (f32[32,768]{1,0:T(8,128)S(1)}, f32[32,2048]{1,0:T(8,128)S(1)}, f32[2,3072]{1,0:T(2,128)S(1)}, f32[2,1]{1,0:T(2,128)S(1)}, f32[8,128]{1,0:T(8,128)S(1)...) custom-call(bf16[1,3072,256]{2,1,0:T(8,128)(2,1)S(1)} %turn.8.refs_0_.refs_1_, ...), custom_call_target="tpu_custom_call" | custom-call | bytes 5535000 | tf_op jit(solution)/shard_map/dual/pallas_call | solution.py:36
  73.5 0.5 collective-permute-start.33
  73.9 1.2 %pull.11 = (bf16[32,896]{1,0:T(8,128)(2,1)S(1)}, bf16[32,768]{1,0:T(8,128)(2,1)S(1)}) custom-call(s32[1]{0:T(128)} %bitcast.place_ref.refs_8_, bf16[8,256,3072]{2,1,0:T(8,128)(2,1)S(1)} %get-tuple-element.76.masked_ref.refs_9_, bf16[32,2048]{1,0:T(8,128)(2,1)S(1)} %get-tuple-element.131.half_dual, f32[8,3072]{1,0:T(8,128)S(1)} %get-tuple-element.132.term_ref, ...), custom_call_target="tpu_custom_call" | custom-call | bytes 4428000 | tf_op jit(solution)/shard_map/pull/pallas_call | solution.py:36
  75.4 1.4 %collective-permute-start.34 = (bf16[32,896]{1,0:T(8,128)(2,1)S(1)}, bf16[32,896]{1,0:T(8,128)(2,1)S(1)}, u32[]{:S(2)}, u32[]{:S(2)}) collective-permute-start(bf16[32,896]{1,0:T(8,128)(2,1)S(1)} %add.83), channel_id=1, source_target_pairs={{0,3},{1,2},{2,1},{3,0},{4,7},{5,6},{6,5},{7,4},{8,11},{9,10},{10,... | collective-permute-start | bytes 172040 | tf_op jit(solution)/shard_map/ppermute | solution.py:476
  76.8 0.6 pull.10
  77.7 1.5 %collective-permute-done.34 = bf16[32,896]{1,0:T(8,128)(2,1)S(1)} collective-permute-done((bf16[32,896]{1,0:T(8,128)(2,1)S(1)}, bf16[32,896]{1,0:T(8,128)(2,1)S(1)}, u32[]{:S(2)}, u32[]{:S(2)}) %collective-permute-start.34) | collective-permute-done | bytes 57376 | tf_op jit(solution)/shard_map/ppermute | solution.py:476
  79.2 1.0 %collective-permute-start.35 = (bf16[32,896]{1,0:T(8,128)(2,1)S(1)}, bf16[32,896]{1,0:T(8,128)(2,1)S(1)}, u32[]{:S(2)}, u32[]{:S(2)}) collective-permute-start(bf16[32,896]{1,0:T(8,128)(2,1)S(1)} %add.84), channel_id=1, source_target_pairs={{0,5},{1,4},{2,7},{3,6},{4,1},{5,0},{6,3},{7,2},{8,13},{9,12},{10,... | collective-permute-start | bytes 172040 | tf_op jit(solution)/shard_map/ppermute | solution.py:476
  80.3 3.1 %collective-permute-done.30 = bf16[32,768]{1,0:T(8,128)(2,1)S(1)} collective-permute-done((bf16[32,768]{1,0:T(8,128)(2,1)S(1)}, bf16[32,768]{1,0:T(8,128)(2,1)S(1)}, u32[]{:S(2)}, u32[]{:S(2)}) %collective-permute-start.30) | collective-permute-done | bytes 49184 | tf_op jit(solution)/shard_map/ppermute | solution.py:476
  83.4 0.5 collective-permute-start.31
  83.8 0.5 collective-permute-done.35
  84.4 0.6 collective-permute-start.36
  85.0 2.2 %collective-permute-done.31 = bf16[32,768]{1,0:T(8,128)(2,1)S(1)} collective-permute-done((bf16[32,768]{1,0:T(8,128)(2,1)S(1)}, bf16[32,768]{1,0:T(8,128)(2,1)S(1)}, u32[]{:S(2)}, u32[]{:S(2)}) %collective-permute-start.31) | collective-permute-done | bytes 49184 | tf_op jit(solution)/shard_map/ppermute | solution.py:476
  87.4 3.0 %collective-permute-done.36 = bf16[32,896]{1,0:T(8,128)(2,1)S(1)} collective-permute-done((bf16[32,896]{1,0:T(8,128)(2,1)S(1)}, bf16[32,896]{1,0:T(8,128)(2,1)S(1)}, u32[]{:S(2)}, u32[]{:S(2)}) %collective-permute-start.36) | collective-permute-done | bytes 57376 | tf_op jit(solution)/shard_map/ppermute | solution.py:476
  90.6 0.8 flow.21
  91.4 0.5 collective-permute-start.37
  91.9 0.7 flow.22
  92.5 0.7 flow.23
  93.3 1.5 %dual.7 = (f32[2,3072]{1,0:T(2,128)}, f32[32,8,256]{2,1,0:T(8,128)}, f32[2,3072]{1,0:T(2,128)}, f32[2]{0:T(128)}) custom-call(bf16[1,3072,256]{2,1,0:T(8,128)(2,1)S(1)} %turn.8.refs_0_.refs_1_, bf16[1,3072,256]{2,1,0:T(8,128)(2,1)S(1)} %turn.9.refs_1_.refs_2_, bf16[1,3072,256]{2,1,0:T(8,128)(2,1)S(1)} %turn.10.refs_2_.refs_3_, ...), custom_call_target="tpu_custom_call" | custom-call | bytes 4428000 | tf_op jit(solution)/shard_map/dual/pallas_call | solution.py:36
  (79 shorter events, 7.6 us)
Async XLA Ops:
  6.7 1.5 %collective-permute-start = (bf16[36,1536]{1,0:T(8,128)(2,1)S(1)}, bf16[36,1536]{1,0:T(8,128)(2,1)S(1)}, u32[]{:S(2)}, u32[]{:S(2)}) collective-permute-start(bf16[36,1536]{1,0:T(8,128)(2,1)S(1)} %get-tuple-element.78), channel_id=1, source_target_pairs={{0,1},{1,0},{2,3},{3,2},{4,5},{5,4},{6,7},{7,6},{8,9},{9,8},{10,11... | collective-permute-start | bytes 331784 | tf_op jit(solution)/shard_map/ppermute | solution.py:476
  8.3 6.2 %collective-permute-start.1 = (bf16[40,896]{1,0:T(8,128)(2,1)S(1)}, bf16[40,896]{1,0:T(8,128)(2,1)S(1)}, u32[]{:S(2)}, u32[]{:S(2)}) collective-permute-start(bf16[40,896]{1,0:T(8,128)(2,1)S(1)} %get-tuple-element.79.before_ref.own_ref), channel_id=1, source_target_pairs={{0,3},{1,2},{2,1},{3,0},{4,7},{5,6},{6,5},{7,4},{8,11},{9,10},{10,... | collective-permute-start | bytes 215048 | tf_op jit(solution)/shard_map/ppermute | solution.py:476
  11.0 4.9 %collective-permute-start.3 = (bf16[40,768]{1,0:T(8,128)(2,1)S(1)}, bf16[40,768]{1,0:T(8,128)(2,1)S(1)}, u32[]{:S(2)}, u32[]{:S(2)}) collective-permute-start(bf16[40,768]{1,0:T(8,128)(2,1)S(1)} %get-tuple-element.80.own_ref), channel_id=1, source_target_pairs={{0,9},{1,8},{2,11},{3,10},{4,13},{5,12},{6,15},{7,14},{8,1},{9,0},... | collective-permute-start | bytes 184328 | tf_op jit(solution)/shard_map/ppermute | solution.py:476
  14.5 4.6 %collective-permute-start.2 = (bf16[48,896]{1,0:T(8,128)(2,1)S(1)}, bf16[48,896]{1,0:T(8,128)(2,1)S(1)}, u32[]{:S(2)}, u32[]{:S(2)}) collective-permute-start(bf16[48,896]{1,0:T(8,128)(2,1)S(1)} %join.6.before_ref.own_ref), channel_id=1, source_target_pairs={{0,5},{1,4},{2,7},{3,6},{4,1},{5,0},{6,3},{7,2},{8,13},{9,12},{10,... | collective-permute-start | bytes 258056 | tf_op jit(solution)/shard_map/ppermute | solution.py:476
  15.9 5.1 %collective-permute-start.4 = (bf16[48,768]{1,0:T(8,128)(2,1)S(1)}, bf16[48,768]{1,0:T(8,128)(2,1)S(1)}, u32[]{:S(2)}, u32[]{:S(2)}) collective-permute-start(bf16[48,768]{1,0:T(8,128)(2,1)S(1)} %join.8.own_ref), channel_id=1, source_target_pairs={{0,3},{1,2},{2,1},{3,0},{4,7},{5,6},{6,5},{7,4},{8,11},{9,10},{10,... | collective-permute-start | bytes 221192 | tf_op jit(solution)/shard_map/ppermute | solution.py:476
  19.1 8.3 %collective-permute-start.7 = (bf16[64,896]{1,0:T(8,128)(2,1)S(1)}, bf16[64,896]{1,0:T(8,128)(2,1)S(1)}, u32[]{:S(2)}, u32[]{:S(2)}) collective-permute-start(bf16[64,896]{1,0:T(8,128)(2,1)S(1)} %join.7.before_ref.own_ref), channel_id=1, source_target_pairs={{0,9},{1,8},{2,11},{3,10},{4,13},{5,12},{6,15},{7,14},{8,1},{9,0},... | collective-permute-start | bytes 344072 | tf_op jit(solution)/shard_map/ppermute | solution.py:476
  21.0 6.8 %collective-permute-start.5 = (bf16[64,768]{1,0:T(8,128)(2,1)S(1)}, bf16[64,768]{1,0:T(8,128)(2,1)S(1)}, u32[]{:S(2)}, u32[]{:S(2)}) collective-permute-start(bf16[64,768]{1,0:T(8,128)(2,1)S(1)} %join.9.own_ref), channel_id=1, source_target_pairs={{0,5},{1,4},{2,7},{3,6},{4,1},{5,0},{6,3},{7,2},{8,13},{9,12},{10,... | collective-permute-start | bytes 294920 | tf_op jit(solution)/shard_map/ppermute | solution.py:476
  27.4 1.5 %collective-permute-start.8 = (bf16[96,896]{1,0:T(8,128)(2,1)S(1)}, bf16[96,896]{1,0:T(8,128)(2,1)S(1)}, u32[]{:S(2)}, u32[]{:S(2)}) collective-permute-start(bf16[96,896]{1,0:T(8,128)(2,1)S(1)} %join.11.refs_9_), channel_id=1, source_target_pairs={{0,1},{1,0},{2,3},{3,2},{4,5},{5,4},{6,7},{7,6},{8,9},{9,8},{10,11... | collective-permute-start | bytes 516104 | tf_op jit(solution)/shard_map/ppermute | solution.py:476
  27.9 2.6 %collective-permute-start.6 = (bf16[96,768]{1,0:T(8,128)(2,1)S(1)}, bf16[96,768]{1,0:T(8,128)(2,1)S(1)}, u32[]{:S(2)}, u32[]{:S(2)}) collective-permute-start(bf16[96,768]{1,0:T(8,128)(2,1)S(1)} %join.10.refs_9_), channel_id=1, source_target_pairs={{0,1},{1,0},{2,3},{3,2},{4,5},{5,4},{6,7},{7,6},{8,9},{9,8},{10,11... | collective-permute-start | bytes 442376 | tf_op jit(solution)/shard_map/ppermute | solution.py:476
  29.7 0.8 copy-start
  32.0 1.9 %collective-permute-start.13 = (bf16[32,896]{1,0:T(8,128)(2,1)S(1)}, bf16[32,896]{1,0:T(8,128)(2,1)S(1)}, u32[]{:S(2)}, u32[]{:S(2)}) collective-permute-start(bf16[32,896]{1,0:T(8,128)(2,1)S(1)} %get-tuple-element.99.send_a), channel_id=1, source_target_pairs={{0,1},{1,0},{2,3},{3,2},{4,5},{5,4},{6,7},{7,6},{8,9},{9,8},{10,11... | collective-permute-start | bytes 172040 | tf_op jit(solution)/shard_map/ppermute | solution.py:476
  33.7 2.4 %collective-permute-start.9 = (bf16[32,768]{1,0:T(8,128)(2,1)S(1)}, bf16[32,768]{1,0:T(8,128)(2,1)S(1)}, u32[]{:S(2)}, u32[]{:S(2)}) collective-permute-start(bf16[32,768]{1,0:T(8,128)(2,1)S(1)} %get-tuple-element.100), channel_id=1, source_target_pairs={{0,1},{1,0},{2,3},{3,2},{4,5},{5,4},{6,7},{7,6},{8,9},{9,8},{10,11... | collective-permute-start | bytes 147464 | tf_op jit(solution)/shard_map/ppermute | solution.py:476
  33.9 4.0 %collective-permute-start.14 = (bf16[32,896]{1,0:T(8,128)(2,1)S(1)}, bf16[32,896]{1,0:T(8,128)(2,1)S(1)}, u32[]{:S(2)}, u32[]{:S(2)}) collective-permute-start(bf16[32,896]{1,0:T(8,128)(2,1)S(1)} %add.69), channel_id=1, source_target_pairs={{0,3},{1,2},{2,1},{3,0},{4,7},{5,6},{6,5},{7,4},{8,11},{9,10},{10,... | collective-permute-start | bytes 172040 | tf_op jit(solution)/shard_map/ppermute | solution.py:476
  36.2 4.5 %collective-permute-start.10 = (bf16[32,768]{1,0:T(8,128)(2,1)S(1)}, bf16[32,768]{1,0:T(8,128)(2,1)S(1)}, u32[]{:S(2)}, u32[]{:S(2)}) collective-permute-start(bf16[32,768]{1,0:T(8,128)(2,1)S(1)} %add.66), channel_id=1, source_target_pairs={{0,9},{1,8},{2,11},{3,10},{4,13},{5,12},{6,15},{7,14},{8,1},{9,0},... | collective-permute-start | bytes 147464 | tf_op jit(solution)/shard_map/ppermute | solution.py:476
  38.0 4.7 %collective-permute-start.15 = (bf16[32,896]{1,0:T(8,128)(2,1)S(1)}, bf16[32,896]{1,0:T(8,128)(2,1)S(1)}, u32[]{:S(2)}, u32[]{:S(2)}) collective-permute-start(bf16[32,896]{1,0:T(8,128)(2,1)S(1)} %add.70), channel_id=1, source_target_pairs={{0,5},{1,4},{2,7},{3,6},{4,1},{5,0},{6,3},{7,2},{8,13},{9,12},{10,... | collective-permute-start | bytes 172040 | tf_op jit(solution)/shard_map/ppermute | solution.py:476
  40.7 4.5 %collective-permute-start.11 = (bf16[32,768]{1,0:T(8,128)(2,1)S(1)}, bf16[32,768]{1,0:T(8,128)(2,1)S(1)}, u32[]{:S(2)}, u32[]{:S(2)}) collective-permute-start(bf16[32,768]{1,0:T(8,128)(2,1)S(1)} %add.67), channel_id=1, source_target_pairs={{0,3},{1,2},{2,1},{3,0},{4,7},{5,6},{6,5},{7,4},{8,11},{9,10},{10,... | collective-permute-start | bytes 147464 | tf_op jit(solution)/shard_map/ppermute | solution.py:476
  42.7 4.9 %collective-permute-start.16 = (bf16[32,896]{1,0:T(8,128)(2,1)S(1)}, bf16[32,896]{1,0:T(8,128)(2,1)S(1)}, u32[]{:S(2)}, u32[]{:S(2)}) collective-permute-start(bf16[32,896]{1,0:T(8,128)(2,1)S(1)} %add.71), channel_id=1, source_target_pairs={{0,9},{1,8},{2,11},{3,10},{4,13},{5,12},{6,15},{7,14},{8,1},{9,0},... | collective-permute-start | bytes 172040 | tf_op jit(solution)/shard_map/ppermute | solution.py:476
  45.2 3.6 %collective-permute-start.12 = (bf16[32,768]{1,0:T(8,128)(2,1)S(1)}, bf16[32,768]{1,0:T(8,128)(2,1)S(1)}, u32[]{:S(2)}, u32[]{:S(2)}) collective-permute-start(bf16[32,768]{1,0:T(8,128)(2,1)S(1)} %add.68.own_ref), channel_id=1, source_target_pairs={{0,5},{1,4},{2,7},{3,6},{4,1},{5,0},{6,3},{7,2},{8,13},{9,12},{10,... | collective-permute-start | bytes 147464 | tf_op jit(solution)/shard_map/ppermute | solution.py:476
  47.6 1.9 %collective-permute-start.18 = (bf16[32,896]{1,0:T(8,128)(2,1)S(1)}, bf16[32,896]{1,0:T(8,128)(2,1)S(1)}, u32[]{:S(2)}, u32[]{:S(2)}) collective-permute-start(bf16[32,896]{1,0:T(8,128)(2,1)S(1)} %add.72.refs_9_), channel_id=1, source_target_pairs={{0,1},{1,0},{2,3},{3,2},{4,5},{5,4},{6,7},{7,6},{8,9},{9,8},{10,11... | collective-permute-start | bytes 172040 | tf_op jit(solution)/shard_map/ppermute | solution.py:476
  48.8 2.0 %collective-permute-start.17 = (bf16[32,768]{1,0:T(8,128)(2,1)S(1)}, bf16[32,768]{1,0:T(8,128)(2,1)S(1)}, u32[]{:S(2)}, u32[]{:S(2)}) collective-permute-start(bf16[32,768]{1,0:T(8,128)(2,1)S(1)} %add.87.refs_9_), channel_id=1, source_target_pairs={{0,1},{1,0},{2,3},{3,2},{4,5},{5,4},{6,7},{7,6},{8,9},{9,8},{10,11... | collective-permute-start | bytes 147464 | tf_op jit(solution)/shard_map/ppermute | solution.py:476
  52.2 1.9 %collective-permute-start.23 = (bf16[32,896]{1,0:T(8,128)(2,1)S(1)}, bf16[32,896]{1,0:T(8,128)(2,1)S(1)}, u32[]{:S(2)}, u32[]{:S(2)}) collective-permute-start(bf16[32,896]{1,0:T(8,128)(2,1)S(1)} %get-tuple-element.116.send_a), channel_id=1, source_target_pairs={{0,1},{1,0},{2,3},{3,2},{4,5},{5,4},{6,7},{7,6},{8,9},{9,8},{10,11... | collective-permute-start | bytes 172040 | tf_op jit(solution)/shard_map/ppermute | solution.py:476
  53.5 3.5 %collective-permute-start.19 = (bf16[32,768]{1,0:T(8,128)(2,1)S(1)}, bf16[32,768]{1,0:T(8,128)(2,1)S(1)}, u32[]{:S(2)}, u32[]{:S(2)}) collective-permute-start(bf16[32,768]{1,0:T(8,128)(2,1)S(1)} %get-tuple-element.117), channel_id=1, source_target_pairs={{0,1},{1,0},{2,3},{3,2},{4,5},{5,4},{6,7},{7,6},{8,9},{9,8},{10,11... | collective-permute-start | bytes 147464 | tf_op jit(solution)/shard_map/ppermute | solution.py:476
  54.1 4.4 %collective-permute-start.24 = (bf16[32,896]{1,0:T(8,128)(2,1)S(1)}, bf16[32,896]{1,0:T(8,128)(2,1)S(1)}, u32[]{:S(2)}, u32[]{:S(2)}) collective-permute-start(bf16[32,896]{1,0:T(8,128)(2,1)S(1)} %add.76), channel_id=1, source_target_pairs={{0,3},{1,2},{2,1},{3,0},{4,7},{5,6},{6,5},{7,4},{8,11},{9,10},{10,... | collective-permute-start | bytes 172040 | tf_op jit(solution)/shard_map/ppermute | solution.py:476
  57.0 5.9 %collective-permute-start.20 = (bf16[32,768]{1,0:T(8,128)(2,1)S(1)}, bf16[32,768]{1,0:T(8,128)(2,1)S(1)}, u32[]{:S(2)}, u32[]{:S(2)}) collective-permute-start(bf16[32,768]{1,0:T(8,128)(2,1)S(1)} %add.73), channel_id=1, source_target_pairs={{0,9},{1,8},{2,11},{3,10},{4,13},{5,12},{6,15},{7,14},{8,1},{9,0},... | collective-permute-start | bytes 147464 | tf_op jit(solution)/shard_map/ppermute | solution.py:476
  58.5 4.6 %collective-permute-start.25 = (bf16[32,896]{1,0:T(8,128)(2,1)S(1)}, bf16[32,896]{1,0:T(8,128)(2,1)S(1)}, u32[]{:S(2)}, u32[]{:S(2)}) collective-permute-start(bf16[32,896]{1,0:T(8,128)(2,1)S(1)} %add.77), channel_id=1, source_target_pairs={{0,5},{1,4},{2,7},{3,6},{4,1},{5,0},{6,3},{7,2},{8,13},{9,12},{10,... | collective-permute-start | bytes 172040 | tf_op jit(solution)/shard_map/ppermute | solution.py:476
  62.9 3.8 %collective-permute-start.21 = (bf16[32,768]{1,0:T(8,128)(2,1)S(1)}, bf16[32,768]{1,0:T(8,128)(2,1)S(1)}, u32[]{:S(2)}, u32[]{:S(2)}) collective-permute-start(bf16[32,768]{1,0:T(8,128)(2,1)S(1)} %add.74), channel_id=1, source_target_pairs={{0,3},{1,2},{2,1},{3,0},{4,7},{5,6},{6,5},{7,4},{8,11},{9,10},{10,... | collective-permute-start | bytes 147464 | tf_op jit(solution)/shard_map/ppermute | solution.py:476
  63.2 4.8 %collective-permute-start.26 = (bf16[32,896]{1,0:T(8,128)(2,1)S(1)}, bf16[32,896]{1,0:T(8,128)(2,1)S(1)}, u32[]{:S(2)}, u32[]{:S(2)}) collective-permute-start(bf16[32,896]{1,0:T(8,128)(2,1)S(1)} %add.78), channel_id=1, source_target_pairs={{0,9},{1,8},{2,11},{3,10},{4,13},{5,12},{6,15},{7,14},{8,1},{9,0},... | collective-permute-start | bytes 172040 | tf_op jit(solution)/shard_map/ppermute | solution.py:476
  66.7 3.8 %collective-permute-start.22 = (bf16[32,768]{1,0:T(8,128)(2,1)S(1)}, bf16[32,768]{1,0:T(8,128)(2,1)S(1)}, u32[]{:S(2)}, u32[]{:S(2)}) collective-permute-start(bf16[32,768]{1,0:T(8,128)(2,1)S(1)} %add.75.own_ref), channel_id=1, source_target_pairs={{0,5},{1,4},{2,7},{3,6},{4,1},{5,0},{6,3},{7,2},{8,13},{9,12},{10,... | collective-permute-start | bytes 147464 | tf_op jit(solution)/shard_map/ppermute | solution.py:476
  68.0 2.7 %collective-permute-start.28 = (bf16[32,896]{1,0:T(8,128)(2,1)S(1)}, bf16[32,896]{1,0:T(8,128)(2,1)S(1)}, u32[]{:S(2)}, u32[]{:S(2)}) collective-permute-start(bf16[32,896]{1,0:T(8,128)(2,1)S(1)} %add.79.refs_9_), channel_id=1, source_target_pairs={{0,1},{1,0},{2,3},{3,2},{4,5},{5,4},{6,7},{7,6},{8,9},{9,8},{10,11... | collective-permute-start | bytes 172040 | tf_op jit(solution)/shard_map/ppermute | solution.py:476
  70.6 1.6 %collective-permute-start.27 = (bf16[32,768]{1,0:T(8,128)(2,1)S(1)}, bf16[32,768]{1,0:T(8,128)(2,1)S(1)}, u32[]{:S(2)}, u32[]{:S(2)}) collective-permute-start(bf16[32,768]{1,0:T(8,128)(2,1)S(1)} %add.88.refs_9_), channel_id=1, source_target_pairs={{0,1},{1,0},{2,3},{3,2},{4,5},{5,4},{6,7},{7,6},{8,9},{9,8},{10,11... | collective-permute-start | bytes 147464 | tf_op jit(solution)/shard_map/ppermute | solution.py:476
  73.5 1.9 %collective-permute-start.33 = (bf16[32,896]{1,0:T(8,128)(2,1)S(1)}, bf16[32,896]{1,0:T(8,128)(2,1)S(1)}, u32[]{:S(2)}, u32[]{:S(2)}) collective-permute-start(bf16[32,896]{1,0:T(8,128)(2,1)S(1)} %get-tuple-element.133.send_a), channel_id=1, source_target_pairs={{0,1},{1,0},{2,3},{3,2},{4,5},{5,4},{6,7},{7,6},{8,9},{9,8},{10,11... | collective-permute-start | bytes 172040 | tf_op jit(solution)/shard_map/ppermute | solution.py:476
  75.2 2.2 %collective-permute-start.29 = (bf16[32,768]{1,0:T(8,128)(2,1)S(1)}, bf16[32,768]{1,0:T(8,128)(2,1)S(1)}, u32[]{:S(2)}, u32[]{:S(2)}) collective-permute-start(bf16[32,768]{1,0:T(8,128)(2,1)S(1)} %get-tuple-element.134), channel_id=1, source_target_pairs={{0,1},{1,0},{2,3},{3,2},{4,5},{5,4},{6,7},{7,6},{8,9},{9,8},{10,11... | collective-permute-start | bytes 147464 | tf_op jit(solution)/shard_map/ppermute | solution.py:476
  75.4 3.8 %collective-permute-start.34 = (bf16[32,896]{1,0:T(8,128)(2,1)S(1)}, bf16[32,896]{1,0:T(8,128)(2,1)S(1)}, u32[]{:S(2)}, u32[]{:S(2)}) collective-permute-start(bf16[32,896]{1,0:T(8,128)(2,1)S(1)} %add.83), channel_id=1, source_target_pairs={{0,3},{1,2},{2,1},{3,0},{4,7},{5,6},{6,5},{7,4},{8,11},{9,10},{10,... | collective-permute-start | bytes 172040 | tf_op jit(solution)/shard_map/ppermute | solution.py:476
  77.4 5.9 %collective-permute-start.30 = (bf16[32,768]{1,0:T(8,128)(2,1)S(1)}, bf16[32,768]{1,0:T(8,128)(2,1)S(1)}, u32[]{:S(2)}, u32[]{:S(2)}) collective-permute-start(bf16[32,768]{1,0:T(8,128)(2,1)S(1)} %add.80), channel_id=1, source_target_pairs={{0,9},{1,8},{2,11},{3,10},{4,13},{5,12},{6,15},{7,14},{8,1},{9,0},... | collective-permute-start | bytes 147464 | tf_op jit(solution)/shard_map/ppermute | solution.py:476
  79.2 5.1 %collective-permute-start.35 = (bf16[32,896]{1,0:T(8,128)(2,1)S(1)}, bf16[32,896]{1,0:T(8,128)(2,1)S(1)}, u32[]{:S(2)}, u32[]{:S(2)}) collective-permute-start(bf16[32,896]{1,0:T(8,128)(2,1)S(1)} %add.84), channel_id=1, source_target_pairs={{0,5},{1,4},{2,7},{3,6},{4,1},{5,0},{6,3},{7,2},{8,13},{9,12},{10,... | collective-permute-start | bytes 172040 | tf_op jit(solution)/shard_map/ppermute | solution.py:476
  83.4 3.9 %collective-permute-start.31 = (bf16[32,768]{1,0:T(8,128)(2,1)S(1)}, bf16[32,768]{1,0:T(8,128)(2,1)S(1)}, u32[]{:S(2)}, u32[]{:S(2)}) collective-permute-start(bf16[32,768]{1,0:T(8,128)(2,1)S(1)} %add.81), channel_id=1, source_target_pairs={{0,3},{1,2},{2,1},{3,0},{4,7},{5,6},{6,5},{7,4},{8,11},{9,10},{10,... | collective-permute-start | bytes 147464 | tf_op jit(solution)/shard_map/ppermute | solution.py:476
  84.4 6.0 %collective-permute-start.36 = (bf16[32,896]{1,0:T(8,128)(2,1)S(1)}, bf16[32,896]{1,0:T(8,128)(2,1)S(1)}, u32[]{:S(2)}, u32[]{:S(2)}) collective-permute-start(bf16[32,896]{1,0:T(8,128)(2,1)S(1)} %add.85), channel_id=1, source_target_pairs={{0,9},{1,8},{2,11},{3,10},{4,13},{5,12},{6,15},{7,14},{8,1},{9,0},... | collective-permute-start | bytes 172040 | tf_op jit(solution)/shard_map/ppermute | solution.py:476
  87.3 4.1 %collective-permute-start.32 = (bf16[32,768]{1,0:T(8,128)(2,1)S(1)}, bf16[32,768]{1,0:T(8,128)(2,1)S(1)}, u32[]{:S(2)}, u32[]{:S(2)}) collective-permute-start(bf16[32,768]{1,0:T(8,128)(2,1)S(1)} %add.82.own_ref), channel_id=1, source_target_pairs={{0,5},{1,4},{2,7},{3,6},{4,1},{5,0},{6,3},{7,2},{8,13},{9,12},{10,... | collective-permute-start | bytes 147464 | tf_op jit(solution)/shard_map/ppermute | solution.py:476
  90.4 1.5 %collective-permute-start.38 = (bf16[32,896]{1,0:T(8,128)(2,1)S(1)}, bf16[32,896]{1,0:T(8,128)(2,1)S(1)}, u32[]{:S(2)}, u32[]{:S(2)}) collective-permute-start(bf16[32,896]{1,0:T(8,128)(2,1)S(1)} %add.86.refs_9_), channel_id=1, source_target_pairs={{0,1},{1,0},{2,3},{3,2},{4,5},{5,4},{6,7},{7,6},{8,9},{9,8},{10,11... | collective-permute-start | bytes 172040 | tf_op jit(solution)/shard_map/ppermute | solution.py:476
  91.4 1.8 %collective-permute-start.37 = (bf16[32,768]{1,0:T(8,128)(2,1)S(1)}, bf16[32,768]{1,0:T(8,128)(2,1)S(1)}, u32[]{:S(2)}, u32[]{:S(2)}) collective-permute-start(bf16[32,768]{1,0:T(8,128)(2,1)S(1)} %add.89.refs_9_), channel_id=1, source_target_pairs={{0,1},{1,0},{2,3},{3,2},{4,5},{5,4},{6,7},{7,6},{8,9},{9,8},{10,11... | collective-permute-start | bytes 147464 | tf_op jit(solution)/shard_map/ppermute | solution.py:476

commit v4 on v3

--- a/solution.py
+++ b/solution.py
@@ -16,8 +16,8 @@
 FULL = jnp.float32
 
 PIECES = 4
-TURNS = (2, 3, 3)
-ORDERS = ((0, 0), (2, 0), (0, 0), (2, 0))
+TURNS = (0, 4, 4)
+ORDERS = ((0, 0), (2, 0), (1, 0), (2, 0))
 
 VMEM = pl.BlockSpec(memory_space=pltpu.VMEM)
 SMEM = pl.BlockSpec(memory_space=pltpu.SMEM)
@@ -33,7 +33,7 @@
 
 
 def call(kernel, name, us, operands, out_shape, scratch=(), smem=(), smem_out=(), limit=12):
-    return pl.pallas_call(
+    outs = pl.pallas_call(
         kernel,
         out_shape=tuple(out_shape),
         in_specs=[SMEM if j in smem else VMEM for j in range(len(operands))],
@@ -43,6 +43,7 @@
         cost_estimate=pl.CostEstimate(flops=0, bytes_accessed=int(us * 3.69e6), transcendentals=0),
         name=name,
     )(*operands)
+    return list(outs)
 
 
 def total(x):
@@ -265,41 +266,43 @@
     return jnp.dot(half, turned_ref[k % turned_refs[0].shape[0], rows, :], preferred_element_type=FULL)
 
 
-def flow_kernel(step_size, piece, devices, turns, first, *refs):
+def flow_kernel(step_size, pieces, devices, turns, first, *refs):
     refs = list(refs)
     turned_refs = [refs.pop(0) for _ in range(turns)]
-    place_ref = refs.pop(0)
-    message_ref, unit_ref = refs[:2]
+    place_ref, unit_ref = refs[:2]
     del refs[:2]
-    level_ref = None if first else refs.pop(0)
-    stat_ref = None if first and piece == 0 else refs.pop(0)
-    flow_ref = refs.pop(0) if piece else None
-    moved_ref, flow_out = refs[:2]
-    del refs[:2]
-    all_hours, quarter = moved_ref.shape
-    if first:
-        level_out = refs.pop(0)
-        levels = starting_levels(piece, devices, place_ref[0], message_ref, all_hours, quarter)
-        level_out[...] = levels
-    else:
-        levels = level_ref[...]
-    if piece == 0:
+    leading = pieces[0] == 0
+    stat_ref = None if first and leading else refs.pop(0)
+    flow_ref = None if leading else refs.pop(0)
+    message_refs = [refs.pop(0) for _ in pieces]
+    level_refs = [refs.pop(0) for _ in pieces]
+    moved_refs = [refs.pop(0) for _ in pieces]
+    flow_out = refs.pop(0)
+    all_hours, quarter = moved_refs[0].shape
+    if leading:
         stat_out = refs.pop(0)
         if first:
             stat_out[...] = jnp.full(stat_out.shape, 1.0, FULL)
         else:
-            dual_sq = total(message_ref[:all_hours, quarter:].astype(FULL))
+            dual_sq = total(message_refs[0][:all_hours, quarter:].astype(FULL))
             primal_sq = stat_ref[1:2, 0:1]
             ratio = (dual_sq + 1e-06) / (primal_sq + 1e-06)
             weight = jnp.sqrt(stat_ref[0:1, 0:1]) * jnp.sqrt(jnp.sqrt(ratio))
             stat_out[...] = jnp.broadcast_to(weight, stat_out.shape)
         stat_ref = stat_out
-    half = primal_piece(piece, step_size, stat_ref, message_ref, levels, unit_ref, moved_ref)
+    halves = []
+    for piece, message_ref, level_ref, moved_ref in zip(pieces, message_refs, level_refs, moved_refs):
+        if first:
+            level_ref[...] = starting_levels(piece, devices, place_ref[0], message_ref, all_hours, quarter)
+        halves.append(primal_piece(piece, step_size, stat_ref, message_ref, level_ref[...], unit_ref, moved_ref))
     lines = turned_refs[0].shape[2]
     for k in range(turns * turned_refs[0].shape[0]):
         at = pl.ds(k * lines, lines)
-        part = piece_flows(piece, half, turned_refs, k)
-        flow_out[:, at] = part if flow_ref is None else flow_ref[:, at] + part
+        part = None if flow_ref is None else flow_ref[:, at]
+        for piece, half in zip(pieces, halves):
+            flows = piece_flows(piece, half, turned_refs, k)
+            part = flows if part is None else part + flows
+        flow_out[:, at] = part
 
 
 def dual_kernel(step_size, balance, devices, turns, first, last, *refs):
@@ -447,8 +450,7 @@
 def split_kernel(all_hours, own_ref, received_ref, a_ref, b_ref, scratch_ref):
     join_kernel(all_hours, own_ref, received_ref, None, scratch_ref)
     quarter = b_ref.shape[1]
-    a_ref[:, :quarter] = scratch_ref[:, :quarter].astype(HALF)
-    a_ref[:, quarter:] = jnp.zeros((a_ref.shape[0], a_ref.shape[1] - quarter), HALF)
+    a_ref[...] = scratch_ref[:, :quarter].astype(HALF)
     b_ref[...] = scratch_ref[:, quarter:].astype(HALF)
 
 
@@ -459,7 +461,7 @@
         "split",
         0.3,
         [own, received],
-        [near(rows, quarter + LANES, dtype=HALF), near(rows, quarter, dtype=HALF)],
+        [near(rows, quarter, dtype=HALF)] * 2,
         [near(rows, 2 * quarter)],
     )
 
@@ -543,7 +545,7 @@
         steps = len(orders[0])
         for step in range(steps):
             before = []
-            if first and step == steps - 1:
+            if first and step == steps - 2:
                 operands = [start_flow_dual, base_flow, monitored, table, row(unit_floor), row(unit_span)]
                 operands += [row(ramp_limit), row(ramp_mask), unit_cost, start_ramp_dual]
                 dual, base, rating, unit, cost, ramp = call(
@@ -579,26 +581,27 @@
         messages = [owns[0], exchange(owns[0], 1)]
         moved, flows = [], None
         levels = [] if first else levels
-        for piece in range(3):
-            if piece == 2:
+        for pieces in ((0,), (1, 2)):
+            if 2 in pieces:
                 if not first:
-                    owns[1] = add_after(owns[1], exchange(owns[1], orders[1][-1]), after)
+                    owns[1] = add_after(owns[1], exchange(owns[1], orders[1][-1]), stat)
                 messages += [owns[1], exchange(owns[1], 1)]
-            operands = [*turned, here, messages[piece], unit]
-            operands += [] if first else [levels[piece]]
-            operands += [] if first and piece == 0 else [stat]
-            operands += [flows] if piece else []
-            out_shape = [near(all_hours, quarter), near(all_hours, ctgs * lines)]
-            out_shape += [near(all_hours, quarter)] if first else []
-            out_shape += [] if piece else [near(8, LANES)]
-            kernel = functools.partial(flow_kernel, step_size, piece, devices, len(turned), first)
-            outs = call(kernel, "flow", 0.7, operands, out_shape, smem=(len(turned),))
-            moved.append(outs[0])
-            flows = outs[1]
+            operands = [*turned, here, unit]
+            operands += [] if first and flows is None else [stat]
+            operands += [] if flows is None else [flows]
+            operands += [messages[piece] for piece in pieces]
+            operands += [] if first else [levels[piece] for piece in pieces]
+            out_shape = [near(all_hours, quarter)] * (len(pieces) * (2 if first else 1))
+            out_shape += [near(all_hours, ctgs * lines)]
+            out_shape += [near(8, LANES)] if flows is None else []
+            kernel = functools.partial(flow_kernel, step_size, pieces, devices, len(turned), first)
+            outs = call(kernel, "flow", 0.7 * len(pieces), operands, out_shape, smem=(len(turned),))
+            if flows is None:
+                stat = outs.pop()
+            flows = outs.pop()
             if first:
-                levels.append(outs[2])
-            if piece == 0:
-                stat = after = outs[-1]
+                levels += outs[: len(pieces)]
+            moved += outs[-len(pieces) :]
         operands = [*turned, here, masked, messages[3], *levels, *moved, stat, flows, dual, base, rating, unit, cost]
         operands += [demands, ramp] if first else [demands, ramp, price]
         kernel = functools.partial(dual_kernel, step_size, balance, devices, len(turned), first, last)
@@ -606,7 +609,7 @@
         if last:
             f32 = lambda *shape: jax.ShapeDtypeStruct(shape, FULL)
             out_shape = [f32(hours, units), f32(all_hours, ctgs, lines), f32(hours, units), f32(hours)]
-            return call(kernel, "dual", 1.2, operands, out_shape, [near(all_hours, quarter)], smem, (3,))
+            return tuple(call(kernel, "dual", 1.2, operands, out_shape, [near(all_hours, quarter)], smem, (3,)))
         out_shape = [near(all_hours, quarter), near(all_hours, ctgs * lines), near(hours, units), near(hours, 1)]
         out_shape += [near(8, LANES), message_a, near(all_hours, ctgs * lines, dtype=HALF), near(8, units)]
         scratch = [near(all_hours, quarter)] if first else []

time: 95.1 us -> 92.9 us (0.977)
  starting transfers between devices: 41.7 us -> 35 us
  waiting for transfers between devices: 19.6 us -> 24.6 us
    ppermute x39, starting transfers between devices: 41.7 us -> 35 us  [exchange(): lax.ppermute(x, 'ctg', [(i, i ^ mask ^ flip) for i in range(devices)])]
    ppermute x39, waiting for transfers between devices: 19.6 us -> 24.6 us  [exchange(): lax.ppermute(x, 'ctg', [(i, i ^ mask ^ flip) for i in range(devices)])]
    pallas_call x41 -> x37, Pallas kernels: 26 us -> 25.4 us  [call(): pl.pallas_call(kernel, out_shape=tuple(out_shape), in_specs=[SMEM if j in...]
  transfers between devices with their start and end apart: 39 -> 39, of which waited for: 19 -> 16; matrix products, arithmetic and copies ran while one was open for 0% -> 0% of each run, Pallas kernels for 21% -> 21%
where the time goes in v4:
time: 92.9 us; the launch traced here: 92.7 us
  starting transfers between devices  35 us (38%)
  Pallas kernels  31.5 us (34%)
  waiting for transfers between devices  24.6 us (26%)
  between operations  1.26 us (1%)
    ppermute x39, starting transfers between devices, exchange(): lax.ppermute(x, 'ctg', [(i, i ^ mask ^ flip) for i in range(devices)])  35 us
    pallas_call x37, Pallas kernels, call(): pl.pallas_call(kernel, out_shape=tuple(out_shape), in_specs=[SMEM if j in...  25.4 us
    ppermute x39, waiting for transfers between devices, exchange(): lax.ppermute(x, 'ctg', [(i, i ^ mask ^ flip) for i in range(devices)])  24.6 us
    pallas_call x1, Pallas kernels, body(): pl.pallas_call(start_kernel, out_shape=(near(ctgs, lines, units, dtype=HA...  6.08 us
  transfers between devices with their start and end apart: 39, of which 16 were waited for; matrix products, arithmetic and copies ran while one was open for 0% of the time, Pallas kernels for 21%

profile of v4, /device:TPU:0, one launch (start us, length us, event | category | flops | bytes accessed | tf_op | source)
XLA Modules:
  0.0 92.7 jit_solution(2039853988542033875)
XLA Ops:
  0.6 6.1 %start.1 = (bf16[8,256,3072]{2,1,0:T(8,128)(2,1)S(1)}, bf16[36,1536]{1,0:T(8,128)(2,1)S(1)}, bf16[36,1536]{1,0:T(8,128)(2,1)S(1)}) custom-call(s32[1]{0:T(128)} %bitcast.place_ref.refs_8_, s32[8,2,24]{2,1,0:T(2,128)} %gate_hbm.1, bf16[8,256,3072]{2,1,0:T(8,128)(2,1)} %tiles_ref.1, f32[32,8,256]{2,1,0:T(8,128)} %dual_ref.3, s32[1,3072]{1,0:T(1,128)} %bitcast.12, ...), custom_call_target="tpu_custom_call" | custom-call | tf_op jit(solution)/shard_map/start/pallas_call | solution.py:520
  6.7 0.5 collective-permute-start
  7.2 1.0 %collective-permute-done.received_ref = bf16[36,1536]{1,0:T(8,128)(2,1)S(1)} collective-permute-done((bf16[36,1536]{1,0:T(8,128)(2,1)S(1)}, bf16[36,1536]{1,0:T(8,128)(2,1)S(1)}, u32[]{:S(2)}, u32[]{:S(2)}) %collective-permute-start) | collective-permute-done | bytes 110624 | tf_op jit(solution)/shard_map/ppermute | solution.py:478
  8.3 2.8 %collective-permute-start.1 = (bf16[40,768]{1,0:T(8,128)(2,1)S(1)}, bf16[40,768]{1,0:T(8,128)(2,1)S(1)}, u32[]{:S(2)}, u32[]{:S(2)}) collective-permute-start(bf16[40,768]{1,0:T(8,128)(2,1)S(1)} %get-tuple-element.75.own_ref), channel_id=1, source_target_pairs={{0,5},{1,4},{2,7},{3,6},{4,1},{5,0},{6,3},{7,2},{8,13},{9,12},{10,... | collective-permute-start | bytes 184328 | tf_op jit(solution)/shard_map/ppermute | solution.py:478
  11.0 2.6 %collective-permute-start.3 = (bf16[40,768]{1,0:T(8,128)(2,1)S(1)}, bf16[40,768]{1,0:T(8,128)(2,1)S(1)}, u32[]{:S(2)}, u32[]{:S(2)}) collective-permute-start(bf16[40,768]{1,0:T(8,128)(2,1)S(1)} %get-tuple-element.77.own_ref), channel_id=1, source_target_pairs={{0,9},{1,8},{2,11},{3,10},{4,13},{5,12},{6,15},{7,14},{8,1},{9,0},... | collective-permute-start | bytes 184328 | tf_op jit(solution)/shard_map/ppermute | solution.py:478
  13.6 2.8 %collective-permute-start.2 = (bf16[48,768]{1,0:T(8,128)(2,1)S(1)}, bf16[48,768]{1,0:T(8,128)(2,1)S(1)}, u32[]{:S(2)}, u32[]{:S(2)}) collective-permute-start(bf16[48,768]{1,0:T(8,128)(2,1)S(1)} %join.6.before_ref.own_ref), channel_id=1, source_target_pairs={{0,9},{1,8},{2,11},{3,10},{4,13},{5,12},{6,15},{7,14},{8,1},{9,0},... | collective-permute-start | bytes 221192 | tf_op jit(solution)/shard_map/ppermute | solution.py:478
  16.4 2.1 %collective-permute-start.4 = (bf16[48,768]{1,0:T(8,128)(2,1)S(1)}, bf16[48,768]{1,0:T(8,128)(2,1)S(1)}, u32[]{:S(2)}, u32[]{:S(2)}) collective-permute-start(bf16[48,768]{1,0:T(8,128)(2,1)S(1)} %join.8.own_ref), channel_id=1, source_target_pairs={{0,3},{1,2},{2,1},{3,0},{4,7},{5,6},{6,5},{7,4},{8,11},{9,10},{10,... | collective-permute-start | bytes 221192 | tf_op jit(solution)/shard_map/ppermute | solution.py:478
  19.0 0.5 turn.10.refs_3_.refs_2_
  19.5 0.5 turn.9.refs_2_.refs_1_
  20.0 0.5 turn.8.refs_1_.refs_0_
  20.4 1.9 %prepare.1 = (f32[32,2048]{1,0:T(8,128)S(1)}, f32[32,2048]{1,0:T(8,128)S(1)}, f32[1,2048]{1,0:T(1,128)S(1)}, f32[4,3072]{1,0:T(4,128)S(1)}, f32[2,3072]{1,0:T(2,128)S(1)}, /*index=5*/f32[2,3072]{1,0:T(2,128)S(1)}) custom-call(s32[1]{0:T(128)} %bitcast.place_ref.refs_8_, bf16[48,768]{1,0:T(8,128)(2,1)S(1)} %join.6.before_ref.own_ref, f32[32,8,256]{2,1,0:T(8,128)} %dual_ref.3, ...), custom_call_target="tpu_custom_call" | custom-call | bytes 5535000 | tf_op jit(solution)/shard_map/prepare/pallas_call | solution.py:36
  22.5 1.5 %collective-permute-start.5 = (bf16[64,768]{1,0:T(8,128)(2,1)S(1)}, bf16[64,768]{1,0:T(8,128)(2,1)S(1)}, u32[]{:S(2)}, u32[]{:S(2)}) collective-permute-start(bf16[64,768]{1,0:T(8,128)(2,1)S(1)} %join.9.own_ref), channel_id=1, source_target_pairs={{0,5},{1,4},{2,7},{3,6},{4,1},{5,0},{6,3},{7,2},{8,13},{9,12},{10,... | collective-permute-start | bytes 294920 | tf_op jit(solution)/shard_map/ppermute | solution.py:478
  24.5 0.5 turn.14.refs_6_
  25.0 0.5 turn.13.refs_5_
  25.4 0.5 turn.12.refs_4_
  25.9 1.4 %collective-permute-done.7.received_ref = bf16[64,768]{1,0:T(8,128)(2,1)S(1)} collective-permute-done((bf16[64,768]{1,0:T(8,128)(2,1)S(1)}, bf16[64,768]{1,0:T(8,128)(2,1)S(1)}, u32[]{:S(2)}, u32[]{:S(2)}) %collective-permute-start.7) | collective-permute-done | bytes 98336 | tf_op jit(solution)/shard_map/ppermute | solution.py:478
  27.4 0.6 collective-permute-start.6
  28.0 0.8 flow.8
  28.8 1.4 %flow.9 = (f32[32,768]{1,0:T(8,128)S(1)}, f32[32,768]{1,0:T(8,128)S(1)}, f32[32,768]{1,0:T(8,128)S(1)}, f32[32,768]{1,0:T(8,128)S(1)}, f32[32,2048]{1,0:T(8,128)S(1)}) custom-call(bf16[1,3072,256]{2,1,0:T(8,128)(2,1)S(1)} %turn.8.refs_1_.refs_0_, bf16[1,3072,256]{2,1,0:T(8,128)(2,1)S(1)} %turn.9.refs_2_.refs_1_, ...), custom_call_target="tpu_custom_call" | custom-call | bytes 5166000 | tf_op jit(solution)/shard_map/flow/pallas_call | solution.py:36
  30.2 1.5 %dual.4 = (f32[32,768]{1,0:T(8,128)S(1)}, f32[32,2048]{1,0:T(8,128)S(1)}, f32[2,3072]{1,0:T(2,128)S(1)}, f32[2,1]{1,0:T(2,128)S(1)}, f32[8,128]{1,0:T(8,128)S(1)...) custom-call(bf16[1,3072,256]{2,1,0:T(8,128)(2,1)S(1)} %turn.8.refs_1_.refs_0_, ...), custom_call_target="tpu_custom_call" | custom-call | bytes 5535000 | tf_op jit(solution)/shard_map/dual/pallas_call | solution.py:36
  31.9 1.2 %pull.7 = (bf16[32,896]{1,0:T(8,128)(2,1)S(1)}, bf16[32,768]{1,0:T(8,128)(2,1)S(1)}) custom-call(s32[1]{0:T(128)} %bitcast.place_ref.refs_8_, bf16[8,256,3072]{2,1,0:T(8,128)(2,1)S(1)} %get-tuple-element.72.masked_ref.refs_9_, bf16[32,2048]{1,0:T(8,128)(2,1)S(1)} %get-tuple-element.92.half_dual, f32[8,3072]{1,0:T(8,128)S(1)} %get-tuple-element.93.term_ref, ...), custom_call_target="tpu_custom_call" | custom-call | bytes 4428000 | tf_op jit(solution)/shard_map/pull/pallas_call | solution.py:36
  33.1 0.5 collective-permute-start.9
  33.6 0.5 collective-permute-start.14
  34.1 0.7 pull.6
  34.8 2.1 %collective-permute-start.10 = (bf16[32,768]{1,0:T(8,128)(2,1)S(1)}, bf16[32,768]{1,0:T(8,128)(2,1)S(1)}, u32[]{:S(2)}, u32[]{:S(2)}) collective-permute-start(bf16[32,768]{1,0:T(8,128)(2,1)S(1)} %add.66), channel_id=1, source_target_pairs={{0,9},{1,8},{2,11},{3,10},{4,13},{5,12},{6,15},{7,14},{8,1},{9,0},... | collective-permute-start | bytes 147464 | tf_op jit(solution)/shard_map/ppermute | solution.py:478
  37.0 0.6 collective-permute-done.14
  37.6 1.6 %collective-permute-start.15 = (bf16[32,896]{1,0:T(8,128)(2,1)S(1)}, bf16[32,896]{1,0:T(8,128)(2,1)S(1)}, u32[]{:S(2)}, u32[]{:S(2)}) collective-permute-start(bf16[32,896]{1,0:T(8,128)(2,1)S(1)} %add.70), channel_id=1, source_target_pairs={{0,5},{1,4},{2,7},{3,6},{4,1},{5,0},{6,3},{7,2},{8,13},{9,12},{10,... | collective-permute-start | bytes 172040 | tf_op jit(solution)/shard_map/ppermute | solution.py:478
  39.3 1.4 %collective-permute-start.11 = (bf16[32,768]{1,0:T(8,128)(2,1)S(1)}, bf16[32,768]{1,0:T(8,128)(2,1)S(1)}, u32[]{:S(2)}, u32[]{:S(2)}) collective-permute-start(bf16[32,768]{1,0:T(8,128)(2,1)S(1)} %add.67), channel_id=1, source_target_pairs={{0,3},{1,2},{2,1},{3,0},{4,7},{5,6},{6,5},{7,4},{8,11},{9,10},{10,... | collective-permute-start | bytes 147464 | tf_op jit(solution)/shard_map/ppermute | solution.py:478
  40.7 0.9 collective-permute-done.15
  41.6 1.4 %collective-permute-start.16 = (bf16[32,896]{1,0:T(8,128)(2,1)S(1)}, bf16[32,896]{1,0:T(8,128)(2,1)S(1)}, u32[]{:S(2)}, u32[]{:S(2)}) collective-permute-start(bf16[32,896]{1,0:T(8,128)(2,1)S(1)} %add.71), channel_id=1, source_target_pairs={{0,9},{1,8},{2,11},{3,10},{4,13},{5,12},{6,15},{7,14},{8,1},{9,0},... | collective-permute-start | bytes 172040 | tf_op jit(solution)/shard_map/ppermute | solution.py:478
  43.1 2.6 %collective-permute-start.12 = (bf16[32,768]{1,0:T(8,128)(2,1)S(1)}, bf16[32,768]{1,0:T(8,128)(2,1)S(1)}, u32[]{:S(2)}, u32[]{:S(2)}) collective-permute-start(bf16[32,768]{1,0:T(8,128)(2,1)S(1)} %add.68.own_ref), channel_id=1, source_target_pairs={{0,5},{1,4},{2,7},{3,6},{4,1},{5,0},{6,3},{7,2},{8,13},{9,12},{10,... | collective-permute-start | bytes 147464 | tf_op jit(solution)/shard_map/ppermute | solution.py:478
  45.6 0.8 collective-permute-done.16
  46.5 1.5 %collective-permute-start.18 = (bf16[32,896]{1,0:T(8,128)(2,1)S(1)}, bf16[32,896]{1,0:T(8,128)(2,1)S(1)}, u32[]{:S(2)}, u32[]{:S(2)}) collective-permute-start(bf16[32,896]{1,0:T(8,128)(2,1)S(1)} %add.72.refs_11_), channel_id=1, source_target_pairs={{0,1},{1,0},{2,3},{3,2},{4,5},{5,4},{6,7},{7,6},{8,9},{9,8},{10,11... | collective-permute-start | bytes 172040 | tf_op jit(solution)/shard_map/ppermute | solution.py:478
  48.0 1.0 %flow.10 = (f32[32,768]{1,0:T(8,128)S(1)}, f32[32,2048]{1,0:T(8,128)S(1)}, f32[8,128]{1,0:T(8,128)S(1)}) custom-call(bf16[1,3072,256]{2,1,0:T(8,128)(2,1)S(1)} %turn.8.refs_1_.refs_0_, bf16[1,3072,256]{2,1,0:T(8,128)(2,1)S(1)} %turn.9.refs_2_.refs_1_, bf16[1,3072,256]{2,1,0:T(8,128)(2,1)S(1)} %turn.10.refs_3_.refs_2_, ...), custom_call_target="tpu_custom_call" | custom-call | bytes 2583000 | tf_op jit(solution)/shard_map/flow/pallas_call | solution.py:36
  49.1 1.2 %flow.11 = (f32[32,768]{1,0:T(8,128)S(1)}, f32[32,768]{1,0:T(8,128)S(1)}, f32[32,2048]{1,0:T(8,128)S(1)}) custom-call(bf16[1,3072,256]{2,1,0:T(8,128)(2,1)S(1)} %turn.8.refs_1_.refs_0_, bf16[1,3072,256]{2,1,0:T(8,128)(2,1)S(1)} %turn.9.refs_2_.refs_1_, bf16[1,3072,256]{2,1,0:T(8,128)(2,1)S(1)} %turn.10.refs_3_.refs_2_, ...), custom_call_target="tpu_custom_call" | custom-call | bytes 5166000 | tf_op jit(solution)/shard_map/flow/pallas_call | solution.py:36
  50.4 1.3 %dual.5 = (f32[32,768]{1,0:T(8,128)S(1)}, f32[32,2048]{1,0:T(8,128)S(1)}, f32[2,3072]{1,0:T(2,128)S(1)}, f32[2,1]{1,0:T(2,128)S(1)}, f32[8,128]{1,0:T(8,128)S(1)...) custom-call(bf16[1,3072,256]{2,1,0:T(8,128)(2,1)S(1)} %turn.8.refs_1_.refs_0_, ...), custom_call_target="tpu_custom_call" | custom-call | bytes 5535000 | tf_op jit(solution)/shard_map/dual/pallas_call | solution.py:36
  51.7 0.6 collective-permute-start.23
  52.2 1.2 %pull.9 = (bf16[32,896]{1,0:T(8,128)(2,1)S(1)}, bf16[32,768]{1,0:T(8,128)(2,1)S(1)}) custom-call(s32[1]{0:T(128)} %bitcast.place_ref.refs_8_, bf16[8,256,3072]{2,1,0:T(8,128)(2,1)S(1)} %get-tuple-element.72.masked_ref.refs_9_, bf16[32,2048]{1,0:T(8,128)(2,1)S(1)} %get-tuple-element.108.half_dual, f32[8,3072]{1,0:T(8,128)S(1)} %get-tuple-element.109.term_ref, ...), custom_call_target="tpu_custom_call" | custom-call | bytes 4428000 | tf_op jit(solution)/shard_map/pull/pallas_call | solution.py:36
  53.6 1.1 %collective-permute-start.24 = (bf16[32,896]{1,0:T(8,128)(2,1)S(1)}, bf16[32,896]{1,0:T(8,128)(2,1)S(1)}, u32[]{:S(2)}, u32[]{:S(2)}) collective-permute-start(bf16[32,896]{1,0:T(8,128)(2,1)S(1)} %add.76), channel_id=1, source_target_pairs={{0,3},{1,2},{2,1},{3,0},{4,7},{5,6},{6,5},{7,4},{8,11},{9,10},{10,... | collective-permute-start | bytes 172040 | tf_op jit(solution)/shard_map/ppermute | solution.py:478
  54.7 0.6 pull.8
  55.3 1.0 %collective-permute-start.20 = (bf16[32,768]{1,0:T(8,128)(2,1)S(1)}, bf16[32,768]{1,0:T(8,128)(2,1)S(1)}, u32[]{:S(2)}, u32[]{:S(2)}) collective-permute-start(bf16[32,768]{1,0:T(8,128)(2,1)S(1)} %add.73), channel_id=1, source_target_pairs={{0,9},{1,8},{2,11},{3,10},{4,13},{5,12},{6,15},{7,14},{8,1},{9,0},... | collective-permute-start | bytes 147464 | tf_op jit(solution)/shard_map/ppermute | solution.py:478
  56.4 0.9 collective-permute-done.24
  57.3 1.3 %collective-permute-start.25 = (bf16[32,896]{1,0:T(8,128)(2,1)S(1)}, bf16[32,896]{1,0:T(8,128)(2,1)S(1)}, u32[]{:S(2)}, u32[]{:S(2)}) collective-permute-start(bf16[32,896]{1,0:T(8,128)(2,1)S(1)} %add.77), channel_id=1, source_target_pairs={{0,5},{1,4},{2,7},{3,6},{4,1},{5,0},{6,3},{7,2},{8,13},{9,12},{10,... | collective-permute-start | bytes 172040 | tf_op jit(solution)/shard_map/ppermute | solution.py:478
  58.6 2.7 %collective-permute-done.20 = bf16[32,768]{1,0:T(8,128)(2,1)S(1)} collective-permute-done((bf16[32,768]{1,0:T(8,128)(2,1)S(1)}, bf16[32,768]{1,0:T(8,128)(2,1)S(1)}, u32[]{:S(2)}, u32[]{:S(2)}) %collective-permute-start.20) | collective-permute-done | bytes 49184 | tf_op jit(solution)/shard_map/ppermute | solution.py:478
  61.3 0.8 collective-permute-start.21
  62.2 1.0 %collective-permute-start.26 = (bf16[32,896]{1,0:T(8,128)(2,1)S(1)}, bf16[32,896]{1,0:T(8,128)(2,1)S(1)}, u32[]{:S(2)}, u32[]{:S(2)}) collective-permute-start(bf16[32,896]{1,0:T(8,128)(2,1)S(1)} %add.78), channel_id=1, source_target_pairs={{0,9},{1,8},{2,11},{3,10},{4,13},{5,12},{6,15},{7,14},{8,1},{9,0},... | collective-permute-start | bytes 172040 | tf_op jit(solution)/shard_map/ppermute | solution.py:478
  63.2 2.1 %collective-permute-done.21 = bf16[32,768]{1,0:T(8,128)(2,1)S(1)} collective-permute-done((bf16[32,768]{1,0:T(8,128)(2,1)S(1)}, bf16[32,768]{1,0:T(8,128)(2,1)S(1)}, u32[]{:S(2)}, u32[]{:S(2)}) %collective-permute-start.21) | collective-permute-done | bytes 49184 | tf_op jit(solution)/shard_map/ppermute | solution.py:478
  65.3 3.1 %collective-permute-done.26 = bf16[32,896]{1,0:T(8,128)(2,1)S(1)} collective-permute-done((bf16[32,896]{1,0:T(8,128)(2,1)S(1)}, bf16[32,896]{1,0:T(8,128)(2,1)S(1)}, u32[]{:S(2)}, u32[]{:S(2)}) %collective-permute-start.26) | collective-permute-done | bytes 57376 | tf_op jit(solution)/shard_map/ppermute | solution.py:478
  68.6 0.8 flow.12
  69.9 1.2 %flow.13 = (f32[32,768]{1,0:T(8,128)S(1)}, f32[32,768]{1,0:T(8,128)S(1)}, f32[32,2048]{1,0:T(8,128)S(1)}) custom-call(bf16[1,3072,256]{2,1,0:T(8,128)(2,1)S(1)} %turn.8.refs_1_.refs_0_, bf16[1,3072,256]{2,1,0:T(8,128)(2,1)S(1)} %turn.9.refs_2_.refs_1_, bf16[1,3072,256]{2,1,0:T(8,128)(2,1)S(1)} %turn.10.refs_3_.refs_2_, ...), custom_call_target="tpu_custom_call" | custom-call | bytes 5166000 | tf_op jit(solution)/shard_map/flow/pallas_call | solution.py:36
  71.2 1.3 %dual.6 = (f32[32,768]{1,0:T(8,128)S(1)}, f32[32,2048]{1,0:T(8,128)S(1)}, f32[2,3072]{1,0:T(2,128)S(1)}, f32[2,1]{1,0:T(2,128)S(1)}, f32[8,128]{1,0:T(8,128)S(1)...) custom-call(bf16[1,3072,256]{2,1,0:T(8,128)(2,1)S(1)} %turn.8.refs_1_.refs_0_, ...), custom_call_target="tpu_custom_call" | custom-call | bytes 5535000 | tf_op jit(solution)/shard_map/dual/pallas_call | solution.py:36
  72.8 1.2 %pull.11 = (bf16[32,896]{1,0:T(8,128)(2,1)S(1)}, bf16[32,768]{1,0:T(8,128)(2,1)S(1)}) custom-call(s32[1]{0:T(128)} %bitcast.place_ref.refs_8_, bf16[8,256,3072]{2,1,0:T(8,128)(2,1)S(1)} %get-tuple-element.72.masked_ref.refs_9_, bf16[32,2048]{1,0:T(8,128)(2,1)S(1)} %get-tuple-element.124.half_dual, f32[8,3072]{1,0:T(8,128)S(1)} %get-tuple-element.125.term_ref, ...), custom_call_target="tpu_custom_call" | custom-call | bytes 4428000 | tf_op jit(solution)/shard_map/pull/pallas_call | solution.py:36
  74.4 0.7 collective-permute-start.34
  75.0 0.6 pull.10
  75.8 2.5 %collective-permute-done.34 = bf16[32,896]{1,0:T(8,128)(2,1)S(1)} collective-permute-done((bf16[32,896]{1,0:T(8,128)(2,1)S(1)}, bf16[32,896]{1,0:T(8,128)(2,1)S(1)}, u32[]{:S(2)}, u32[]{:S(2)}) %collective-permute-start.34) | collective-permute-done | bytes 57376 | tf_op jit(solution)/shard_map/ppermute | solution.py:478
  78.4 2.8 %collective-permute-done.30 = bf16[32,768]{1,0:T(8,128)(2,1)S(1)} collective-permute-done((bf16[32,768]{1,0:T(8,128)(2,1)S(1)}, bf16[32,768]{1,0:T(8,128)(2,1)S(1)}, u32[]{:S(2)}, u32[]{:S(2)}) %collective-permute-start.30) | collective-permute-done | bytes 49184 | tf_op jit(solution)/shard_map/ppermute | solution.py:478
  81.3 0.9 collective-permute-start.31
  82.3 0.6 collective-permute-start.36
  82.9 2.2 %collective-permute-done.31 = bf16[32,768]{1,0:T(8,128)(2,1)S(1)} collective-permute-done((bf16[32,768]{1,0:T(8,128)(2,1)S(1)}, bf16[32,768]{1,0:T(8,128)(2,1)S(1)}, u32[]{:S(2)}, u32[]{:S(2)}) %collective-permute-start.31) | collective-permute-done | bytes 49184 | tf_op jit(solution)/shard_map/ppermute | solution.py:478
  85.2 3.1 %collective-permute-done.36 = bf16[32,896]{1,0:T(8,128)(2,1)S(1)} collective-permute-done((bf16[32,896]{1,0:T(8,128)(2,1)S(1)}, bf16[32,896]{1,0:T(8,128)(2,1)S(1)}, u32[]{:S(2)}, u32[]{:S(2)}) %collective-permute-start.36) | collective-permute-done | bytes 57376 | tf_op jit(solution)/shard_map/ppermute | solution.py:478
  88.5 0.8 flow.14
  89.4 0.5 collective-permute-start.37
  89.8 1.2 %flow.15 = (f32[32,768]{1,0:T(8,128)S(1)}, f32[32,768]{1,0:T(8,128)S(1)}, f32[32,2048]{1,0:T(8,128)S(1)}) custom-call(bf16[1,3072,256]{2,1,0:T(8,128)(2,1)S(1)} %turn.8.refs_1_.refs_0_, bf16[1,3072,256]{2,1,0:T(8,128)(2,1)S(1)} %turn.9.refs_2_.refs_1_, bf16[1,3072,256]{2,1,0:T(8,128)(2,1)S(1)} %turn.10.refs_3_.refs_2_, ...), custom_call_target="tpu_custom_call" | custom-call | bytes 5166000 | tf_op jit(solution)/shard_map/flow/pallas_call | solution.py:36
  91.1 1.5 %dual.7 = (f32[2,3072]{1,0:T(2,128)}, f32[32,8,256]{2,1,0:T(8,128)}, f32[2,3072]{1,0:T(2,128)}, f32[2]{0:T(128)}) custom-call(bf16[1,3072,256]{2,1,0:T(8,128)(2,1)S(1)} %turn.8.refs_1_.refs_0_, bf16[1,3072,256]{2,1,0:T(8,128)(2,1)S(1)} %turn.9.refs_2_.refs_1_, bf16[1,3072,256]{2,1,0:T(8,128)(2,1)S(1)} %turn.10.refs_3_.refs_2_, ...), custom_call_target="tpu_custom_call" | custom-call | bytes 4428000 | tf_op jit(solution)/shard_map/dual/pallas_call | solution.py:36
  (75 shorter events, 4.0 us)
Async XLA Ops:
  6.7 1.5 %collective-permute-start = (bf16[36,1536]{1,0:T(8,128)(2,1)S(1)}, bf16[36,1536]{1,0:T(8,128)(2,1)S(1)}, u32[]{:S(2)}, u32[]{:S(2)}) collective-permute-start(bf16[36,1536]{1,0:T(8,128)(2,1)S(1)} %get-tuple-element.74), channel_id=1, source_target_pairs={{0,1},{1,0},{2,3},{3,2},{4,5},{5,4},{6,7},{7,6},{8,9},{9,8},{10,11... | collective-permute-start | bytes 331784 | tf_op jit(solution)/shard_map/ppermute | solution.py:478
  8.3 5.3 %collective-permute-start.1 = (bf16[40,768]{1,0:T(8,128)(2,1)S(1)}, bf16[40,768]{1,0:T(8,128)(2,1)S(1)}, u32[]{:S(2)}, u32[]{:S(2)}) collective-permute-start(bf16[40,768]{1,0:T(8,128)(2,1)S(1)} %get-tuple-element.75.own_ref), channel_id=1, source_target_pairs={{0,5},{1,4},{2,7},{3,6},{4,1},{5,0},{6,3},{7,2},{8,13},{9,12},{10,... | collective-permute-start | bytes 184328 | tf_op jit(solution)/shard_map/ppermute | solution.py:478
  11.0 5.4 %collective-permute-start.3 = (bf16[40,768]{1,0:T(8,128)(2,1)S(1)}, bf16[40,768]{1,0:T(8,128)(2,1)S(1)}, u32[]{:S(2)}, u32[]{:S(2)}) collective-permute-start(bf16[40,768]{1,0:T(8,128)(2,1)S(1)} %get-tuple-element.77.own_ref), channel_id=1, source_target_pairs={{0,9},{1,8},{2,11},{3,10},{4,13},{5,12},{6,15},{7,14},{8,1},{9,0},... | collective-permute-start | bytes 184328 | tf_op jit(solution)/shard_map/ppermute | solution.py:478
  13.6 8.8 %collective-permute-start.2 = (bf16[48,768]{1,0:T(8,128)(2,1)S(1)}, bf16[48,768]{1,0:T(8,128)(2,1)S(1)}, u32[]{:S(2)}, u32[]{:S(2)}) collective-permute-start(bf16[48,768]{1,0:T(8,128)(2,1)S(1)} %join.6.before_ref.own_ref), channel_id=1, source_target_pairs={{0,9},{1,8},{2,11},{3,10},{4,13},{5,12},{6,15},{7,14},{8,1},{9,0},... | collective-permute-start | bytes 221192 | tf_op jit(solution)/shard_map/ppermute | solution.py:478
  16.4 6.0 %collective-permute-start.4 = (bf16[48,768]{1,0:T(8,128)(2,1)S(1)}, bf16[48,768]{1,0:T(8,128)(2,1)S(1)}, u32[]{:S(2)}, u32[]{:S(2)}) collective-permute-start(bf16[48,768]{1,0:T(8,128)(2,1)S(1)} %join.8.own_ref), channel_id=1, source_target_pairs={{0,3},{1,2},{2,1},{3,0},{4,7},{5,6},{6,5},{7,4},{8,11},{9,10},{10,... | collective-permute-start | bytes 221192 | tf_op jit(solution)/shard_map/ppermute | solution.py:478
  22.4 4.9 %collective-permute-start.7 = (bf16[64,768]{1,0:T(8,128)(2,1)S(1)}, bf16[64,768]{1,0:T(8,128)(2,1)S(1)}, u32[]{:S(2)}, u32[]{:S(2)}) collective-permute-start(bf16[64,768]{1,0:T(8,128)(2,1)S(1)} %join.7.before_ref.own_ref), channel_id=1, source_target_pairs={{0,3},{1,2},{2,1},{3,0},{4,7},{5,6},{6,5},{7,4},{8,11},{9,10},{10,... | collective-permute-start | bytes 294920 | tf_op jit(solution)/shard_map/ppermute | solution.py:478
  22.5 4.9 %collective-permute-start.5 = (bf16[64,768]{1,0:T(8,128)(2,1)S(1)}, bf16[64,768]{1,0:T(8,128)(2,1)S(1)}, u32[]{:S(2)}, u32[]{:S(2)}) collective-permute-start(bf16[64,768]{1,0:T(8,128)(2,1)S(1)} %join.9.own_ref), channel_id=1, source_target_pairs={{0,5},{1,4},{2,7},{3,6},{4,1},{5,0},{6,3},{7,2},{8,13},{9,12},{10,... | collective-permute-start | bytes 294920 | tf_op jit(solution)/shard_map/ppermute | solution.py:478
  27.3 1.5 %collective-permute-start.8 = (bf16[96,768]{1,0:T(8,128)(2,1)S(1)}, bf16[96,768]{1,0:T(8,128)(2,1)S(1)}, u32[]{:S(2)}, u32[]{:S(2)}) collective-permute-start(bf16[96,768]{1,0:T(8,128)(2,1)S(1)} %join.11.refs_10_), channel_id=1, source_target_pairs={{0,1},{1,0},{2,3},{3,2},{4,5},{5,4},{6,7},{7,6},{8,9},{9,8},{10,11... | collective-permute-start | bytes 442376 | tf_op jit(solution)/shard_map/ppermute | solution.py:478
  27.4 2.8 %collective-permute-start.6 = (bf16[96,768]{1,0:T(8,128)(2,1)S(1)}, bf16[96,768]{1,0:T(8,128)(2,1)S(1)}, u32[]{:S(2)}, u32[]{:S(2)}) collective-permute-start(bf16[96,768]{1,0:T(8,128)(2,1)S(1)} %join.10.refs_13_), channel_id=1, source_target_pairs={{0,1},{1,0},{2,3},{3,2},{4,5},{5,4},{6,7},{7,6},{8,9},{9,8},{10,11... | collective-permute-start | bytes 442376 | tf_op jit(solution)/shard_map/ppermute | solution.py:478
  28.8 1.4 %copy-start = (f32[2]{0:T(128)S(1)}, f32[2]{0:T(128)}, u32[]{:S(2)}) copy-start(f32[2]{0:T(128)} %param.24) | copy-start | bytes 28
  31.7 1.9 %collective-permute-start.13 = (bf16[32,896]{1,0:T(8,128)(2,1)S(1)}, bf16[32,896]{1,0:T(8,128)(2,1)S(1)}, u32[]{:S(2)}, u32[]{:S(2)}) collective-permute-start(bf16[32,896]{1,0:T(8,128)(2,1)S(1)} %get-tuple-element.94.send_a), channel_id=1, source_target_pairs={{0,1},{1,0},{2,3},{3,2},{4,5},{5,4},{6,7},{7,6},{8,9},{9,8},{10,11... | collective-permute-start | bytes 172040 | tf_op jit(solution)/shard_map/ppermute | solution.py:478
  33.1 1.7 %collective-permute-start.9 = (bf16[32,768]{1,0:T(8,128)(2,1)S(1)}, bf16[32,768]{1,0:T(8,128)(2,1)S(1)}, u32[]{:S(2)}, u32[]{:S(2)}) collective-permute-start(bf16[32,768]{1,0:T(8,128)(2,1)S(1)} %get-tuple-element.95), channel_id=1, source_target_pairs={{0,1},{1,0},{2,3},{3,2},{4,5},{5,4},{6,7},{7,6},{8,9},{9,8},{10,11... | collective-permute-start | bytes 147464 | tf_op jit(solution)/shard_map/ppermute | solution.py:478
  33.6 4.0 %collective-permute-start.14 = (bf16[32,896]{1,0:T(8,128)(2,1)S(1)}, bf16[32,896]{1,0:T(8,128)(2,1)S(1)}, u32[]{:S(2)}, u32[]{:S(2)}) collective-permute-start(bf16[32,896]{1,0:T(8,128)(2,1)S(1)} %add.69), channel_id=1, source_target_pairs={{0,3},{1,2},{2,1},{3,0},{4,7},{5,6},{6,5},{7,4},{8,11},{9,10},{10,... | collective-permute-start | bytes 172040 | tf_op jit(solution)/shard_map/ppermute | solution.py:478
  34.8 4.5 %collective-permute-start.10 = (bf16[32,768]{1,0:T(8,128)(2,1)S(1)}, bf16[32,768]{1,0:T(8,128)(2,1)S(1)}, u32[]{:S(2)}, u32[]{:S(2)}) collective-permute-start(bf16[32,768]{1,0:T(8,128)(2,1)S(1)} %add.66), channel_id=1, source_target_pairs={{0,9},{1,8},{2,11},{3,10},{4,13},{5,12},{6,15},{7,14},{8,1},{9,0},... | collective-permute-start | bytes 147464 | tf_op jit(solution)/shard_map/ppermute | solution.py:478
  37.6 4.0 %collective-permute-start.15 = (bf16[32,896]{1,0:T(8,128)(2,1)S(1)}, bf16[32,896]{1,0:T(8,128)(2,1)S(1)}, u32[]{:S(2)}, u32[]{:S(2)}) collective-permute-start(bf16[32,896]{1,0:T(8,128)(2,1)S(1)} %add.70), channel_id=1, source_target_pairs={{0,5},{1,4},{2,7},{3,6},{4,1},{5,0},{6,3},{7,2},{8,13},{9,12},{10,... | collective-permute-start | bytes 172040 | tf_op jit(solution)/shard_map/ppermute | solution.py:478
  39.3 3.7 %collective-permute-start.11 = (bf16[32,768]{1,0:T(8,128)(2,1)S(1)}, bf16[32,768]{1,0:T(8,128)(2,1)S(1)}, u32[]{:S(2)}, u32[]{:S(2)}) collective-permute-start(bf16[32,768]{1,0:T(8,128)(2,1)S(1)} %add.67), channel_id=1, source_target_pairs={{0,3},{1,2},{2,1},{3,0},{4,7},{5,6},{6,5},{7,4},{8,11},{9,10},{10,... | collective-permute-start | bytes 147464 | tf_op jit(solution)/shard_map/ppermute | solution.py:478
  41.6 4.9 %collective-permute-start.16 = (bf16[32,896]{1,0:T(8,128)(2,1)S(1)}, bf16[32,896]{1,0:T(8,128)(2,1)S(1)}, u32[]{:S(2)}, u32[]{:S(2)}) collective-permute-start(bf16[32,896]{1,0:T(8,128)(2,1)S(1)} %add.71), channel_id=1, source_target_pairs={{0,9},{1,8},{2,11},{3,10},{4,13},{5,12},{6,15},{7,14},{8,1},{9,0},... | collective-permute-start | bytes 172040 | tf_op jit(solution)/shard_map/ppermute | solution.py:478
  43.1 5.9 %collective-permute-start.12 = (bf16[32,768]{1,0:T(8,128)(2,1)S(1)}, bf16[32,768]{1,0:T(8,128)(2,1)S(1)}, u32[]{:S(2)}, u32[]{:S(2)}) collective-permute-start(bf16[32,768]{1,0:T(8,128)(2,1)S(1)} %add.68.own_ref), channel_id=1, source_target_pairs={{0,5},{1,4},{2,7},{3,6},{4,1},{5,0},{6,3},{7,2},{8,13},{9,12},{10,... | collective-permute-start | bytes 147464 | tf_op jit(solution)/shard_map/ppermute | solution.py:478
  46.5 2.6 %collective-permute-start.18 = (bf16[32,896]{1,0:T(8,128)(2,1)S(1)}, bf16[32,896]{1,0:T(8,128)(2,1)S(1)}, u32[]{:S(2)}, u32[]{:S(2)}) collective-permute-start(bf16[32,896]{1,0:T(8,128)(2,1)S(1)} %add.72.refs_11_), channel_id=1, source_target_pairs={{0,1},{1,0},{2,3},{3,2},{4,5},{5,4},{6,7},{7,6},{8,9},{9,8},{10,11... | collective-permute-start | bytes 172040 | tf_op jit(solution)/shard_map/ppermute | solution.py:478
  49.0 1.3 %collective-permute-start.17 = (bf16[32,768]{1,0:T(8,128)(2,1)S(1)}, bf16[32,768]{1,0:T(8,128)(2,1)S(1)}, u32[]{:S(2)}, u32[]{:S(2)}) collective-permute-start(bf16[32,768]{1,0:T(8,128)(2,1)S(1)} %add.87.refs_13_), channel_id=1, source_target_pairs={{0,1},{1,0},{2,3},{3,2},{4,5},{5,4},{6,7},{7,6},{8,9},{9,8},{10,11... | collective-permute-start | bytes 147464 | tf_op jit(solution)/shard_map/ppermute | solution.py:478
  51.7 1.9 %collective-permute-start.23 = (bf16[32,896]{1,0:T(8,128)(2,1)S(1)}, bf16[32,896]{1,0:T(8,128)(2,1)S(1)}, u32[]{:S(2)}, u32[]{:S(2)}) collective-permute-start(bf16[32,896]{1,0:T(8,128)(2,1)S(1)} %get-tuple-element.110.send_a), channel_id=1, source_target_pairs={{0,1},{1,0},{2,3},{3,2},{4,5},{5,4},{6,7},{7,6},{8,9},{9,8},{10,11... | collective-permute-start | bytes 172040 | tf_op jit(solution)/shard_map/ppermute | solution.py:478
  53.5 1.9 %collective-permute-start.19 = (bf16[32,768]{1,0:T(8,128)(2,1)S(1)}, bf16[32,768]{1,0:T(8,128)(2,1)S(1)}, u32[]{:S(2)}, u32[]{:S(2)}) collective-permute-start(bf16[32,768]{1,0:T(8,128)(2,1)S(1)} %get-tuple-element.111), channel_id=1, source_target_pairs={{0,1},{1,0},{2,3},{3,2},{4,5},{5,4},{6,7},{7,6},{8,9},{9,8},{10,11... | collective-permute-start | bytes 147464 | tf_op jit(solution)/shard_map/ppermute | solution.py:478
  53.6 3.7 %collective-permute-start.24 = (bf16[32,896]{1,0:T(8,128)(2,1)S(1)}, bf16[32,896]{1,0:T(8,128)(2,1)S(1)}, u32[]{:S(2)}, u32[]{:S(2)}) collective-permute-start(bf16[32,896]{1,0:T(8,128)(2,1)S(1)} %add.76), channel_id=1, source_target_pairs={{0,3},{1,2},{2,1},{3,0},{4,7},{5,6},{6,5},{7,4},{8,11},{9,10},{10,... | collective-permute-start | bytes 172040 | tf_op jit(solution)/shard_map/ppermute | solution.py:478
  55.3 6.0 %collective-permute-start.20 = (bf16[32,768]{1,0:T(8,128)(2,1)S(1)}, bf16[32,768]{1,0:T(8,128)(2,1)S(1)}, u32[]{:S(2)}, u32[]{:S(2)}) collective-permute-start(bf16[32,768]{1,0:T(8,128)(2,1)S(1)} %add.73), channel_id=1, source_target_pairs={{0,9},{1,8},{2,11},{3,10},{4,13},{5,12},{6,15},{7,14},{8,1},{9,0},... | collective-permute-start | bytes 147464 | tf_op jit(solution)/shard_map/ppermute | solution.py:478
  57.3 4.9 %collective-permute-start.25 = (bf16[32,896]{1,0:T(8,128)(2,1)S(1)}, bf16[32,896]{1,0:T(8,128)(2,1)S(1)}, u32[]{:S(2)}, u32[]{:S(2)}) collective-permute-start(bf16[32,896]{1,0:T(8,128)(2,1)S(1)} %add.77), channel_id=1, source_target_pairs={{0,5},{1,4},{2,7},{3,6},{4,1},{5,0},{6,3},{7,2},{8,13},{9,12},{10,... | collective-permute-start | bytes 172040 | tf_op jit(solution)/shard_map/ppermute | solution.py:478
  61.3 3.9 %collective-permute-start.21 = (bf16[32,768]{1,0:T(8,128)(2,1)S(1)}, bf16[32,768]{1,0:T(8,128)(2,1)S(1)}, u32[]{:S(2)}, u32[]{:S(2)}) collective-permute-start(bf16[32,768]{1,0:T(8,128)(2,1)S(1)} %add.74), channel_id=1, source_target_pairs={{0,3},{1,2},{2,1},{3,0},{4,7},{5,6},{6,5},{7,4},{8,11},{9,10},{10,... | collective-permute-start | bytes 147464 | tf_op jit(solution)/shard_map/ppermute | solution.py:478
  62.2 6.3 %collective-permute-start.26 = (bf16[32,896]{1,0:T(8,128)(2,1)S(1)}, bf16[32,896]{1,0:T(8,128)(2,1)S(1)}, u32[]{:S(2)}, u32[]{:S(2)}) collective-permute-start(bf16[32,896]{1,0:T(8,128)(2,1)S(1)} %add.78), channel_id=1, source_target_pairs={{0,9},{1,8},{2,11},{3,10},{4,13},{5,12},{6,15},{7,14},{8,1},{9,0},... | collective-permute-start | bytes 172040 | tf_op jit(solution)/shard_map/ppermute | solution.py:478
  65.2 4.3 %collective-permute-start.22 = (bf16[32,768]{1,0:T(8,128)(2,1)S(1)}, bf16[32,768]{1,0:T(8,128)(2,1)S(1)}, u32[]{:S(2)}, u32[]{:S(2)}) collective-permute-start(bf16[32,768]{1,0:T(8,128)(2,1)S(1)} %add.75.own_ref), channel_id=1, source_target_pairs={{0,5},{1,4},{2,7},{3,6},{4,1},{5,0},{6,3},{7,2},{8,13},{9,12},{10,... | collective-permute-start | bytes 147464 | tf_op jit(solution)/shard_map/ppermute | solution.py:478
  68.4 1.5 %collective-permute-start.28 = (bf16[32,896]{1,0:T(8,128)(2,1)S(1)}, bf16[32,896]{1,0:T(8,128)(2,1)S(1)}, u32[]{:S(2)}, u32[]{:S(2)}) collective-permute-start(bf16[32,896]{1,0:T(8,128)(2,1)S(1)} %add.79.refs_11_), channel_id=1, source_target_pairs={{0,1},{1,0},{2,3},{3,2},{4,5},{5,4},{6,7},{7,6},{8,9},{9,8},{10,11... | collective-permute-start | bytes 172040 | tf_op jit(solution)/shard_map/ppermute | solution.py:478
  69.6 1.6 %collective-permute-start.27 = (bf16[32,768]{1,0:T(8,128)(2,1)S(1)}, bf16[32,768]{1,0:T(8,128)(2,1)S(1)}, u32[]{:S(2)}, u32[]{:S(2)}) collective-permute-start(bf16[32,768]{1,0:T(8,128)(2,1)S(1)} %add.88.refs_13_), channel_id=1, source_target_pairs={{0,1},{1,0},{2,3},{3,2},{4,5},{5,4},{6,7},{7,6},{8,9},{9,8},{10,11... | collective-permute-start | bytes 147464 | tf_op jit(solution)/shard_map/ppermute | solution.py:478
  72.5 1.9 %collective-permute-start.33 = (bf16[32,896]{1,0:T(8,128)(2,1)S(1)}, bf16[32,896]{1,0:T(8,128)(2,1)S(1)}, u32[]{:S(2)}, u32[]{:S(2)}) collective-permute-start(bf16[32,896]{1,0:T(8,128)(2,1)S(1)} %get-tuple-element.126.send_a), channel_id=1, source_target_pairs={{0,1},{1,0},{2,3},{3,2},{4,5},{5,4},{6,7},{7,6},{8,9},{9,8},{10,11... | collective-permute-start | bytes 172040 | tf_op jit(solution)/shard_map/ppermute | solution.py:478
  74.0 1.7 %collective-permute-start.29 = (bf16[32,768]{1,0:T(8,128)(2,1)S(1)}, bf16[32,768]{1,0:T(8,128)(2,1)S(1)}, u32[]{:S(2)}, u32[]{:S(2)}) collective-permute-start(bf16[32,768]{1,0:T(8,128)(2,1)S(1)} %get-tuple-element.127), channel_id=1, source_target_pairs={{0,1},{1,0},{2,3},{3,2},{4,5},{5,4},{6,7},{7,6},{8,9},{9,8},{10,11... | collective-permute-start | bytes 147464 | tf_op jit(solution)/shard_map/ppermute | solution.py:478
  74.4 3.9 %collective-permute-start.34 = (bf16[32,896]{1,0:T(8,128)(2,1)S(1)}, bf16[32,896]{1,0:T(8,128)(2,1)S(1)}, u32[]{:S(2)}, u32[]{:S(2)}) collective-permute-start(bf16[32,896]{1,0:T(8,128)(2,1)S(1)} %add.83), channel_id=1, source_target_pairs={{0,3},{1,2},{2,1},{3,0},{4,7},{5,6},{6,5},{7,4},{8,11},{9,10},{10,... | collective-permute-start | bytes 172040 | tf_op jit(solution)/shard_map/ppermute | solution.py:478
  75.7 5.5 %collective-permute-start.30 = (bf16[32,768]{1,0:T(8,128)(2,1)S(1)}, bf16[32,768]{1,0:T(8,128)(2,1)S(1)}, u32[]{:S(2)}, u32[]{:S(2)}) collective-permute-start(bf16[32,768]{1,0:T(8,128)(2,1)S(1)} %add.80), channel_id=1, source_target_pairs={{0,9},{1,8},{2,11},{3,10},{4,13},{5,12},{6,15},{7,14},{8,1},{9,0},... | collective-permute-start | bytes 147464 | tf_op jit(solution)/shard_map/ppermute | solution.py:478
  78.3 3.9 %collective-permute-start.35 = (bf16[32,896]{1,0:T(8,128)(2,1)S(1)}, bf16[32,896]{1,0:T(8,128)(2,1)S(1)}, u32[]{:S(2)}, u32[]{:S(2)}) collective-permute-start(bf16[32,896]{1,0:T(8,128)(2,1)S(1)} %add.84), channel_id=1, source_target_pairs={{0,5},{1,4},{2,7},{3,6},{4,1},{5,0},{6,3},{7,2},{8,13},{9,12},{10,... | collective-permute-start | bytes 172040 | tf_op jit(solution)/shard_map/ppermute | solution.py:478
  81.3 3.8 %collective-permute-start.31 = (bf16[32,768]{1,0:T(8,128)(2,1)S(1)}, bf16[32,768]{1,0:T(8,128)(2,1)S(1)}, u32[]{:S(2)}, u32[]{:S(2)}) collective-permute-start(bf16[32,768]{1,0:T(8,128)(2,1)S(1)} %add.81), channel_id=1, source_target_pairs={{0,3},{1,2},{2,1},{3,0},{4,7},{5,6},{6,5},{7,4},{8,11},{9,10},{10,... | collective-permute-start | bytes 147464 | tf_op jit(solution)/shard_map/ppermute | solution.py:478
  82.3 6.0 %collective-permute-start.36 = (bf16[32,896]{1,0:T(8,128)(2,1)S(1)}, bf16[32,896]{1,0:T(8,128)(2,1)S(1)}, u32[]{:S(2)}, u32[]{:S(2)}) collective-permute-start(bf16[32,896]{1,0:T(8,128)(2,1)S(1)} %add.85), channel_id=1, source_target_pairs={{0,9},{1,8},{2,11},{3,10},{4,13},{5,12},{6,15},{7,14},{8,1},{9,0},... | collective-permute-start | bytes 172040 | tf_op jit(solution)/shard_map/ppermute | solution.py:478
  85.1 4.2 %collective-permute-start.32 = (bf16[32,768]{1,0:T(8,128)(2,1)S(1)}, bf16[32,768]{1,0:T(8,128)(2,1)S(1)}, u32[]{:S(2)}, u32[]{:S(2)}) collective-permute-start(bf16[32,768]{1,0:T(8,128)(2,1)S(1)} %add.82.own_ref), channel_id=1, source_target_pairs={{0,5},{1,4},{2,7},{3,6},{4,1},{5,0},{6,3},{7,2},{8,13},{9,12},{10,... | collective-permute-start | bytes 147464 | tf_op jit(solution)/shard_map/ppermute | solution.py:478
  88.3 1.5 %collective-permute-start.38 = (bf16[32,896]{1,0:T(8,128)(2,1)S(1)}, bf16[32,896]{1,0:T(8,128)(2,1)S(1)}, u32[]{:S(2)}, u32[]{:S(2)}) collective-permute-start(bf16[32,896]{1,0:T(8,128)(2,1)S(1)} %add.86.refs_11_), channel_id=1, source_target_pairs={{0,1},{1,0},{2,3},{3,2},{4,5},{5,4},{6,7},{7,6},{8,9},{9,8},{10,11... | collective-permute-start | bytes 172040 | tf_op jit(solution)/shard_map/ppermute | solution.py:478
  89.4 1.7 %collective-permute-start.37 = (bf16[32,768]{1,0:T(8,128)(2,1)S(1)}, bf16[32,768]{1,0:T(8,128)(2,1)S(1)}, u32[]{:S(2)}, u32[]{:S(2)}) collective-permute-start(bf16[32,768]{1,0:T(8,128)(2,1)S(1)} %add.89.refs_13_), channel_id=1, source_target_pairs={{0,1},{1,0},{2,3},{3,2},{4,5},{5,4},{6,7},{7,6},{8,9},{9,8},{10,11... | collective-permute-start | bytes 147464 | tf_op jit(solution)/shard_map/ppermute | solution.py:478

commit v5 on v4

--- a/solution.py
+++ b/solution.py
@@ -16,8 +16,9 @@
 FULL = jnp.float32
 
 PIECES = 4
+SUMMANDS = 16
 TURNS = (0, 4, 4)
-ORDERS = ((0, 0), (2, 0), (1, 0), (2, 0))
+ORDERS = ((2, 1), (0, 1), (1, 0), (2, 0))
 
 VMEM = pl.BlockSpec(memory_space=pltpu.VMEM)
 SMEM = pl.BlockSpec(memory_space=pltpu.SMEM)
@@ -284,7 +285,7 @@
         if first:
             stat_out[...] = jnp.full(stat_out.shape, 1.0, FULL)
         else:
-            dual_sq = total(message_refs[0][:all_hours, quarter:].astype(FULL))
+            dual_sq = total(message_refs[0][:SUMMANDS, quarter:].astype(FULL))
             primal_sq = stat_ref[1:2, 0:1]
             ratio = (dual_sq + 1e-06) / (primal_sq + 1e-06)
             weight = jnp.sqrt(stat_ref[0:1, 0:1]) * jnp.sqrt(jnp.sqrt(ratio))

time: 92.9 us -> 92.8 us (level)
  transfers between devices with their start and end apart: 39 -> 39, of which waited for: 16 -> 17; matrix products, arithmetic and copies ran while one was open for 0% -> 0% of each run, Pallas kernels for 21% -> 21%
where the time goes in v5:
time: 92.8 us; the launch traced here: 92.6 us
  starting transfers between devices  35.6 us (38%)
  Pallas kernels  31.5 us (34%)
  waiting for transfers between devices  23.9 us (26%)
  between operations  1.25 us (1%)
    ppermute x39, starting transfers between devices, exchange(): lax.ppermute(x, 'ctg', [(i, i ^ mask ^ flip) for i in range(devices)])  35.6 us
    pallas_call x37, Pallas kernels, call(): pl.pallas_call(kernel, out_shape=tuple(out_shape), in_specs=[SMEM if j in...  25.4 us
    ppermute x39, waiting for transfers between devices, exchange(): lax.ppermute(x, 'ctg', [(i, i ^ mask ^ flip) for i in range(devices)])  23.9 us
    pallas_call x1, Pallas kernels, body(): pl.pallas_call(start_kernel, out_shape=(near(ctgs, lines, units, dtype=HA...  6.08 us
  transfers between devices with their start and end apart: 39, of which 17 were waited for; matrix products, arithmetic and copies ran while one was open for 0% of the time, Pallas kernels for 21%

profile of v5, /device:TPU:0, one launch (start us, length us, event | category | flops | bytes accessed | tf_op | source)
XLA Modules:
  0.0 92.6 jit_solution(5276925260014140545)
XLA Ops:
  0.6 6.1 %start.1 = (bf16[8,256,3072]{2,1,0:T(8,128)(2,1)S(1)}, bf16[36,1536]{1,0:T(8,128)(2,1)S(1)}, bf16[36,1536]{1,0:T(8,128)(2,1)S(1)}) custom-call(s32[1]{0:T(128)} %bitcast.place_ref.refs_8_, s32[8,2,24]{2,1,0:T(2,128)} %gate_hbm.1, bf16[8,256,3072]{2,1,0:T(8,128)(2,1)} %tiles_ref.1, f32[32,8,256]{2,1,0:T(8,128)} %dual_ref.3, s32[1,3072]{1,0:T(1,128)} %bitcast.12, ...), custom_call_target="tpu_custom_call" | custom-call | tf_op jit(solution)/shard_map/start/pallas_call | solution.py:521
  6.7 0.5 collective-permute-start
  7.2 1.0 %collective-permute-done.received_ref = bf16[36,1536]{1,0:T(8,128)(2,1)S(1)} collective-permute-done((bf16[36,1536]{1,0:T(8,128)(2,1)S(1)}, bf16[36,1536]{1,0:T(8,128)(2,1)S(1)}, u32[]{:S(2)}, u32[]{:S(2)}) %collective-permute-start) | collective-permute-done | bytes 110624 | tf_op jit(solution)/shard_map/ppermute | solution.py:479
  8.3 2.8 %collective-permute-start.1 = (bf16[40,768]{1,0:T(8,128)(2,1)S(1)}, bf16[40,768]{1,0:T(8,128)(2,1)S(1)}, u32[]{:S(2)}, u32[]{:S(2)}) collective-permute-start(bf16[40,768]{1,0:T(8,128)(2,1)S(1)} %get-tuple-element.75.own_ref), channel_id=1, source_target_pairs={{0,5},{1,4},{2,7},{3,6},{4,1},{5,0},{6,3},{7,2},{8,13},{9,12},{10,... | collective-permute-start | bytes 184328 | tf_op jit(solution)/shard_map/ppermute | solution.py:479
  11.0 2.6 %collective-permute-start.3 = (bf16[40,768]{1,0:T(8,128)(2,1)S(1)}, bf16[40,768]{1,0:T(8,128)(2,1)S(1)}, u32[]{:S(2)}, u32[]{:S(2)}) collective-permute-start(bf16[40,768]{1,0:T(8,128)(2,1)S(1)} %get-tuple-element.77.own_ref), channel_id=1, source_target_pairs={{0,9},{1,8},{2,11},{3,10},{4,13},{5,12},{6,15},{7,14},{8,1},{9,0},... | collective-permute-start | bytes 184328 | tf_op jit(solution)/shard_map/ppermute | solution.py:479
  13.6 2.8 %collective-permute-start.2 = (bf16[48,768]{1,0:T(8,128)(2,1)S(1)}, bf16[48,768]{1,0:T(8,128)(2,1)S(1)}, u32[]{:S(2)}, u32[]{:S(2)}) collective-permute-start(bf16[48,768]{1,0:T(8,128)(2,1)S(1)} %join.6.before_ref.own_ref), channel_id=1, source_target_pairs={{0,9},{1,8},{2,11},{3,10},{4,13},{5,12},{6,15},{7,14},{8,1},{9,0},... | collective-permute-start | bytes 221192 | tf_op jit(solution)/shard_map/ppermute | solution.py:479
  16.4 2.1 %collective-permute-start.4 = (bf16[48,768]{1,0:T(8,128)(2,1)S(1)}, bf16[48,768]{1,0:T(8,128)(2,1)S(1)}, u32[]{:S(2)}, u32[]{:S(2)}) collective-permute-start(bf16[48,768]{1,0:T(8,128)(2,1)S(1)} %join.8.own_ref), channel_id=1, source_target_pairs={{0,3},{1,2},{2,1},{3,0},{4,7},{5,6},{6,5},{7,4},{8,11},{9,10},{10,... | collective-permute-start | bytes 221192 | tf_op jit(solution)/shard_map/ppermute | solution.py:479
  19.0 0.5 turn.10.refs_3_.refs_2_
  19.5 0.5 turn.9.refs_2_.refs_1_
  20.0 0.5 turn.8.refs_1_.refs_0_
  20.4 1.9 %prepare.1 = (f32[32,2048]{1,0:T(8,128)S(1)}, f32[32,2048]{1,0:T(8,128)S(1)}, f32[1,2048]{1,0:T(1,128)S(1)}, f32[4,3072]{1,0:T(4,128)S(1)}, f32[2,3072]{1,0:T(2,128)S(1)}, /*index=5*/f32[2,3072]{1,0:T(2,128)S(1)}) custom-call(s32[1]{0:T(128)} %bitcast.place_ref.refs_8_, bf16[48,768]{1,0:T(8,128)(2,1)S(1)} %join.6.before_ref.own_ref, f32[32,8,256]{2,1,0:T(8,128)} %dual_ref.3, ...), custom_call_target="tpu_custom_call" | custom-call | bytes 5535000 | tf_op jit(solution)/shard_map/prepare/pallas_call | solution.py:37
  22.5 1.5 %collective-permute-start.5 = (bf16[64,768]{1,0:T(8,128)(2,1)S(1)}, bf16[64,768]{1,0:T(8,128)(2,1)S(1)}, u32[]{:S(2)}, u32[]{:S(2)}) collective-permute-start(bf16[64,768]{1,0:T(8,128)(2,1)S(1)} %join.9.own_ref), channel_id=1, source_target_pairs={{0,5},{1,4},{2,7},{3,6},{4,1},{5,0},{6,3},{7,2},{8,13},{9,12},{10,... | collective-permute-start | bytes 294920 | tf_op jit(solution)/shard_map/ppermute | solution.py:479
  25.9 1.4 %collective-permute-done.7.received_ref = bf16[64,768]{1,0:T(8,128)(2,1)S(1)} collective-permute-done((bf16[64,768]{1,0:T(8,128)(2,1)S(1)}, bf16[64,768]{1,0:T(8,128)(2,1)S(1)}, u32[]{:S(2)}, u32[]{:S(2)}) %collective-permute-start.7) | collective-permute-done | bytes 98336 | tf_op jit(solution)/shard_map/ppermute | solution.py:479
  27.4 0.6 collective-permute-start.6
  28.0 0.8 flow.8
  28.8 1.4 %flow.9 = (f32[32,768]{1,0:T(8,128)S(1)}, f32[32,768]{1,0:T(8,128)S(1)}, f32[32,768]{1,0:T(8,128)S(1)}, f32[32,768]{1,0:T(8,128)S(1)}, f32[32,2048]{1,0:T(8,128)S(1)}) custom-call(bf16[1,3072,256]{2,1,0:T(8,128)(2,1)S(1)} %turn.8.refs_1_.refs_0_, bf16[1,3072,256]{2,1,0:T(8,128)(2,1)S(1)} %turn.9.refs_2_.refs_1_, ...), custom_call_target="tpu_custom_call" | custom-call | bytes 5166000 | tf_op jit(solution)/shard_map/flow/pallas_call | solution.py:37
  30.2 1.5 %dual.4 = (f32[32,768]{1,0:T(8,128)S(1)}, f32[32,2048]{1,0:T(8,128)S(1)}, f32[2,3072]{1,0:T(2,128)S(1)}, f32[2,1]{1,0:T(2,128)S(1)}, f32[8,128]{1,0:T(8,128)S(1)...) custom-call(bf16[1,3072,256]{2,1,0:T(8,128)(2,1)S(1)} %turn.8.refs_1_.refs_0_, ...), custom_call_target="tpu_custom_call" | custom-call | bytes 5535000 | tf_op jit(solution)/shard_map/dual/pallas_call | solution.py:37
  31.9 1.2 %pull.7 = (bf16[32,896]{1,0:T(8,128)(2,1)S(1)}, bf16[32,768]{1,0:T(8,128)(2,1)S(1)}) custom-call(s32[1]{0:T(128)} %bitcast.place_ref.refs_8_, bf16[8,256,3072]{2,1,0:T(8,128)(2,1)S(1)} %get-tuple-element.72.masked_ref.refs_9_, bf16[32,2048]{1,0:T(8,128)(2,1)S(1)} %get-tuple-element.92.half_dual, f32[8,3072]{1,0:T(8,128)S(1)} %get-tuple-element.93.term_ref, ...), custom_call_target="tpu_custom_call" | custom-call | bytes 4428000 | tf_op jit(solution)/shard_map/pull/pallas_call | solution.py:37
  33.1 0.5 collective-permute-start.9
  33.6 1.8 %collective-permute-start.14 = (bf16[32,896]{1,0:T(8,128)(2,1)S(1)}, bf16[32,896]{1,0:T(8,128)(2,1)S(1)}, u32[]{:S(2)}, u32[]{:S(2)}) collective-permute-start(bf16[32,896]{1,0:T(8,128)(2,1)S(1)} %add.69), channel_id=1, source_target_pairs={{0,5},{1,4},{2,7},{3,6},{4,1},{5,0},{6,3},{7,2},{8,13},{9,12},{10,... | collective-permute-start | bytes 172040 | tf_op jit(solution)/shard_map/ppermute | solution.py:479
  35.4 0.7 pull.6
  36.1 1.2 %collective-permute-start.10 = (bf16[32,768]{1,0:T(8,128)(2,1)S(1)}, bf16[32,768]{1,0:T(8,128)(2,1)S(1)}, u32[]{:S(2)}, u32[]{:S(2)}) collective-permute-start(bf16[32,768]{1,0:T(8,128)(2,1)S(1)} %add.66), channel_id=1, source_target_pairs={{0,9},{1,8},{2,11},{3,10},{4,13},{5,12},{6,15},{7,14},{8,1},{9,0},... | collective-permute-start | bytes 147464 | tf_op jit(solution)/shard_map/ppermute | solution.py:479
  37.6 1.0 %collective-permute-start.15 = (bf16[32,896]{1,0:T(8,128)(2,1)S(1)}, bf16[32,896]{1,0:T(8,128)(2,1)S(1)}, u32[]{:S(2)}, u32[]{:S(2)}) collective-permute-start(bf16[32,896]{1,0:T(8,128)(2,1)S(1)} %add.70), channel_id=1, source_target_pairs={{0,3},{1,2},{2,1},{3,0},{4,7},{5,6},{6,5},{7,4},{8,11},{9,10},{10,... | collective-permute-start | bytes 172040 | tf_op jit(solution)/shard_map/ppermute | solution.py:479
  38.6 3.4 %collective-permute-done.10 = bf16[32,768]{1,0:T(8,128)(2,1)S(1)} collective-permute-done((bf16[32,768]{1,0:T(8,128)(2,1)S(1)}, bf16[32,768]{1,0:T(8,128)(2,1)S(1)}, u32[]{:S(2)}, u32[]{:S(2)}) %collective-permute-start.10) | collective-permute-done | bytes 49184 | tf_op jit(solution)/shard_map/ppermute | solution.py:479
  42.1 0.6 collective-permute-start.16
  42.7 3.1 %collective-permute-done.11 = bf16[32,768]{1,0:T(8,128)(2,1)S(1)} collective-permute-done((bf16[32,768]{1,0:T(8,128)(2,1)S(1)}, bf16[32,768]{1,0:T(8,128)(2,1)S(1)}, u32[]{:S(2)}, u32[]{:S(2)}) %collective-permute-start.11) | collective-permute-done | bytes 49184 | tf_op jit(solution)/shard_map/ppermute | solution.py:479
  45.8 1.2 %collective-permute-start.12 = (bf16[32,768]{1,0:T(8,128)(2,1)S(1)}, bf16[32,768]{1,0:T(8,128)(2,1)S(1)}, u32[]{:S(2)}, u32[]{:S(2)}) collective-permute-start(bf16[32,768]{1,0:T(8,128)(2,1)S(1)} %add.68.own_ref), channel_id=1, source_target_pairs={{0,3},{1,2},{2,1},{3,0},{4,7},{5,6},{6,5},{7,4},{8,11},{9,10},{10,... | collective-permute-start | bytes 147464 | tf_op jit(solution)/shard_map/ppermute | solution.py:479
  47.2 1.0 %flow.10 = (f32[32,768]{1,0:T(8,128)S(1)}, f32[32,2048]{1,0:T(8,128)S(1)}, f32[8,128]{1,0:T(8,128)S(1)}) custom-call(bf16[1,3072,256]{2,1,0:T(8,128)(2,1)S(1)} %turn.8.refs_1_.refs_0_, bf16[1,3072,256]{2,1,0:T(8,128)(2,1)S(1)} %turn.9.refs_2_.refs_1_, bf16[1,3072,256]{2,1,0:T(8,128)(2,1)S(1)} %turn.10.refs_3_.refs_2_, ...), custom_call_target="tpu_custom_call" | custom-call | bytes 2583000 | tf_op jit(solution)/shard_map/flow/pallas_call | solution.py:37
  48.2 1.2 %collective-permute-done.12.received_ref = bf16[32,768]{1,0:T(8,128)(2,1)S(1)} collective-permute-done((bf16[32,768]{1,0:T(8,128)(2,1)S(1)}, bf16[32,768]{1,0:T(8,128)(2,1)S(1)}, u32[]{:S(2)}, u32[]{:S(2)}) %collective-permute-start.12) | collective-permute-done | bytes 49184 | tf_op jit(solution)/shard_map/ppermute | solution.py:479
  49.4 0.5 collective-permute-start.17
  49.9 1.2 %flow.11 = (f32[32,768]{1,0:T(8,128)S(1)}, f32[32,768]{1,0:T(8,128)S(1)}, f32[32,2048]{1,0:T(8,128)S(1)}) custom-call(bf16[1,3072,256]{2,1,0:T(8,128)(2,1)S(1)} %turn.8.refs_1_.refs_0_, bf16[1,3072,256]{2,1,0:T(8,128)(2,1)S(1)} %turn.9.refs_2_.refs_1_, bf16[1,3072,256]{2,1,0:T(8,128)(2,1)S(1)} %turn.10.refs_3_.refs_2_, ...), custom_call_target="tpu_custom_call" | custom-call | bytes 5166000 | tf_op jit(solution)/shard_map/flow/pallas_call | solution.py:37
  51.1 1.3 %dual.5 = (f32[32,768]{1,0:T(8,128)S(1)}, f32[32,2048]{1,0:T(8,128)S(1)}, f32[2,3072]{1,0:T(2,128)S(1)}, f32[2,1]{1,0:T(2,128)S(1)}, f32[8,128]{1,0:T(8,128)S(1)...) custom-call(bf16[1,3072,256]{2,1,0:T(8,128)(2,1)S(1)} %turn.8.refs_1_.refs_0_, ...), custom_call_target="tpu_custom_call" | custom-call | bytes 5535000 | tf_op jit(solution)/shard_map/dual/pallas_call | solution.py:37
  52.6 1.2 %pull.9 = (bf16[32,896]{1,0:T(8,128)(2,1)S(1)}, bf16[32,768]{1,0:T(8,128)(2,1)S(1)}) custom-call(s32[1]{0:T(128)} %bitcast.place_ref.refs_8_, bf16[8,256,3072]{2,1,0:T(8,128)(2,1)S(1)} %get-tuple-element.72.masked_ref.refs_9_, bf16[32,2048]{1,0:T(8,128)(2,1)S(1)} %get-tuple-element.108.half_dual, f32[8,3072]{1,0:T(8,128)S(1)} %get-tuple-element.109.term_ref, ...), custom_call_target="tpu_custom_call" | custom-call | bytes 4428000 | tf_op jit(solution)/shard_map/pull/pallas_call | solution.py:37
  53.8 0.5 collective-permute-start.19
  54.6 0.6 pull.8
  55.3 2.4 %collective-permute-start.20 = (bf16[32,768]{1,0:T(8,128)(2,1)S(1)}, bf16[32,768]{1,0:T(8,128)(2,1)S(1)}, u32[]{:S(2)}, u32[]{:S(2)}) collective-permute-start(bf16[32,768]{1,0:T(8,128)(2,1)S(1)} %add.73), channel_id=1, source_target_pairs={{0,9},{1,8},{2,11},{3,10},{4,13},{5,12},{6,15},{7,14},{8,1},{9,0},... | collective-permute-start | bytes 147464 | tf_op jit(solution)/shard_map/ppermute | solution.py:479
  57.7 0.6 collective-permute-done.24
  58.4 0.9 collective-permute-start.25
  59.3 0.8 collective-permute-done.20
  60.1 1.3 %collective-permute-start.21 = (bf16[32,768]{1,0:T(8,128)(2,1)S(1)}, bf16[32,768]{1,0:T(8,128)(2,1)S(1)}, u32[]{:S(2)}, u32[]{:S(2)}) collective-permute-start(bf16[32,768]{1,0:T(8,128)(2,1)S(1)} %add.74), channel_id=1, source_target_pairs={{0,5},{1,4},{2,7},{3,6},{4,1},{5,0},{6,3},{7,2},{8,13},{9,12},{10,... | collective-permute-start | bytes 147464 | tf_op jit(solution)/shard_map/ppermute | solution.py:479
  61.4 1.0 %collective-permute-done.25 = bf16[32,896]{1,0:T(8,128)(2,1)S(1)} collective-permute-done((bf16[32,896]{1,0:T(8,128)(2,1)S(1)}, bf16[32,896]{1,0:T(8,128)(2,1)S(1)}, u32[]{:S(2)}, u32[]{:S(2)}) %collective-permute-start.25) | collective-permute-done | bytes 57376 | tf_op jit(solution)/shard_map/ppermute | solution.py:479
  62.8 0.8 collective-permute-done.21
  63.7 2.0 %collective-permute-start.22 = (bf16[32,768]{1,0:T(8,128)(2,1)S(1)}, bf16[32,768]{1,0:T(8,128)(2,1)S(1)}, u32[]{:S(2)}, u32[]{:S(2)}) collective-permute-start(bf16[32,768]{1,0:T(8,128)(2,1)S(1)} %add.75.own_ref), channel_id=1, source_target_pairs={{0,3},{1,2},{2,1},{3,0},{4,7},{5,6},{6,5},{7,4},{8,11},{9,10},{10,... | collective-permute-start | bytes 147464 | tf_op jit(solution)/shard_map/ppermute | solution.py:479
  65.6 3.1 %collective-permute-done.26 = bf16[32,896]{1,0:T(8,128)(2,1)S(1)} collective-permute-done((bf16[32,896]{1,0:T(8,128)(2,1)S(1)}, bf16[32,896]{1,0:T(8,128)(2,1)S(1)}, u32[]{:S(2)}, u32[]{:S(2)}) %collective-permute-start.26) | collective-permute-done | bytes 57376 | tf_op jit(solution)/shard_map/ppermute | solution.py:479
  68.9 0.8 flow.12
  69.7 0.5 collective-permute-start.27
  70.2 1.2 %flow.13 = (f32[32,768]{1,0:T(8,128)S(1)}, f32[32,768]{1,0:T(8,128)S(1)}, f32[32,2048]{1,0:T(8,128)S(1)}) custom-call(bf16[1,3072,256]{2,1,0:T(8,128)(2,1)S(1)} %turn.8.refs_1_.refs_0_, bf16[1,3072,256]{2,1,0:T(8,128)(2,1)S(1)} %turn.9.refs_2_.refs_1_, bf16[1,3072,256]{2,1,0:T(8,128)(2,1)S(1)} %turn.10.refs_3_.refs_2_, ...), custom_call_target="tpu_custom_call" | custom-call | bytes 5166000 | tf_op jit(solution)/shard_map/flow/pallas_call | solution.py:37
  71.4 1.3 %dual.6 = (f32[32,768]{1,0:T(8,128)S(1)}, f32[32,2048]{1,0:T(8,128)S(1)}, f32[2,3072]{1,0:T(2,128)S(1)}, f32[2,1]{1,0:T(2,128)S(1)}, f32[8,128]{1,0:T(8,128)S(1)...) custom-call(bf16[1,3072,256]{2,1,0:T(8,128)(2,1)S(1)} %turn.8.refs_1_.refs_0_, ...), custom_call_target="tpu_custom_call" | custom-call | bytes 5535000 | tf_op jit(solution)/shard_map/dual/pallas_call | solution.py:37
  72.9 1.2 %pull.11 = (bf16[32,896]{1,0:T(8,128)(2,1)S(1)}, bf16[32,768]{1,0:T(8,128)(2,1)S(1)}) custom-call(s32[1]{0:T(128)} %bitcast.place_ref.refs_8_, bf16[8,256,3072]{2,1,0:T(8,128)(2,1)S(1)} %get-tuple-element.72.masked_ref.refs_9_, bf16[32,2048]{1,0:T(8,128)(2,1)S(1)} %get-tuple-element.124.half_dual, f32[8,3072]{1,0:T(8,128)S(1)} %get-tuple-element.125.term_ref, ...), custom_call_target="tpu_custom_call" | custom-call | bytes 4428000 | tf_op jit(solution)/shard_map/pull/pallas_call | solution.py:37
  74.1 0.5 collective-permute-start.29
  74.7 0.7 pull.10
  75.5 1.8 %collective-permute-start.30 = (bf16[32,768]{1,0:T(8,128)(2,1)S(1)}, bf16[32,768]{1,0:T(8,128)(2,1)S(1)}, u32[]{:S(2)}, u32[]{:S(2)}) collective-permute-start(bf16[32,768]{1,0:T(8,128)(2,1)S(1)} %add.80), channel_id=1, source_target_pairs={{0,9},{1,8},{2,11},{3,10},{4,13},{5,12},{6,15},{7,14},{8,1},{9,0},... | collective-permute-start | bytes 147464 | tf_op jit(solution)/shard_map/ppermute | solution.py:479
  77.3 1.3 %collective-permute-done.34 = bf16[32,896]{1,0:T(8,128)(2,1)S(1)} collective-permute-done((bf16[32,896]{1,0:T(8,128)(2,1)S(1)}, bf16[32,896]{1,0:T(8,128)(2,1)S(1)}, u32[]{:S(2)}, u32[]{:S(2)}) %collective-permute-start.34) | collective-permute-done | bytes 57376 | tf_op jit(solution)/shard_map/ppermute | solution.py:479
  78.6 0.8 collective-permute-start.35
  79.4 0.5 collective-permute-done.30
  80.0 1.7 %collective-permute-start.31 = (bf16[32,768]{1,0:T(8,128)(2,1)S(1)}, bf16[32,768]{1,0:T(8,128)(2,1)S(1)}, u32[]{:S(2)}, u32[]{:S(2)}) collective-permute-start(bf16[32,768]{1,0:T(8,128)(2,1)S(1)} %add.81), channel_id=1, source_target_pairs={{0,5},{1,4},{2,7},{3,6},{4,1},{5,0},{6,3},{7,2},{8,13},{9,12},{10,... | collective-permute-start | bytes 147464 | tf_op jit(solution)/shard_map/ppermute | solution.py:479
  81.7 0.9 collective-permute-done.35
  82.7 0.9 collective-permute-done.31
  83.6 1.0 %collective-permute-start.32 = (bf16[32,768]{1,0:T(8,128)(2,1)S(1)}, bf16[32,768]{1,0:T(8,128)(2,1)S(1)}, u32[]{:S(2)}, u32[]{:S(2)}) collective-permute-start(bf16[32,768]{1,0:T(8,128)(2,1)S(1)} %add.82.own_ref), channel_id=1, source_target_pairs={{0,3},{1,2},{2,1},{3,0},{4,7},{5,6},{6,5},{7,4},{8,11},{9,10},{10,... | collective-permute-start | bytes 147464 | tf_op jit(solution)/shard_map/ppermute | solution.py:479
  84.6 3.6 %collective-permute-done.36 = bf16[32,896]{1,0:T(8,128)(2,1)S(1)} collective-permute-done((bf16[32,896]{1,0:T(8,128)(2,1)S(1)}, bf16[32,896]{1,0:T(8,128)(2,1)S(1)}, u32[]{:S(2)}, u32[]{:S(2)}) %collective-permute-start.36) | collective-permute-done | bytes 57376 | tf_op jit(solution)/shard_map/ppermute | solution.py:479
  88.4 0.8 flow.14
  89.2 0.5 collective-permute-start.37
  89.7 1.2 %flow.15 = (f32[32,768]{1,0:T(8,128)S(1)}, f32[32,768]{1,0:T(8,128)S(1)}, f32[32,2048]{1,0:T(8,128)S(1)}) custom-call(bf16[1,3072,256]{2,1,0:T(8,128)(2,1)S(1)} %turn.8.refs_1_.refs_0_, bf16[1,3072,256]{2,1,0:T(8,128)(2,1)S(1)} %turn.9.refs_2_.refs_1_, bf16[1,3072,256]{2,1,0:T(8,128)(2,1)S(1)} %turn.10.refs_3_.refs_2_, ...), custom_call_target="tpu_custom_call" | custom-call | bytes 5166000 | tf_op jit(solution)/shard_map/flow/pallas_call | solution.py:37
  91.0 1.5 %dual.7 = (f32[2,3072]{1,0:T(2,128)}, f32[32,8,256]{2,1,0:T(8,128)}, f32[2,3072]{1,0:T(2,128)}, f32[2]{0:T(128)}) custom-call(bf16[1,3072,256]{2,1,0:T(8,128)(2,1)S(1)} %turn.8.refs_1_.refs_0_, bf16[1,3072,256]{2,1,0:T(8,128)(2,1)S(1)} %turn.9.refs_2_.refs_1_, bf16[1,3072,256]{2,1,0:T(8,128)(2,1)S(1)} %turn.10.refs_3_.refs_2_, ...), custom_call_target="tpu_custom_call" | custom-call | bytes 4428000 | tf_op jit(solution)/shard_map/dual/pallas_call | solution.py:37
  (75 shorter events, 5.4 us)
Async XLA Ops:
  6.7 1.5 %collective-permute-start = (bf16[36,1536]{1,0:T(8,128)(2,1)S(1)}, bf16[36,1536]{1,0:T(8,128)(2,1)S(1)}, u32[]{:S(2)}, u32[]{:S(2)}) collective-permute-start(bf16[36,1536]{1,0:T(8,128)(2,1)S(1)} %get-tuple-element.74), channel_id=1, source_target_pairs={{0,1},{1,0},{2,3},{3,2},{4,5},{5,4},{6,7},{7,6},{8,9},{9,8},{10,11... | collective-permute-start | bytes 331784 | tf_op jit(solution)/shard_map/ppermute | solution.py:479
  8.3 5.3 %collective-permute-start.1 = (bf16[40,768]{1,0:T(8,128)(2,1)S(1)}, bf16[40,768]{1,0:T(8,128)(2,1)S(1)}, u32[]{:S(2)}, u32[]{:S(2)}) collective-permute-start(bf16[40,768]{1,0:T(8,128)(2,1)S(1)} %get-tuple-element.75.own_ref), channel_id=1, source_target_pairs={{0,5},{1,4},{2,7},{3,6},{4,1},{5,0},{6,3},{7,2},{8,13},{9,12},{10,... | collective-permute-start | bytes 184328 | tf_op jit(solution)/shard_map/ppermute | solution.py:479
  11.0 5.4 %collective-permute-start.3 = (bf16[40,768]{1,0:T(8,128)(2,1)S(1)}, bf16[40,768]{1,0:T(8,128)(2,1)S(1)}, u32[]{:S(2)}, u32[]{:S(2)}) collective-permute-start(bf16[40,768]{1,0:T(8,128)(2,1)S(1)} %get-tuple-element.77.own_ref), channel_id=1, source_target_pairs={{0,9},{1,8},{2,11},{3,10},{4,13},{5,12},{6,15},{7,14},{8,1},{9,0},... | collective-permute-start | bytes 184328 | tf_op jit(solution)/shard_map/ppermute | solution.py:479
  13.6 8.8 %collective-permute-start.2 = (bf16[48,768]{1,0:T(8,128)(2,1)S(1)}, bf16[48,768]{1,0:T(8,128)(2,1)S(1)}, u32[]{:S(2)}, u32[]{:S(2)}) collective-permute-start(bf16[48,768]{1,0:T(8,128)(2,1)S(1)} %join.6.before_ref.own_ref), channel_id=1, source_target_pairs={{0,9},{1,8},{2,11},{3,10},{4,13},{5,12},{6,15},{7,14},{8,1},{9,0},... | collective-permute-start | bytes 221192 | tf_op jit(solution)/shard_map/ppermute | solution.py:479
  16.4 6.0 %collective-permute-start.4 = (bf16[48,768]{1,0:T(8,128)(2,1)S(1)}, bf16[48,768]{1,0:T(8,128)(2,1)S(1)}, u32[]{:S(2)}, u32[]{:S(2)}) collective-permute-start(bf16[48,768]{1,0:T(8,128)(2,1)S(1)} %join.8.own_ref), channel_id=1, source_target_pairs={{0,3},{1,2},{2,1},{3,0},{4,7},{5,6},{6,5},{7,4},{8,11},{9,10},{10,... | collective-permute-start | bytes 221192 | tf_op jit(solution)/shard_map/ppermute | solution.py:479
  22.4 4.9 %collective-permute-start.7 = (bf16[64,768]{1,0:T(8,128)(2,1)S(1)}, bf16[64,768]{1,0:T(8,128)(2,1)S(1)}, u32[]{:S(2)}, u32[]{:S(2)}) collective-permute-start(bf16[64,768]{1,0:T(8,128)(2,1)S(1)} %join.7.before_ref.own_ref), channel_id=1, source_target_pairs={{0,3},{1,2},{2,1},{3,0},{4,7},{5,6},{6,5},{7,4},{8,11},{9,10},{10,... | collective-permute-start | bytes 294920 | tf_op jit(solution)/shard_map/ppermute | solution.py:479
  22.5 4.9 %collective-permute-start.5 = (bf16[64,768]{1,0:T(8,128)(2,1)S(1)}, bf16[64,768]{1,0:T(8,128)(2,1)S(1)}, u32[]{:S(2)}, u32[]{:S(2)}) collective-permute-start(bf16[64,768]{1,0:T(8,128)(2,1)S(1)} %join.9.own_ref), channel_id=1, source_target_pairs={{0,5},{1,4},{2,7},{3,6},{4,1},{5,0},{6,3},{7,2},{8,13},{9,12},{10,... | collective-permute-start | bytes 294920 | tf_op jit(solution)/shard_map/ppermute | solution.py:479
  27.3 1.5 %collective-permute-start.8 = (bf16[96,768]{1,0:T(8,128)(2,1)S(1)}, bf16[96,768]{1,0:T(8,128)(2,1)S(1)}, u32[]{:S(2)}, u32[]{:S(2)}) collective-permute-start(bf16[96,768]{1,0:T(8,128)(2,1)S(1)} %join.11.refs_10_), channel_id=1, source_target_pairs={{0,1},{1,0},{2,3},{3,2},{4,5},{5,4},{6,7},{7,6},{8,9},{9,8},{10,11... | collective-permute-start | bytes 442376 | tf_op jit(solution)/shard_map/ppermute | solution.py:479
  27.4 2.8 %collective-permute-start.6 = (bf16[96,768]{1,0:T(8,128)(2,1)S(1)}, bf16[96,768]{1,0:T(8,128)(2,1)S(1)}, u32[]{:S(2)}, u32[]{:S(2)}) collective-permute-start(bf16[96,768]{1,0:T(8,128)(2,1)S(1)} %join.10.refs_13_), channel_id=1, source_target_pairs={{0,1},{1,0},{2,3},{3,2},{4,5},{5,4},{6,7},{7,6},{8,9},{9,8},{10,11... | collective-permute-start | bytes 442376 | tf_op jit(solution)/shard_map/ppermute | solution.py:479
  28.8 1.4 %copy-start = (f32[2]{0:T(128)S(1)}, f32[2]{0:T(128)}, u32[]{:S(2)}) copy-start(f32[2]{0:T(128)} %param.24) | copy-start | bytes 28
  31.7 1.9 %collective-permute-start.13 = (bf16[32,896]{1,0:T(8,128)(2,1)S(1)}, bf16[32,896]{1,0:T(8,128)(2,1)S(1)}, u32[]{:S(2)}, u32[]{:S(2)}) collective-permute-start(bf16[32,896]{1,0:T(8,128)(2,1)S(1)} %get-tuple-element.94.send_a), channel_id=1, source_target_pairs={{0,1},{1,0},{2,3},{3,2},{4,5},{5,4},{6,7},{7,6},{8,9},{9,8},{10,11... | collective-permute-start | bytes 172040 | tf_op jit(solution)/shard_map/ppermute | solution.py:479
  33.1 3.0 %collective-permute-start.9 = (bf16[32,768]{1,0:T(8,128)(2,1)S(1)}, bf16[32,768]{1,0:T(8,128)(2,1)S(1)}, u32[]{:S(2)}, u32[]{:S(2)}) collective-permute-start(bf16[32,768]{1,0:T(8,128)(2,1)S(1)} %get-tuple-element.95), channel_id=1, source_target_pairs={{0,1},{1,0},{2,3},{3,2},{4,5},{5,4},{6,7},{7,6},{8,9},{9,8},{10,11... | collective-permute-start | bytes 147464 | tf_op jit(solution)/shard_map/ppermute | solution.py:479
  33.6 4.0 %collective-permute-start.14 = (bf16[32,896]{1,0:T(8,128)(2,1)S(1)}, bf16[32,896]{1,0:T(8,128)(2,1)S(1)}, u32[]{:S(2)}, u32[]{:S(2)}) collective-permute-start(bf16[32,896]{1,0:T(8,128)(2,1)S(1)} %add.69), channel_id=1, source_target_pairs={{0,5},{1,4},{2,7},{3,6},{4,1},{5,0},{6,3},{7,2},{8,13},{9,12},{10,... | collective-permute-start | bytes 172040 | tf_op jit(solution)/shard_map/ppermute | solution.py:479
  36.1 5.8 %collective-permute-start.10 = (bf16[32,768]{1,0:T(8,128)(2,1)S(1)}, bf16[32,768]{1,0:T(8,128)(2,1)S(1)}, u32[]{:S(2)}, u32[]{:S(2)}) collective-permute-start(bf16[32,768]{1,0:T(8,128)(2,1)S(1)} %add.66), channel_id=1, source_target_pairs={{0,9},{1,8},{2,11},{3,10},{4,13},{5,12},{6,15},{7,14},{8,1},{9,0},... | collective-permute-start | bytes 147464 | tf_op jit(solution)/shard_map/ppermute | solution.py:479
  37.6 4.4 %collective-permute-start.15 = (bf16[32,896]{1,0:T(8,128)(2,1)S(1)}, bf16[32,896]{1,0:T(8,128)(2,1)S(1)}, u32[]{:S(2)}, u32[]{:S(2)}) collective-permute-start(bf16[32,896]{1,0:T(8,128)(2,1)S(1)} %add.70), channel_id=1, source_target_pairs={{0,3},{1,2},{2,1},{3,0},{4,7},{5,6},{6,5},{7,4},{8,11},{9,10},{10,... | collective-permute-start | bytes 172040 | tf_op jit(solution)/shard_map/ppermute | solution.py:479
  41.9 3.8 %collective-permute-start.11 = (bf16[32,768]{1,0:T(8,128)(2,1)S(1)}, bf16[32,768]{1,0:T(8,128)(2,1)S(1)}, u32[]{:S(2)}, u32[]{:S(2)}) collective-permute-start(bf16[32,768]{1,0:T(8,128)(2,1)S(1)} %add.67), channel_id=1, source_target_pairs={{0,5},{1,4},{2,7},{3,6},{4,1},{5,0},{6,3},{7,2},{8,13},{9,12},{10,... | collective-permute-start | bytes 147464 | tf_op jit(solution)/shard_map/ppermute | solution.py:479
  42.1 4.9 %collective-permute-start.16 = (bf16[32,896]{1,0:T(8,128)(2,1)S(1)}, bf16[32,896]{1,0:T(8,128)(2,1)S(1)}, u32[]{:S(2)}, u32[]{:S(2)}) collective-permute-start(bf16[32,896]{1,0:T(8,128)(2,1)S(1)} %add.71), channel_id=1, source_target_pairs={{0,9},{1,8},{2,11},{3,10},{4,13},{5,12},{6,15},{7,14},{8,1},{9,0},... | collective-permute-start | bytes 172040 | tf_op jit(solution)/shard_map/ppermute | solution.py:479
  45.8 3.6 %collective-permute-start.12 = (bf16[32,768]{1,0:T(8,128)(2,1)S(1)}, bf16[32,768]{1,0:T(8,128)(2,1)S(1)}, u32[]{:S(2)}, u32[]{:S(2)}) collective-permute-start(bf16[32,768]{1,0:T(8,128)(2,1)S(1)} %add.68.own_ref), channel_id=1, source_target_pairs={{0,3},{1,2},{2,1},{3,0},{4,7},{5,6},{6,5},{7,4},{8,11},{9,10},{10,... | collective-permute-start | bytes 147464 | tf_op jit(solution)/shard_map/ppermute | solution.py:479
  47.0 2.9 %collective-permute-start.18 = (bf16[32,896]{1,0:T(8,128)(2,1)S(1)}, bf16[32,896]{1,0:T(8,128)(2,1)S(1)}, u32[]{:S(2)}, u32[]{:S(2)}) collective-permute-start(bf16[32,896]{1,0:T(8,128)(2,1)S(1)} %add.72.refs_11_), channel_id=1, source_target_pairs={{0,1},{1,0},{2,3},{3,2},{4,5},{5,4},{6,7},{7,6},{8,9},{9,8},{10,11... | collective-permute-start | bytes 172040 | tf_op jit(solution)/shard_map/ppermute | solution.py:479
  49.4 1.7 %collective-permute-start.17 = (bf16[32,768]{1,0:T(8,128)(2,1)S(1)}, bf16[32,768]{1,0:T(8,128)(2,1)S(1)}, u32[]{:S(2)}, u32[]{:S(2)}) collective-permute-start(bf16[32,768]{1,0:T(8,128)(2,1)S(1)} %add.87.refs_13_), channel_id=1, source_target_pairs={{0,1},{1,0},{2,3},{3,2},{4,5},{5,4},{6,7},{7,6},{8,9},{9,8},{10,11... | collective-permute-start | bytes 147464 | tf_op jit(solution)/shard_map/ppermute | solution.py:479
  52.4 1.9 %collective-permute-start.23 = (bf16[32,896]{1,0:T(8,128)(2,1)S(1)}, bf16[32,896]{1,0:T(8,128)(2,1)S(1)}, u32[]{:S(2)}, u32[]{:S(2)}) collective-permute-start(bf16[32,896]{1,0:T(8,128)(2,1)S(1)} %get-tuple-element.110.send_a), channel_id=1, source_target_pairs={{0,1},{1,0},{2,3},{3,2},{4,5},{5,4},{6,7},{7,6},{8,9},{9,8},{10,11... | collective-permute-start | bytes 172040 | tf_op jit(solution)/shard_map/ppermute | solution.py:479
  53.8 1.5 %collective-permute-start.19 = (bf16[32,768]{1,0:T(8,128)(2,1)S(1)}, bf16[32,768]{1,0:T(8,128)(2,1)S(1)}, u32[]{:S(2)}, u32[]{:S(2)}) collective-permute-start(bf16[32,768]{1,0:T(8,128)(2,1)S(1)} %get-tuple-element.111), channel_id=1, source_target_pairs={{0,1},{1,0},{2,3},{3,2},{4,5},{5,4},{6,7},{7,6},{8,9},{9,8},{10,11... | collective-permute-start | bytes 147464 | tf_op jit(solution)/shard_map/ppermute | solution.py:479
  54.3 4.0 %collective-permute-start.24 = (bf16[32,896]{1,0:T(8,128)(2,1)S(1)}, bf16[32,896]{1,0:T(8,128)(2,1)S(1)}, u32[]{:S(2)}, u32[]{:S(2)}) collective-permute-start(bf16[32,896]{1,0:T(8,128)(2,1)S(1)} %add.76), channel_id=1, source_target_pairs={{0,5},{1,4},{2,7},{3,6},{4,1},{5,0},{6,3},{7,2},{8,13},{9,12},{10,... | collective-permute-start | bytes 172040 | tf_op jit(solution)/shard_map/ppermute | solution.py:479
  55.3 4.7 %collective-permute-start.20 = (bf16[32,768]{1,0:T(8,128)(2,1)S(1)}, bf16[32,768]{1,0:T(8,128)(2,1)S(1)}, u32[]{:S(2)}, u32[]{:S(2)}) collective-permute-start(bf16[32,768]{1,0:T(8,128)(2,1)S(1)} %add.73), channel_id=1, source_target_pairs={{0,9},{1,8},{2,11},{3,10},{4,13},{5,12},{6,15},{7,14},{8,1},{9,0},... | collective-permute-start | bytes 147464 | tf_op jit(solution)/shard_map/ppermute | solution.py:479
  58.4 4.0 %collective-permute-start.25 = (bf16[32,896]{1,0:T(8,128)(2,1)S(1)}, bf16[32,896]{1,0:T(8,128)(2,1)S(1)}, u32[]{:S(2)}, u32[]{:S(2)}) collective-permute-start(bf16[32,896]{1,0:T(8,128)(2,1)S(1)} %add.77), channel_id=1, source_target_pairs={{0,3},{1,2},{2,1},{3,0},{4,7},{5,6},{6,5},{7,4},{8,11},{9,10},{10,... | collective-permute-start | bytes 172040 | tf_op jit(solution)/shard_map/ppermute | solution.py:479
  60.1 3.6 %collective-permute-start.21 = (bf16[32,768]{1,0:T(8,128)(2,1)S(1)}, bf16[32,768]{1,0:T(8,128)(2,1)S(1)}, u32[]{:S(2)}, u32[]{:S(2)}) collective-permute-start(bf16[32,768]{1,0:T(8,128)(2,1)S(1)} %add.74), channel_id=1, source_target_pairs={{0,5},{1,4},{2,7},{3,6},{4,1},{5,0},{6,3},{7,2},{8,13},{9,12},{10,... | collective-permute-start | bytes 147464 | tf_op jit(solution)/shard_map/ppermute | solution.py:479
  62.4 6.3 %collective-permute-start.26 = (bf16[32,896]{1,0:T(8,128)(2,1)S(1)}, bf16[32,896]{1,0:T(8,128)(2,1)S(1)}, u32[]{:S(2)}, u32[]{:S(2)}) collective-permute-start(bf16[32,896]{1,0:T(8,128)(2,1)S(1)} %add.78), channel_id=1, source_target_pairs={{0,9},{1,8},{2,11},{3,10},{4,13},{5,12},{6,15},{7,14},{8,1},{9,0},... | collective-permute-start | bytes 172040 | tf_op jit(solution)/shard_map/ppermute | solution.py:479
  63.7 6.0 %collective-permute-start.22 = (bf16[32,768]{1,0:T(8,128)(2,1)S(1)}, bf16[32,768]{1,0:T(8,128)(2,1)S(1)}, u32[]{:S(2)}, u32[]{:S(2)}) collective-permute-start(bf16[32,768]{1,0:T(8,128)(2,1)S(1)} %add.75.own_ref), channel_id=1, source_target_pairs={{0,3},{1,2},{2,1},{3,0},{4,7},{5,6},{6,5},{7,4},{8,11},{9,10},{10,... | collective-permute-start | bytes 147464 | tf_op jit(solution)/shard_map/ppermute | solution.py:479
  68.7 1.5 %collective-permute-start.28 = (bf16[32,896]{1,0:T(8,128)(2,1)S(1)}, bf16[32,896]{1,0:T(8,128)(2,1)S(1)}, u32[]{:S(2)}, u32[]{:S(2)}) collective-permute-start(bf16[32,896]{1,0:T(8,128)(2,1)S(1)} %add.79.refs_11_), channel_id=1, source_target_pairs={{0,1},{1,0},{2,3},{3,2},{4,5},{5,4},{6,7},{7,6},{8,9},{9,8},{10,11... | collective-permute-start | bytes 172040 | tf_op jit(solution)/shard_map/ppermute | solution.py:479
  69.7 1.7 %collective-permute-start.27 = (bf16[32,768]{1,0:T(8,128)(2,1)S(1)}, bf16[32,768]{1,0:T(8,128)(2,1)S(1)}, u32[]{:S(2)}, u32[]{:S(2)}) collective-permute-start(bf16[32,768]{1,0:T(8,128)(2,1)S(1)} %add.88.refs_13_), channel_id=1, source_target_pairs={{0,1},{1,0},{2,3},{3,2},{4,5},{5,4},{6,7},{7,6},{8,9},{9,8},{10,11... | collective-permute-start | bytes 147464 | tf_op jit(solution)/shard_map/ppermute | solution.py:479
  72.7 1.9 %collective-permute-start.33 = (bf16[32,896]{1,0:T(8,128)(2,1)S(1)}, bf16[32,896]{1,0:T(8,128)(2,1)S(1)}, u32[]{:S(2)}, u32[]{:S(2)}) collective-permute-start(bf16[32,896]{1,0:T(8,128)(2,1)S(1)} %get-tuple-element.126.send_a), channel_id=1, source_target_pairs={{0,1},{1,0},{2,3},{3,2},{4,5},{5,4},{6,7},{7,6},{8,9},{9,8},{10,11... | collective-permute-start | bytes 172040 | tf_op jit(solution)/shard_map/ppermute | solution.py:479
  74.1 1.3 %collective-permute-start.29 = (bf16[32,768]{1,0:T(8,128)(2,1)S(1)}, bf16[32,768]{1,0:T(8,128)(2,1)S(1)}, u32[]{:S(2)}, u32[]{:S(2)}) collective-permute-start(bf16[32,768]{1,0:T(8,128)(2,1)S(1)} %get-tuple-element.127), channel_id=1, source_target_pairs={{0,1},{1,0},{2,3},{3,2},{4,5},{5,4},{6,7},{7,6},{8,9},{9,8},{10,11... | collective-permute-start | bytes 147464 | tf_op jit(solution)/shard_map/ppermute | solution.py:479
  74.6 4.0 %collective-permute-start.34 = (bf16[32,896]{1,0:T(8,128)(2,1)S(1)}, bf16[32,896]{1,0:T(8,128)(2,1)S(1)}, u32[]{:S(2)}, u32[]{:S(2)}) collective-permute-start(bf16[32,896]{1,0:T(8,128)(2,1)S(1)} %add.83), channel_id=1, source_target_pairs={{0,5},{1,4},{2,7},{3,6},{4,1},{5,0},{6,3},{7,2},{8,13},{9,12},{10,... | collective-permute-start | bytes 172040 | tf_op jit(solution)/shard_map/ppermute | solution.py:479
  75.5 4.5 %collective-permute-start.30 = (bf16[32,768]{1,0:T(8,128)(2,1)S(1)}, bf16[32,768]{1,0:T(8,128)(2,1)S(1)}, u32[]{:S(2)}, u32[]{:S(2)}) collective-permute-start(bf16[32,768]{1,0:T(8,128)(2,1)S(1)} %add.80), channel_id=1, source_target_pairs={{0,9},{1,8},{2,11},{3,10},{4,13},{5,12},{6,15},{7,14},{8,1},{9,0},... | collective-permute-start | bytes 147464 | tf_op jit(solution)/shard_map/ppermute | solution.py:479
  78.6 4.0 %collective-permute-start.35 = (bf16[32,896]{1,0:T(8,128)(2,1)S(1)}, bf16[32,896]{1,0:T(8,128)(2,1)S(1)}, u32[]{:S(2)}, u32[]{:S(2)}) collective-permute-start(bf16[32,896]{1,0:T(8,128)(2,1)S(1)} %add.84), channel_id=1, source_target_pairs={{0,3},{1,2},{2,1},{3,0},{4,7},{5,6},{6,5},{7,4},{8,11},{9,10},{10,... | collective-permute-start | bytes 172040 | tf_op jit(solution)/shard_map/ppermute | solution.py:479
  80.0 3.6 %collective-permute-start.31 = (bf16[32,768]{1,0:T(8,128)(2,1)S(1)}, bf16[32,768]{1,0:T(8,128)(2,1)S(1)}, u32[]{:S(2)}, u32[]{:S(2)}) collective-permute-start(bf16[32,768]{1,0:T(8,128)(2,1)S(1)} %add.81), channel_id=1, source_target_pairs={{0,5},{1,4},{2,7},{3,6},{4,1},{5,0},{6,3},{7,2},{8,13},{9,12},{10,... | collective-permute-start | bytes 147464 | tf_op jit(solution)/shard_map/ppermute | solution.py:479
  82.6 5.6 %collective-permute-start.36 = (bf16[32,896]{1,0:T(8,128)(2,1)S(1)}, bf16[32,896]{1,0:T(8,128)(2,1)S(1)}, u32[]{:S(2)}, u32[]{:S(2)}) collective-permute-start(bf16[32,896]{1,0:T(8,128)(2,1)S(1)} %add.85), channel_id=1, source_target_pairs={{0,9},{1,8},{2,11},{3,10},{4,13},{5,12},{6,15},{7,14},{8,1},{9,0},... | collective-permute-start | bytes 172040 | tf_op jit(solution)/shard_map/ppermute | solution.py:479
  83.6 5.6 %collective-permute-start.32 = (bf16[32,768]{1,0:T(8,128)(2,1)S(1)}, bf16[32,768]{1,0:T(8,128)(2,1)S(1)}, u32[]{:S(2)}, u32[]{:S(2)}) collective-permute-start(bf16[32,768]{1,0:T(8,128)(2,1)S(1)} %add.82.own_ref), channel_id=1, source_target_pairs={{0,3},{1,2},{2,1},{3,0},{4,7},{5,6},{6,5},{7,4},{8,11},{9,10},{10,... | collective-permute-start | bytes 147464 | tf_op jit(solution)/shard_map/ppermute | solution.py:479
  88.2 1.5 %collective-permute-start.38 = (bf16[32,896]{1,0:T(8,128)(2,1)S(1)}, bf16[32,896]{1,0:T(8,128)(2,1)S(1)}, u32[]{:S(2)}, u32[]{:S(2)}) collective-permute-start(bf16[32,896]{1,0:T(8,128)(2,1)S(1)} %add.86.refs_11_), channel_id=1, source_target_pairs={{0,1},{1,0},{2,3},{3,2},{4,5},{5,4},{6,7},{7,6},{8,9},{9,8},{10,11... | collective-permute-start | bytes 172040 | tf_op jit(solution)/shard_map/ppermute | solution.py:479
  89.2 1.7 %collective-permute-start.37 = (bf16[32,768]{1,0:T(8,128)(2,1)S(1)}, bf16[32,768]{1,0:T(8,128)(2,1)S(1)}, u32[]{:S(2)}, u32[]{:S(2)}) collective-permute-start(bf16[32,768]{1,0:T(8,128)(2,1)S(1)} %add.89.refs_13_), channel_id=1, source_target_pairs={{0,1},{1,0},{2,3},{3,2},{4,5},{5,4},{6,7},{7,6},{8,9},{9,8},{10,11... | collective-permute-start | bytes 147464 | tf_op jit(solution)/shard_map/ppermute | solution.py:479
